TPU v7x, 256 devices: a whole 4x4x8 slice. The times are simulated.
256 devices in a mesh: sample: 16 (over x_hi, y, core), tensor: 16 (over z, x_lo).
Axes of the slice: x: 4 (x_hi: 2, x_lo: 2; x = x_hi * 2 + x_lo), y: 4, z: 8, core: 2. Of those that a mesh axis runs over, the one named last changes fastest.
Arguments:
- response_hidden: bfloat16 [1024, 8192], P('sample', 'tensor'), may hold values from -6 to 6, as said below
- prompt_hidden: bfloat16 [4096, 8192], P('sample', 'tensor'), may hold values from -6 to 6
- norm_gain: bfloat16 [8192], replicated, may hold values from 0.099609375 to 1.8984375
- query_weight: bfloat16 [8192, 4096], P(None, 'tensor'), may hold values from -16 to 16
- key_weight: bfloat16 [8192, 512], P(None, 'tensor'), may hold values from -16 to 16
- value_weight: bfloat16 [8192, 512], P(None, 'tensor'), may hold values from -0.0625 to 0.0625
- output_weight: bfloat16 [4096, 8192], P('tensor'), may hold values from -1 to 1
- response_lengths: int32 [16], P('sample'), may hold values from 8 to 64, as said below
- prompt_length: int32 [1], replicated, may hold values from 2048 to 4096
Outputs:
- mixed: bfloat16 [1024, 8192], P('sample', 'tensor')
Inputs may be any that keep to these rules, and one draw needn't show every extreme that they name: `response_hidden`: activations. `response_lengths`: some response has all 64 rows live in every draw.
All inputs are finite; a program needn't handle non-finite values.
Results may differ from a plain program's by a relative error of at most 0.025.
Values may be sent and summed in bfloat16 or wider, within the bound.
No kernel may reach another device: no remote copies, remote signals or barrier semaphores. Data moves between devices by JAX's collectives and lax.ppermute only.
A program may use at most 320 MiB of HBM per device.

v0:
```python
import math

import jax
import jax.numpy as jnp
from jax import lax
from jax.sharding import PartitionSpec as P

HEAD_DIM = 128
HEADS_DEV = 2
GROUP = 8


epsilon = 1e-05
rope_base = 500000.0
neg_big = -1e30


def rms_norm(row_data, gain):
    values = row_data.astype(jnp.float32)
    factor = lax.rsqrt(jnp.mean(values * values, axis=1, keepdims=True) + epsilon)
    return (values * factor * gain.astype(jnp.float32)[None, :]).astype(jnp.bfloat16)


def rotate(values, positions):
    head_width = values.shape[-1]
    half_width = head_width // 2
    inverse = rope_base ** (-(jnp.arange(half_width).astype(jnp.float32) * 2.0 / head_width))
    angles = positions.astype(jnp.float32)[:, None] * inverse[None, :]
    cosine = jnp.cos(angles)[:, None, :]
    sine_part = jnp.sin(angles)[:, None, :]
    first_half = values[..., :half_width]
    second_half = values[..., half_width:]
    return jnp.concatenate(
        [
            first_half * cosine - second_half * sine_part,
            second_half * cosine + first_half * sine_part,
        ],
        axis=-1,
    )


def rope_head(key_block, positions):
    return rotate(key_block.astype(jnp.float32)[:, None, :], positions)[:, 0, :].astype(
        jnp.bfloat16
    )


def body(
    response_hidden,
    prompt_hidden,
    norm_gain,
    query_weight,
    key_weight,
    value_weight,
    output_weight,
    response_lengths,
    prompt_length,
):
    resp_rows = response_hidden.shape[0]
    full_resp, full_prompt = (
        lax.all_gather(response_hidden, "tensor", axis=1, tiled=True),
        lax.all_gather(prompt_hidden, "tensor", axis=1, tiled=True),
    )
    normed_resp = rms_norm(full_resp, norm_gain)
    normed_prompt = rms_norm(full_prompt, norm_gain)
    prompt_size = prompt_length[0]
    shared_head = lax.axis_index("tensor") * HEADS_DEV // GROUP
    offsets = jnp.arange(resp_rows, dtype=jnp.int32)
    response_positions = prompt_size + offsets
    score_scale = HEAD_DIM ** (-0.5)
    queries = jnp.dot(normed_resp, query_weight, preferred_element_type=jnp.float32).reshape(
        resp_rows, HEADS_DEV, HEAD_DIM
    )
    queries = rotate(queries, response_positions).astype(jnp.bfloat16)
    resp_keys_raw = jnp.dot(normed_resp, key_weight, preferred_element_type=jnp.float32).astype(
        jnp.bfloat16
    )
    resp_vals_raw = jnp.dot(normed_resp, value_weight, preferred_element_type=jnp.float32).astype(
        jnp.bfloat16
    )
    prompt_keys_raw = jnp.dot(normed_prompt, key_weight, preferred_element_type=jnp.float32).astype(
        jnp.bfloat16
    )
    prompt_vals_raw = jnp.dot(
        normed_prompt, value_weight, preferred_element_type=jnp.float32
    ).astype(jnp.bfloat16)

    def own_head(columns):
        head_count = columns.shape[1] // HEAD_DIM
        picker = (jnp.arange(head_count, dtype=jnp.int32) == shared_head).astype(jnp.bfloat16)
        grouped = columns.reshape(columns.shape[0], HEAD_DIM, head_count)
        return jnp.einsum("rek,k->re", grouped, picker, preferred_element_type=jnp.float32).astype(
            jnp.bfloat16
        )

    def attend(running, key_rows, value_rows, allowed):
        weighted, row_max, row_total = running
        scores = (
            jnp.einsum("rhd,nd->hrn", queries, key_rows, preferred_element_type=jnp.float32)
            * score_scale
        )
        scores = jnp.where(allowed[None], scores, neg_big)
        new_max = jnp.maximum(row_max, jnp.max(scores, axis=-1))
        factor = jnp.exp(row_max - new_max)
        weights = jnp.where(allowed[None], jnp.exp(scores - new_max[..., None]), 0.0)
        row_total = row_total * factor + jnp.sum(weights, axis=-1)
        update = jnp.einsum(
            "hrn,nd->hrd",
            weights.astype(jnp.bfloat16),
            value_rows,
            preferred_element_type=jnp.float32,
        )
        return (weighted * factor[..., None] + update, new_max, row_total)

    def prefix_step(running, shards, first_row):
        key_rows, value_rows = shards
        piece_rows = key_rows.shape[0]
        allowed = (first_row + jnp.arange(piece_rows, dtype=jnp.int32) < prompt_size)[None, :]
        return attend(running, key_rows, value_rows, allowed)

    initial = (
        jnp.zeros((HEADS_DEV, resp_rows, HEAD_DIM), jnp.float32),
        jnp.full((HEADS_DEV, resp_rows), neg_big, jnp.float32),
        jnp.zeros((HEADS_DEV, resp_rows), jnp.float32),
    )
    resp_keys_all, resp_vals_all = (
        lax.all_gather(resp_keys_raw, "tensor", axis=1, tiled=True),
        lax.all_gather(resp_vals_raw, "tensor", axis=1, tiled=True),
    )
    keys_by_rows, vals_by_rows = (
        lax.all_gather(prompt_keys_raw, "sample", axis=0, tiled=True),
        lax.all_gather(prompt_vals_raw, "sample", axis=0, tiled=True),
    )
    prompt_keys_all, prompt_vals_all = (
        lax.all_gather(keys_by_rows, "tensor", axis=1, tiled=True),
        lax.all_gather(vals_by_rows, "tensor", axis=1, tiled=True),
    )
    prompt_total = prompt_keys_all.shape[0]
    prompt_keys = rope_head(own_head(prompt_keys_all), jnp.arange(prompt_total, dtype=jnp.int32))
    prompt_vals = own_head(prompt_vals_all)
    block_rows = math.gcd(512, prompt_total)

    def block_step(block_index, running):
        first_row = block_index * block_rows
        shards = (
            lax.dynamic_slice_in_dim(prompt_keys, first_row, block_rows, 0),
            lax.dynamic_slice_in_dim(prompt_vals, first_row, block_rows, 0),
        )
        return prefix_step(running, shards, first_row)

    running = lax.fori_loop(0, prompt_total // block_rows, block_step, initial)
    own_keys = rope_head(own_head(resp_keys_all), response_positions)
    own_vals = own_head(resp_vals_all)
    causal = offsets[None, :] <= offsets[:, None]
    weighted, row_max, row_total = attend(running, own_keys, own_vals, causal)
    attention = (weighted / row_total[..., None]).astype(jnp.bfloat16)
    attention = jnp.transpose(attention, (1, 0, 2)).reshape(resp_rows, HEADS_DEV * HEAD_DIM)
    partial_value = jnp.dot(attention, output_weight, preferred_element_type=jnp.float32)
    summed = lax.psum_scatter(
        partial_value.astype(jnp.bfloat16), "tensor", scatter_dimension=1, tiled=True
    ).astype(jnp.float32)
    live_rows = offsets < response_lengths[0]
    return jnp.where(live_rows[:, None], summed, 0.0).astype(jnp.bfloat16)


def solution(mesh):
    return jax.shard_map(
        body,
        mesh=mesh,
        in_specs=(
            P("sample", "tensor"),
            P("sample", "tensor"),
            P(),
            P(None, "tensor"),
            P(None, "tensor"),
            P(None, "tensor"),
            P("tensor", None),
            P("sample"),
            P(),
        ),
        out_specs=P("sample", "tensor"),
        check_vma=False,
    )
```

profile of v0, /device:TPU:2, one launch (start us, length us, event | category | flops | bytes accessed | tf_op | source)
XLA Modules:
  0.0 656.7 jit_solution(11040137518724872912)
XLA Ops:
  6.5 0.7 all-gather.5.cloned.1.call-update
  7.3 0.7 all-gather.9.cloned.1.call-update
  8.1 0.7 convert_element_type.118
  8.8 101.8 %all-gather.5.cloned.1.call-done = bf16[256,8192]{1,0:T(8,128)(2,1)} async-done(((bf16[256,512]{1,0:T(8,128)(2,1)}), bf16[256,8192]{1,0:T(8,128)(2,1)}) %all-gather.5.cloned.1.call-update) | async-done | bytes 4194320 | tf_op jit(solution)/shard_map/all_gather | solution.py:62
  110.6 3.3 fusion.17
  114.1 1.4 fusion.39
  115.5 25.4 %all_gather.28 = bf16[4096,32]{0,1:T(8,128)(2,1)} all-gather(bf16[256,32]{0,1:T(8,128)(2,1)S(1)} %fusion.39), channel_id=1, replica_groups=mesh['sample'=16,'tensor'=16] {'sample'}, dimensions={0}, use_global_device_ids=true | all-gather | bytes 278528 | tf_op jit(solution)/shard_map/all_gather | solution.py:132
  140.9 3.6 fusion.36
  144.5 22.5 %all_gather.25 = bf16[4096,32]{0,1:T(8,128)(2,1)} all-gather(bf16[256,32]{0,1:T(8,128)(2,1)S(1)} %fusion.36), channel_id=1, replica_groups=mesh['sample'=16,'tensor'=16] {'sample'}, dimensions={0}, use_global_device_ids=true | all-gather | bytes 278528 | tf_op jit(solution)/shard_map/all_gather | solution.py:131
  168.1 13.8 %all-gather.9.cloned.1.call-done = bf16[64,8192]{1,0:T(8,128)(2,1)} async-done(((bf16[64,512]{1,0:T(8,128)(2,1)}), bf16[64,8192]{1,0:T(8,128)(2,1)}) %all-gather.9.cloned.1.call-update) | async-done | bytes 1048592 | tf_op jit(solution)/shard_map/all_gather | solution.py:61
  181.8 1.6 fusion.20
  183.5 3.4 fusion.74
  186.9 0.5 convolution_convert_fusion.1
  187.4 33.6 %all_gather.31 = bf16[64,512]{0,1:T(8,128)(2,1)S(1)} all-gather(bf16[64,32]{0,1:T(8,128)(2,1)S(1)} %convolution_convert_fusion.1), channel_id=1, replica_groups=mesh['sample'=16,'tensor'=16] {'tensor'}, dimensions={1}, use_global_device_ids=true | all-gather | bytes 69632 | tf_op jit(solution)/shard_map/all_gather | solution.py:128
  221.1 0.2 fusion.82
  221.4 0.5 convolution_convert_fusion.2
  221.9 31.9 %all_gather.30 = bf16[64,512]{0,1:T(8,128)(2,1)S(1)} all-gather(bf16[64,32]{0,1:T(8,128)(2,1)S(1)} %convolution_convert_fusion.2), channel_id=1, replica_groups=mesh['sample'=16,'tensor'=16] {'tensor'}, dimensions={1}, use_global_device_ids=true | all-gather | bytes 69632 | tf_op jit(solution)/shard_map/all_gather | solution.py:127
  253.8 0.2 fusion.81
  254.6 0.2 fusion.78
  254.8 31.6 %all-gather.11.cloned.1.call-done = bf16[4096,512]{0,1:T(8,128)(2,1)} async-done(((bf16[4096,32]{0,1:T(8,128)(2,1)}), bf16[4096,512]{0,1:T(8,128)(2,1)}) %all-gather.11.cloned.1.call-update) | async-done | bytes 4194320 | tf_op jit(solution)/shard_map/all_gather | solution.py:136
  286.5 7.2 %reshape.255 = bf16[4096,128,4]{0,2,1:T(4,128)(2,1)} reshape(bf16[4096,512]{0,1:T(8,128)(2,1)} %all-gather.11.cloned.1.call-done) | data formatting | bytes 8388608 | tf_op jit(solution)/shard_map/reshape | solution.py:91
  293.6 6.0 fusion.80
  299.6 5.1 copy.23
  304.7 82.8 %all-gather.7.cloned.1.call-done = bf16[4096,512]{0,1:T(8,128)(2,1)} async-done(((bf16[4096,32]{0,1:T(8,128)(2,1)}), bf16[4096,512]{0,1:T(8,128)(2,1)}) %all-gather.7.cloned.1.call-update) | async-done | bytes 4194320 | tf_op jit(solution)/shard_map/all_gather | solution.py:135
  387.6 7.2 %reshape.253 = bf16[4096,128,4]{0,2,1:T(4,128)(2,1)} reshape(bf16[4096,512]{0,1:T(8,128)(2,1)} %all-gather.7.cloned.1.call-done) | data formatting | bytes 8388608 | tf_op jit(solution)/shard_map/reshape | solution.py:91
  394.8 60.8 %fusion.79 = bf16[1,4096,128]{0,1,2:T(8,128)(2,1)} fusion(bf16[4096,128,4]{0,2,1:T(4,128)(2,1)} %reshape.253, pred[4,1,1]{0,1,2:T(4,128)(4,1)S(1)} %compare_bitcast_fusion), kind=kOutput, calls=%fused_computation.111 | convolution fusion | flops 4194304 | bytes 5242884 | tf_op jit(solution)/shard_map/rek,k->re/dot_general | solution.py:92
  455.6 103.3 %copy.22 = bf16[1,4096,128]{1,2,0:T(8,128)(2,1)S(1)} copy(bf16[1,4096,128]{0,1,2:T(8,128)(2,1)} %fusion.79) | data formatting | bytes 2097152 | tf_op jit(solution)/shard_map/rek,k->re/dot_general | solution.py:92
  558.8 0.2 fusion.47
  559.1 4.2 fusion.43
  563.4 11.5 %while.18 = (s32[]{:T(128)}, f32[2,64,128]{2,1,0:T(8,128)S(1)}, f32[2,64]{1,0:T(2,128)S(1)}, f32[2,64]{1,0:T(2,128)S(1)}, s32[]{:T(128)}, /*index=5*/bf16[4096,1...) while((s32[]{:T(128)}, f32[2,64,128]{2,1,0:T(8,128)S(1)}, ...), condition=%wide.region_5.6_spmd.clone, body=%wide.region_2.5_spmd.clone.sunk | while | flops 34195076 | bytes 1223879 | solution.py:151
  563.4 0.7 add_compare_fusion.2
  564.1 0.3 fusion.109
  564.3 0.2 fusion.111
  564.6 0.2 convolution_add_fusion.3
  564.8 0.7 add_compare_fusion.2
  565.5 0.3 fusion.109
  565.8 0.2 fusion.111
  566.0 0.2 convolution_add_fusion.3
  566.3 0.7 add_compare_fusion.2
  566.9 0.3 fusion.109
  567.2 0.2 fusion.111
  567.4 0.2 convolution_add_fusion.3
  567.7 0.7 add_compare_fusion.2
  568.4 0.3 fusion.109
  568.7 0.2 fusion.111
  568.9 0.2 convolution_add_fusion.3
  569.2 0.7 add_compare_fusion.2
  569.8 0.3 fusion.109
  570.1 0.2 fusion.111
  570.3 0.2 convolution_add_fusion.3
  570.6 0.7 add_compare_fusion.2
  571.3 0.3 fusion.109
  571.5 0.2 fusion.111
  571.8 0.2 convolution_add_fusion.3
  572.0 0.7 add_compare_fusion.2
  572.7 0.3 fusion.109
  573.0 0.2 fusion.111
  573.2 0.2 convolution_add_fusion.3
  573.5 0.7 add_compare_fusion.2
  574.1 0.3 fusion.109
  574.6 0.2 convolution_add_fusion.3
  575.2 4.0 convolution_convert_fusion
  579.9 68.8 %reduce-scatter.2.cloned.1.call-done = bf16[64,512]{1,0:T(8,128)(2,1)} async-done(((bf16[64,8192]{1,0:T(8,128)(2,1)}), bf16[64,512]{1,0:T(8,128)(2,1)}) %reduce-scatter.2.cloned.1.call-update) | async-done | bytes 65552 | tf_op jit(solution)/shard_map/reduce_scatter | solution.py:159
  648.6 1.5 select_convert_fusion
  (66 shorter events, 2.1 us)
Async XLA Ops:
  6.5 107.3 %copy-start = (bf16[8192,32]{0,1:T(8,128)(2,1)S(1)}, bf16[8192,32]{0,1:T(8,128)(2,1)}, u32[]{:S(2)}) copy-start(bf16[8192,32]{0,1:T(8,128)(2,1)} %param.16) | copy-start | bytes 1572868
  6.5 104.1 %all-gather.5.cloned.1.call-start = ((), (), s32[]{:S(2)}) async-start(), calls=%async_computation.1 | async-start | bytes 4456448 | tf_op jit(solution)/shard_map/all_gather | solution.py:62
  7.3 174.6 %all-gather.9.cloned.1.call-start = ((), (), s32[]{:S(2)}) async-start(), calls=%async_computation.3 | async-start | bytes 1114112 | tf_op jit(solution)/shard_map/all_gather | solution.py:61
  8.0 278.4 %all-gather.11.cloned.1.call-start = ((), (), s32[]{:S(2)}) async-start(), calls=%async_computation.4 | async-start | bytes 4456448 | tf_op jit(solution)/shard_map/all_gather | solution.py:136
  110.6 3.4 copy-start.1
  114.1 26.8 %copy-start.3 = (bf16[8192,32]{0,1:T(8,128)(2,1)S(1)}, bf16[8192,32]{0,1:T(8,128)(2,1)}, u32[]{:S(2)}) copy-start(bf16[8192,32]{0,1:T(8,128)(2,1)} %param.15) | copy-start | bytes 1572868
  140.9 246.7 %all-gather.7.cloned.1.call-start = ((), (), s32[]{:S(2)}) async-start(), calls=%async_computation.2 | async-start | bytes 4456448 | tf_op jit(solution)/shard_map/all_gather | solution.py:135
  167.0 481.6 %reduce-scatter.2.cloned.1.call-start = ((), (), s32[]{:S(2)}) async-start(), calls=%async_computation.5 | async-start | bytes 1114112 | tf_op jit(solution)/shard_map/reduce_scatter | solution.py:159
  181.8 5.1 copy-start.2
Sparse Core Ops, SparseCore 0:
  9.2 101.4 all-gather.4
  112.4 69.3 all-gather.8
  183.6 102.7 all-gather.10
  288.1 99.4 all-gather.6
  579.3 69.2 reduce-scatter.1
where the time goes:
time: 663 us; the launch traced here: 657 us
  waiting for transfers between devices  300 us (45%)
  local copies, waits for them, and re-layouts  123 us (19%)
  blocking collectives  113 us (17%)
  matrix products  85.2 us (13%)
  other arithmetic  19.3 us (3%)
  between operations  14.7 us (2%)
    dot_general x4, local copies, waits for them, and re-layouts, own_head(): jnp.einsum('rek,k->re', grouped, picker, preferred_element_type=jnp.float32)  109 us
    all_gather x1, waiting for transfers between devices, body(): lax.all_gather(prompt_hidden, 'tensor', axis=1, tiled=True)  102 us
    all_gather x1, waiting for transfers between devices, body(): lax.all_gather(keys_by_rows, 'tensor', axis=1, tiled=True)  82.8 us
    reduce_scatter x1, waiting for transfers between devices, body(): lax.psum_scatter(partial_value.astype(jnp.bfloat16), 'tensor', scatter_di...  68.8 us
    dot_general x4, matrix products, own_head(): jnp.einsum('rek,k->re', grouped, picker, preferred_element_type=jnp.float32)  67.2 us
    all_gather x1, blocking collectives, body(): lax.all_gather(resp_vals_raw, 'tensor', axis=1, tiled=True)  33.6 us
    all_gather x1, blocking collectives, body(): lax.all_gather(resp_keys_raw, 'tensor', axis=1, tiled=True)  31.9 us
    all_gather x1, waiting for transfers between devices, body(): lax.all_gather(vals_by_rows, 'tensor', axis=1, tiled=True)  31.6 us
  transfers between devices with their start and end apart: 5, of which 5 were waited for; matrix products, arithmetic and copies ran while one was open for 5% of the time, Pallas kernels for 0%

commit v1 on v0

v1 whole, which is shorter than its diff:
```python
import functools

import jax
import jax.numpy as jnp
from jax import lax
from jax.experimental import pallas as pl
from jax.experimental.pallas import tpu as pltpu
from jax.sharding import Mesh
from jax.sharding import PartitionSpec as P

PARTS = (("xh", 2), ("y", 4), ("core", 2), ("k", 4), ("zl", 2), ("xl", 2))
SAMPLE = ("xh", "y", "core")
TENSOR = ("k", "zl", "xl")
ZRING = ("k", "zl")
OWN_HEAD = ("zl", "xl")
KEY_GROUP = ("xh", "core", "zl", "xl")
QUERY_GROUP = "y"

D = 8192
BLOCK = 512
HEAD_DIM = 128
HALF = 64
RESP = 64
PROMPT_ROWS = 256
ROWS = 80
SENT_ROWS = 96
EPSILON = 1e-05
ROPE_BASE = 500000.0
NEG_BIG = -1e30
F32 = jnp.float32
BF16 = jnp.bfloat16
VMEM_LIMIT = 48 * 1024 * 1024


def iota(shape, dim):
    return lax.broadcasted_iota(jnp.int32, shape, dim)


def dot_t(a, b):
    return lax.dot_general(a, b, (((1,), (1,)), ((), ())), preferred_element_type=F32)


def dot(a, b):
    return lax.dot_general(a, b, (((1,), (0,)), ((), ())), preferred_element_type=F32)


def params():
    return pltpu.CompilerParams(vmem_limit_bytes=VMEM_LIMIT)


def pack_kernel(core_ref, key_ref, value_ref, out_ref):
    core = core_ref[0]
    row, col = iota((32, 64), 0), iota((32, 64), 1)
    source = ((row >> 3) & 1) * 32 + (row & 7) * 4 + 2 * core + (row >> 4)
    pick = jnp.where(col == source, 1.0, 0.0).astype(BF16)
    both = jnp.concatenate([key_ref[...], value_ref[...]], axis=0)
    for i in range(out_ref.shape[0]):
        out_ref[i] = dot(pick, both[:, i * BLOCK : (i + 1) * BLOCK]).astype(BF16)


def pack_weights(core, key_rows, value_rows):
    steps = 2
    each = 16 // steps
    return pl.pallas_call(
        pack_kernel,
        grid=(steps,),
        in_specs=[
            pl.BlockSpec(memory_space=pltpu.SMEM),
            pl.BlockSpec((32, each * BLOCK), lambda i: (0, i)),
            pl.BlockSpec((32, each * BLOCK), lambda i: (0, i)),
        ],
        out_specs=pl.BlockSpec((each, 32, BLOCK), lambda i: (i, 0, 0)),
        out_shape=jax.ShapeDtypeStruct((16, 32, BLOCK), BF16),
        compiler_params=params(),
        name="pack_weights",
    )(core, key_rows, value_rows)


def partial_kernel(t_ref, weight_ref, prompt_ref, resp_ref, gain_ref, out_ref, scaled, high, low, sums):
    @pl.when(pl.program_id(0) == 0)
    def _():
        gain = gain_ref[t_ref[0]]
        high[320:384] = jnp.zeros((64, BLOCK), BF16)
        low[320:384] = jnp.zeros((64, BLOCK), BF16)

        def put(at, count, values):
            values = values.astype(F32)
            scaled[at : at + count] = (values * gain).astype(BF16)
            square = values * values
            top = square.astype(BF16)
            high[at : at + count] = top
            low[at : at + count] = (square - top.astype(F32)).astype(BF16)

        for c in range(4):
            put(80 * c, 64, prompt_ref[64 * c : 64 * c + 64])
            put(80 * c + 64, 16, resp_ref[16 * c : 16 * c + 16])
        ones = jnp.ones((16, BLOCK), BF16)
        row = iota((16, 128), 0)
        for c in range(4):
            total = dot_t(ones, high[80 * c : 80 * c + 128]) + dot_t(ones, low[80 * c : 80 * c + 128])
            top = total.astype(BF16).astype(F32)
            rest = total - top
            rows = jnp.where(row == 0, top, jnp.where(row == 1, rest, 0.0))
            sums[c, :, :128] = rows.astype(BF16)
            sums[c, :, 128:] = jnp.zeros((16, 128), BF16)

    weights = weight_ref[0].reshape(256, BLOCK)
    raw = dot_t(scaled[...], weights).astype(BF16)
    row, col = iota((256, 256), 0), iota((256, 256), 1)
    target = ((row >> 3) & 1) * 128 + (row >> 4) * 8 + (row & 7)
    pick = jnp.where(col == target, 1.0, 0.0).astype(BF16)
    ordered = dot(raw, pick).astype(BF16)
    for c in range(4):
        out_ref[c, :ROWS] = ordered[ROWS * c : ROWS * c + ROWS]
        out_ref[c, ROWS:] = sums[c]


def partial_products(t, weights, prompt, resp, gain):
    return pl.pallas_call(
        partial_kernel,
        grid=(4,),
        in_specs=[
            pl.BlockSpec(memory_space=pltpu.SMEM),
            pl.BlockSpec((1, 16, 16, BLOCK), lambda k: (k // 2, 0, k % 2, 0)),
            pl.BlockSpec((PROMPT_ROWS, BLOCK), lambda k: (0, 0)),
            pl.BlockSpec((RESP, BLOCK), lambda k: (0, 0)),
            pl.BlockSpec((16, 1, BLOCK), lambda k: (0, 0, 0)),
        ],
        out_specs=pl.BlockSpec((4, SENT_ROWS, 256), lambda k: (k, 0, 0)),
        out_shape=jax.ShapeDtypeStruct((16, SENT_ROWS, 256), BF16),
        scratch_shapes=[
            pltpu.VMEM((320, BLOCK), BF16),
            pltpu.VMEM((384, BLOCK), BF16),
            pltpu.VMEM((384, BLOCK), BF16),
            pltpu.VMEM((4, 16, 256), BF16),
        ],
        compiler_params=params(),
        name="partial_products",
    )(t, weights, prompt, resp, gain)


def turn(values, cosine, sine):
    return values * cosine + pltpu.roll(values, HALF, 1) * sine


def finish_kernel(parts_ref, cos_ref, sin_ref, out_ref):
    total = jnp.sum(parts_ref[...].astype(F32), axis=0)
    sums = total[ROWS : ROWS + 1, :128] + total[ROWS + 1 : ROWS + 2, :128]
    diagonal = iota((ROWS, 128), 0) == iota((ROWS, 128), 1)
    column = jnp.sum(jnp.where(diagonal, jnp.broadcast_to(sums, (ROWS, 128)), 0.0), axis=1, keepdims=True)
    factor = lax.rsqrt(column * (1.0 / D) + EPSILON)
    scaled = total[:ROWS] * factor
    keys = turn(scaled[:, :HEAD_DIM], cos_ref[...], sin_ref[...])
    out_ref[:, :HEAD_DIM] = keys.astype(BF16)
    out_ref[:, HEAD_DIM:] = scaled[:, HEAD_DIM:].astype(BF16)


def finish_keys(parts, cosine, sine):
    return pl.pallas_call(
        finish_kernel,
        out_shape=jax.ShapeDtypeStruct((ROWS, 256), BF16),
        compiler_params=params(),
        name="finish_keys",
    )(parts, cosine, sine)


def query_kernel(index_ref, hidden_ref, weight_ref, gain_ref, cos_ref, sin_ref, out_ref, total, squares):
    step = pl.program_id(0)

    @pl.when(step == 0)
    def _():
        total[...] = jnp.zeros_like(total)
        squares[...] = jnp.zeros_like(squares)

    for j in range(2):
        hidden = hidden_ref[0, j].astype(F32)
        scaled = (hidden * gain_ref[j]).astype(BF16)
        total[...] += dot(scaled, weight_ref[j * BLOCK : (j + 1) * BLOCK])
        squares[...] += jnp.sum(hidden * hidden, axis=1, keepdims=True)

    @pl.when(step == pl.num_programs(0) - 1)
    def _():
        factor = lax.rsqrt(squares[...] * (1.0 / D) + EPSILON)
        for h in range(2):
            part = slice(h * HEAD_DIM, (h + 1) * HEAD_DIM)
            query = turn(total[:, part] * factor, cos_ref[...], sin_ref[...])
            out_ref[:, part] = query.astype(BF16)


def queries_of(index, hidden, weight, gain, cosine, sine):
    return pl.pallas_call(
        query_kernel,
        grid_spec=pltpu.PrefetchScalarGridSpec(
            num_scalar_prefetch=1,
            grid=(8,),
            in_specs=[
                pl.BlockSpec((1, 2, RESP, BLOCK), lambda i, index: (i, 0, 0, 0)),
                pl.BlockSpec((2 * BLOCK, 256), lambda i, index: (index[i], 0)),
                pl.BlockSpec((2, 1, BLOCK), lambda i, index: (index[i], 0, 0)),
                pl.BlockSpec((RESP, HEAD_DIM), lambda i, index: (0, 0)),
                pl.BlockSpec((RESP, HEAD_DIM), lambda i, index: (0, 0)),
            ],
            out_specs=pl.BlockSpec((RESP, 256), lambda i, index: (0, 0)),
            scratch_shapes=[pltpu.VMEM((RESP, 256), F32), pltpu.VMEM((RESP, 1), F32)],
        ),
        out_shape=jax.ShapeDtypeStruct((RESP, 256), BF16),
        compiler_params=params(),
        name="queries",
    )(index, hidden, weight, gain, cosine, sine)


def attend_kernel(info_ref, query_ref, rows_ref, out_ref):
    own_y, own_place, length = info_ref[0], info_ref[1], info_ref[2]
    rows = rows_ref[...].reshape(16, ROWS, 256)
    prompt = rows[:, :64].reshape(1024, 256)
    prompt_keys, prompt_values = prompt[:, :HEAD_DIM], prompt[:, HEAD_DIM:]
    own = rows_ref[own_place]
    own = own[:, 64:].reshape(RESP, 256)
    own_keys, own_values = own[:, :HEAD_DIM], own[:, HEAD_DIM:]
    scale = HEAD_DIM ** (-0.5)

    column = iota((1, 1024), 1)
    place = column >> 8
    sample = (place >> 1) * 8 + own_y * 2 + (place & 1)
    live = sample * PROMPT_ROWS + (column & 255) < length
    causal = iota((RESP, RESP), 1) <= iota((RESP, RESP), 0)
    lane = iota((RESP, 128), 1)

    for y in range(4):
        mine = jnp.logical_and(causal, own_y == y)
        extra = jnp.zeros((RESP, 128), F32)
        for h in range(2):
            part = slice(h * HEAD_DIM, (h + 1) * HEAD_DIM)
            query = query_ref[y, :, part]
            far = jnp.where(live, dot_t(query, prompt_keys) * scale, NEG_BIG)
            near = jnp.where(mine, dot_t(query, own_keys) * scale, NEG_BIG)
            top = jnp.maximum(jnp.max(far, axis=1, keepdims=True), jnp.max(near, axis=1, keepdims=True))
            far = jnp.where(live, jnp.exp(far - top), 0.0)
            near = jnp.where(mine, jnp.exp(near - top), 0.0)
            total = jnp.sum(far, axis=1, keepdims=True) + jnp.sum(near, axis=1, keepdims=True)
            summed = dot(far.astype(BF16), prompt_values) + dot(near.astype(BF16), own_values)
            some = total > 0.0
            safe = jnp.where(some, total, 1.0)
            out_ref[y, :, part] = (summed / safe).astype(BF16)
            level = jnp.where(some, top + jnp.log(safe), NEG_BIG)
            first = level.astype(BF16).astype(F32)
            rest = level - first
            second = rest.astype(BF16).astype(F32)
            third = rest - second
            for i, piece in enumerate((first, second, third)):
                extra = jnp.where(lane == 3 * h + i, piece, extra)
        out_ref[y, :, 256:] = extra.astype(BF16)


def attend(info, queries, rows):
    return pl.pallas_call(
        attend_kernel,
        in_specs=[
            pl.BlockSpec(memory_space=pltpu.SMEM),
            pl.BlockSpec(memory_space=pltpu.VMEM),
            pl.BlockSpec(memory_space=pltpu.VMEM),
        ],
        out_shape=jax.ShapeDtypeStruct((4, RESP, 384), BF16),
        compiler_params=params(),
        name="attend",
    )(info, queries, rows)


def project_kernel(parts_ref, weight_ref, out_ref, attention):
    @pl.when(pl.program_id(0) == 0)
    def _():
        lane = iota((RESP, 128), 1)
        extras = [parts_ref[y, :, 256:].astype(F32) for y in range(4)]
        for h in range(2):
            part = slice(h * HEAD_DIM, (h + 1) * HEAD_DIM)
            mine = jnp.logical_and(lane >= 3 * h, lane < 3 * h + 3)
            levels = [jnp.sum(jnp.where(mine, e, 0.0), axis=1, keepdims=True) for e in extras]
            top = functools.reduce(jnp.maximum, levels)
            shares = [jnp.exp(level - top) for level in levels]
            total = functools.reduce(jnp.add, shares)
            summed = functools.reduce(jnp.add, [s * parts_ref[y, :, part].astype(F32) for y, s in enumerate(shares)])
            attention[:, part] = (summed / total).astype(BF16)

    for j in range(out_ref.shape[0]):
        out_ref[j] = dot(attention[...], weight_ref[:, j * BLOCK : (j + 1) * BLOCK]).astype(BF16)


def project(parts, weight):
    steps = 4
    each = 16 // steps
    return pl.pallas_call(
        project_kernel,
        grid=(steps,),
        in_specs=[
            pl.BlockSpec((4, RESP, 384), lambda i: (0, 0, 0)),
            pl.BlockSpec((256, each * BLOCK), lambda i: (0, i)),
        ],
        out_specs=pl.BlockSpec((each, RESP, BLOCK), lambda i: (i, 0, 0)),
        out_shape=jax.ShapeDtypeStruct((16, RESP, BLOCK), BF16),
        scratch_shapes=[pltpu.VMEM((RESP, 256), BF16)],
        compiler_params=params(),
        name="project",
    )(parts, weight)


def swap(values, axis):
    return lax.all_to_all(values, axis, 0, 0, tiled=False)


def share(values, axis, count):
    return swap(jnp.broadcast_to(values[None], (count,) + values.shape), axis)


def ring(hidden):
    other = lax.ppermute(hidden, "xl", [(0, 1), (1, 0)])
    first = lax.axis_index("xl") == 0
    pair = jnp.stack([jnp.where(first, hidden, other), jnp.where(first, other, hidden)])
    onward = [(i, (i + 1) % 8) for i in range(8)]
    back = [(i, (i + 7) % 8) for i in range(8)]
    z = lax.axis_index(ZRING)
    blocks, index = [pair], [z]
    up = down = pair
    for step in range(1, 5):
        up = lax.ppermute(up, ZRING, onward)
        blocks.append(up)
        index.append((z + 8 - step) % 8)
        if step < 4:
            down = lax.ppermute(down, ZRING, back)
            blocks.append(down)
            index.append((z + step) % 8)
    return jnp.stack(index).astype(jnp.int32), jnp.stack(blocks)


def body(
    response_hidden,
    prompt_hidden,
    norm_gain,
    query_weight,
    key_weight,
    value_weight,
    output_weight,
    response_lengths,
    prompt_length,
):
    length = prompt_length[0]
    core, y = lax.axis_index("core"), lax.axis_index("y")
    sample, quarter = lax.axis_index(SAMPLE), lax.axis_index(OWN_HEAD)
    gain = norm_gain.astype(F32).reshape(16, 1, BLOCK)

    row = jnp.arange(144, dtype=jnp.int32)
    positions = jnp.where(
        row < 64,
        sample * PROMPT_ROWS + quarter * 64 + row,
        jnp.where(row < 80, length + quarter * 16 + row - 64, length + row - 80),
    )
    lane = jnp.arange(HEAD_DIM, dtype=jnp.int32)
    inverse = ROPE_BASE ** (-((lane % HALF).astype(F32) * 2.0 / HEAD_DIM))
    angles = positions.astype(F32)[:, None] * inverse[None, :]
    cosine = jnp.cos(angles)
    sine = jnp.sin(angles) * jnp.where(lane < HALF, -1.0, 1.0)[None, :]

    index, hidden = ring(response_hidden)

    packed = pack_weights(core.reshape(1), key_weight.T, value_weight.T)
    half = swap(packed, TENSOR)
    other = lax.ppermute(half, "core", [(0, 1), (1, 0)])
    weights = jnp.stack([jnp.where(core == 0, half, other), jnp.where(core == 0, other, half)])

    partial_kv = partial_products(
        lax.axis_index(TENSOR).reshape(1), weights, prompt_hidden, response_hidden, gain
    )
    rows = finish_keys(swap(partial_kv, TENSOR), cosine[:80], sine[:80])
    rows = share(rows, KEY_GROUP, 16).reshape(4, 4, ROWS, 256)

    queries = queries_of(index, hidden, query_weight, gain, cosine[80:], sine[80:])
    queries = share(queries, QUERY_GROUP, 4)

    place = lax.axis_index(("xh", "core"))
    info = jnp.stack([y, place, length]).astype(jnp.int32)
    parts = swap(attend(info, queries, rows), QUERY_GROUP)
    partial = project(parts, output_weight)
    summed = jnp.sum(swap(partial, TENSOR).astype(F32), axis=0)
    live = jnp.arange(RESP, dtype=jnp.int32) < response_lengths[0]
    return jnp.where(live[:, None], summed, 0.0).astype(BF16)


def solution(mesh):
    names = tuple(name for name, _ in PARTS)
    sizes = tuple(size for _, size in PARTS)
    fine = Mesh(mesh.devices.reshape(sizes), names)
    return jax.shard_map(
        body,
        mesh=fine,
        in_specs=(
            P(SAMPLE, TENSOR),
            P(SAMPLE, TENSOR),
            P(),
            P(None, TENSOR),
            P(None, TENSOR),
            P(None, TENSOR),
            P(TENSOR, None),
            P(SAMPLE),
            P(),
        ),
        out_specs=P(SAMPLE, TENSOR),
        check_vma=False,
    )
```

time: 663 us -> 162 us (0.24)
  waiting for transfers between devices: 300 us -> 81.9 us
  local copies, waits for them, and re-layouts: 123 us -> 10 us
  blocking collectives: 113 us -> 8.69 us
  matrix products: 85.2 us -> 0 us
  starting transfers between devices: 0.16 us -> 42.2 us
  other arithmetic: 19.3 us -> 3.06 us
  Pallas kernels: 0 us -> 13.5 us
  between operations: 14.7 us -> 1.65 us
    all_gather x4 -> x0, waiting for transfers between devices: 230 us -> none  [the longest x1 102 us: body(): lax.all_gather(prompt_hidden, 'tensor', axis=1, tiled=True)]
    all_gather x4 -> x0, blocking collectives: 113 us -> none  [the longest x1 33.6 us: body(): lax.all_gather(resp_vals_raw, 'tensor', axis=1, tiled=True)]
    dot_general x4 -> x0, local copies, waits for them, and re-layouts: 109 us -> none  [own_head(): jnp.einsum('rek,k->re', grouped, picker, preferred_element_type=jnp.float32)]
    dot_general x28 -> x0, matrix products: 85.2 us -> none  [the longest x4 67.2 us: own_head(): jnp.einsum('rek,k->re', grouped, picker, preferred_element_type=jnp.float32)]
    reduce_scatter x1 -> x0, waiting for transfers between devices: 68.8 us -> none  [body(): lax.psum_scatter(partial_value.astype(jnp.bfloat16), 'tensor', scatter_di...]
    all_to_all x0 -> x5, waiting for transfers between devices: none -> 56.1 us  [swap(): return lax.all_to_all(values, axis, 0, 0, tiled=False)]
    all_to_all x0 -> x5, starting transfers between devices: none -> 33.7 us  [swap(): return lax.all_to_all(values, axis, 0, 0, tiled=False)]
    ppermute x0 -> x9, waiting for transfers between devices: none -> 25.7 us  [the longest x3 19.2 us: ring(): down = lax.ppermute(down, ZRING, back)]
  transfers between devices with their start and end apart: 5 -> 14, of which waited for: 5 -> 8; matrix products, arithmetic and copies ran while one was open for 5% -> 3% of each run, Pallas kernels for 0% -> 4%
where the time goes in v1:
time: 162 us; the launch traced here: 161 us
  waiting for transfers between devices  81.9 us (51%)
  starting transfers between devices  42.2 us (26%)
  Pallas kernels  13.5 us (8%)
  local copies, waits for them, and re-layouts  10 us (6%)
  blocking collectives  8.69 us (5%)
  other arithmetic  3.06 us (2%)
  between operations  1.65 us (1%)
    all_to_all x5, waiting for transfers between devices, swap(): return lax.all_to_all(values, axis, 0, 0, tiled=False)  56.1 us
    all_to_all x5, starting transfers between devices, swap(): return lax.all_to_all(values, axis, 0, 0, tiled=False)  33.7 us
    ppermute x3, waiting for transfers between devices, ring(): down = lax.ppermute(down, ZRING, back)  19.2 us
    all_to_all x1, blocking collectives, swap(): return lax.all_to_all(values, axis, 0, 0, tiled=False)  8.69 us
    unnamed x18, local copies, waits for them, and re-layouts  8.36 us
    ppermute x3, starting transfers between devices, ring(): down = lax.ppermute(down, ZRING, back)  7.34 us
    ppermute x4, waiting for transfers between devices, ring(): up = lax.ppermute(up, ZRING, onward)  6.51 us
    pallas_call x1, Pallas kernels, attend(): pl.pallas_call(attend_kernel, in_specs=[pl.BlockSpec(memory_space=pltpu.S...  3.44 us
  transfers between devices with their start and end apart: 14, of which 8 were waited for; matrix products, arithmetic and copies ran while one was open for 3% of the time, Pallas kernels for 4%

profile of v1, /device:TPU:2, one launch (start us, length us, event | category | flops | bytes accessed | tf_op | source)
XLA Modules:
  0.0 161.0 jit_solution(14142640687406156963)
XLA Ops:
  0.0 0.0 copy-start.2
  0.0 1.0 copy-done.2
  1.0 0.0 copy-start.3
  1.0 1.0 copy-done.3
  2.1 0.0 copy-start.4
  2.1 0.0 copy-start.5
  2.1 1.2 pack_weights.1
  3.3 9.9 %all-to-all-start.1 = ((bf16[16,32,512]{2,1,0:T(8,128)(2,1)}), bf16[16,32,512]{2,1,0:T(8,128)(2,1)S(1)}, u32[]{:S(2)}, u32[]{:S(2)}) async-start(bf16[16,32,512]{2,1,0:T(8,128)(2,1)} %pack_weights.1), calls=%async_computation.1 | async-start | bytes 1048576 | tf_op jit(solution)/shard_map/all_to_all | solution.py:307
  13.3 0.2 collective-permute-start
  14.1 14.4 %all-to-all-done.1 = bf16[16,32,512]{2,1,0:T(8,128)(2,1)S(1)} async-done(((bf16[16,32,512]{2,1,0:T(8,128)(2,1)}), bf16[16,32,512]{2,1,0:T(8,128)(2,1)S(1)}, u32[]{:S(2)}, u32[]{:S(2)}) %all-to-all-start.1) | async-done | bytes 524320 | tf_op jit(solution)/shard_map/all_to_all | solution.py:307
  28.6 0.0 collective-permute-start.8
  28.6 0.0 collective-permute-done
  28.6 0.9 select_bitcast_fusion.3
  29.5 0.5 collective-permute-start.1
  29.9 0.3 fusion
  30.4 0.7 reshape.60
  31.2 0.1 stack.92.index_ref
  31.2 2.9 %collective-permute-start.2 = (bf16[2,64,512]{2,1,0:T(8,128)(2,1)S(1)}, bf16[2,64,512]{2,1,0:T(8,128)(2,1)}, u32[]{:S(2)}, u32[]{:S(2)}) collective-permute-start(bf16[2,64,512]{2,1,0:T(8,128)(2,1)S(1)} %pad_maximum_fusion.1), channel_id=1, source_target_pairs={{0,14},{2,0},{4,2},{6,4},{8,6},{10,8},{12,10},{14,12},{1,15},{3,1}... | collective-permute-start | bytes 393224 | tf_op jit(solution)/shard_map/ppermute | solution.py:328
  34.1 2.6 %collective-permute-done.1 = bf16[2,64,512]{2,1,0:T(8,128)(2,1)S(1)} collective-permute-done((bf16[2,64,512]{2,1,0:T(8,128)(2,1)S(1)}, bf16[2,64,512]{2,1,0:T(8,128)(2,1)S(1)}, u32[]{:S(2)}, u32[]{:S(2)}) %collective-permute-start.1) | collective-permute-done | bytes 131104 | tf_op jit(solution)/shard_map/ppermute | solution.py:324
  36.7 0.0 collective-permute-start.3
  36.7 0.0 collective-permute-done.8
  36.7 0.1 select_bitcast_fusion.1
  36.7 0.1 pad_maximum_fusion.weight_ref
  36.9 0.0 copy-done.4
  36.9 0.0 copy-done.5
  36.9 3.4 %partial_products.1 = bf16[16,96,256]{2,1,0:T(8,128)(2,1)} custom-call(s32[1]{0:T(128)} %bitcast.23.t_ref, bf16[2,16,32,512]{3,2,1,0:T(8,128)(2,1)S(1)} %pad_maximum_fusion.weight_ref, bf16[256,512]{1,0:T(8,128)(2,1)S(1)} %copy-done.4, bf16[64,512]{1,0:T(8,128)(2,1)S(1)} %copy-done.5, f32[16,1,512]{2,1,0:T(1,128)S(1)} %bitcast.48), custom_call_target="tpu_custom_call" | custom-call | tf_op jit(solution)/shard_map/partial_products/pallas_call | solution.py:119
  40.3 6.4 %all-to-all-start.2 = ((bf16[16,96,256]{2,1,0:T(8,128)(2,1)}), bf16[16,96,256]{2,1,0:T(8,128)(2,1)S(1)}, u32[]{:S(2)}, u32[]{:S(2)}) async-start(bf16[16,96,256]{2,1,0:T(8,128)(2,1)} %partial_products.1), calls=%async_computation.2 | async-start | bytes 1572864 | tf_op jit(solution)/shard_map/all_to_all | solution.py:307
  46.7 0.0 collective-permute-done.2
  46.7 2.8 %collective-permute-start.4 = (bf16[2,64,512]{2,1,0:T(8,128)(2,1)}, bf16[2,64,512]{2,1,0:T(8,128)(2,1)S(1)}, u32[]{:S(2)}, u32[]{:S(2)}) collective-permute-start(bf16[2,64,512]{2,1,0:T(8,128)(2,1)} %collective-permute-done.2), channel_id=1, source_target_pairs={{0,14},{2,0},{4,2},{6,4},{8,6},{10,8},{12,10},{14,12},{1,15},{3,1}... | collective-permute-start | bytes 393224 | tf_op jit(solution)/shard_map/ppermute | solution.py:328
  49.5 0.9 bitcast_dynamic-update-slice_fusion.5
  50.4 0.0 collective-permute-done.3
  50.4 0.1 collective-permute-start.5
  50.5 17.3 %collective-permute-done.4 = bf16[2,64,512]{2,1,0:T(8,128)(2,1)S(1)} collective-permute-done((bf16[2,64,512]{2,1,0:T(8,128)(2,1)}, bf16[2,64,512]{2,1,0:T(8,128)(2,1)S(1)}, u32[]{:S(2)}, u32[]{:S(2)}) %collective-permute-start.4) | collective-permute-done | bytes 131104 | tf_op jit(solution)/shard_map/ppermute | solution.py:328
  67.8 1.7 %collective-permute-start.6 = (bf16[2,64,512]{2,1,0:T(8,128)(2,1)S(1)}, bf16[2,64,512]{2,1,0:T(8,128)(2,1)S(1)}, u32[]{:S(2)}, u32[]{:S(2)}) collective-permute-start(bf16[2,64,512]{2,1,0:T(8,128)(2,1)S(1)} %collective-permute-done.4), channel_id=1, source_target_pairs={{0,14},{2,0},{4,2},{6,4},{8,6},{10,8},{12,10},{14,12},{1,15},{3,1}... | collective-permute-start | bytes 393224 | tf_op jit(solution)/shard_map/ppermute | solution.py:328
  69.6 0.9 bitcast_dynamic-update-slice_fusion.4
  70.5 0.0 collective-permute-done.5
  70.5 0.4 collective-permute-start.7
  70.9 1.9 %collective-permute-done.6 = bf16[2,64,512]{2,1,0:T(8,128)(2,1)S(1)} collective-permute-done((bf16[2,64,512]{2,1,0:T(8,128)(2,1)S(1)}, bf16[2,64,512]{2,1,0:T(8,128)(2,1)S(1)}, u32[]{:S(2)}, u32[]{:S(2)}) %collective-permute-start.6) | collective-permute-done | bytes 131104 | tf_op jit(solution)/shard_map/ppermute | solution.py:328
  72.8 4.0 %collective-permute-done.7 = bf16[2,64,512]{2,1,0:T(8,128)(2,1)S(1)} collective-permute-done((bf16[2,64,512]{2,1,0:T(8,128)(2,1)S(1)}, bf16[2,64,512]{2,1,0:T(8,128)(2,1)S(1)}, u32[]{:S(2)}, u32[]{:S(2)}) %collective-permute-start.7) | collective-permute-done | bytes 131104 | tf_op jit(solution)/shard_map/ppermute | solution.py:324
  76.8 0.0 copy-start
  76.8 2.2 %copy-done = bf16[8192,256]{1,0:T(8,128)(2,1)S(1)} copy-done((bf16[8192,256]{1,0:T(8,128)(2,1)S(1)}, bf16[8192,256]{1,0:T(8,128)(2,1)}, u32[]{:S(2)}) %copy-start) | copy-done | bytes 4194328
  79.0 2.5 %queries.1 = bf16[64,256]{1,0:T(8,128)(2,1)S(1)} custom-call(s32[8]{0:T(128)S(1)} %stack.92.index_ref, bf16[8,2,64,512]{3,2,1,0:T(8,128)(2,1)S(1)} %bitcast_dynamic-update-slice_fusion.hidden_ref, bf16[8192,256]{1,0:T(8,128)(2,1)S(1)} %copy-done, f32[16,1,512]{2,1,0:T(1,128)S(1)} %bitcast.49, f32[64,128]{1,0:T(8,128)S(1)} %slice.16.cos_ref, ...), custom_call_target="tpu_custom_call" | custom-call | tf_op jit(solution)/shard_map/queries/pallas_call | solution.py:191
  81.5 0.0 all-to-all-done.2.parts_ref
  81.5 0.7 broadcast_in_dim.39
  82.2 4.4 %all-to-all-start = ((bf16[4,64,256]{2,1,0:T(8,128)(2,1)}), bf16[4,64,256]{2,1,0:T(8,128)(2,1)S(1)}, u32[]{:S(2)}, u32[]{:S(2)}) async-start(bf16[4,64,256]{2,1,0:T(8,128)(2,1)} %broadcast_in_dim.39), calls=%async_computation | async-start | bytes 262144 | tf_op jit(solution)/shard_map/all_to_all | solution.py:307
  86.6 0.2 finish_keys.1
  86.8 5.8 %all-to-all-done.query_ref = bf16[4,64,256]{2,1,0:T(8,128)(2,1)S(1)} async-done(((bf16[4,64,256]{2,1,0:T(8,128)(2,1)}), bf16[4,64,256]{2,1,0:T(8,128)(2,1)S(1)}, u32[]{:S(2)}, u32[]{:S(2)}) %all-to-all-start) | async-done | bytes 131104 | tf_op jit(solution)/shard_map/all_to_all | solution.py:307
  92.6 0.9 broadcast_in_dim.40
  93.5 4.6 %all-to-all-start.3 = ((bf16[16,80,256]{2,1,0:T(8,128)(2,1)}), bf16[16,80,256]{2,1,0:T(8,128)(2,1)S(1)}, u32[]{:S(2)}, u32[]{:S(2)}) async-start(bf16[16,80,256]{2,1,0:T(8,128)(2,1)} %broadcast_in_dim.40), calls=%async_computation.3 | async-start | bytes 1310720 | tf_op jit(solution)/shard_map/all_to_all | solution.py:307
  98.1 0.1 pad_add_fusion.info_ref
  98.1 10.6 %all-to-all-done.3 = bf16[16,80,256]{2,1,0:T(8,128)(2,1)S(1)} async-done(((bf16[16,80,256]{2,1,0:T(8,128)(2,1)}), bf16[16,80,256]{2,1,0:T(8,128)(2,1)S(1)}, u32[]{:S(2)}, u32[]{:S(2)}) %all-to-all-start.3) | async-done | bytes 655392 | tf_op jit(solution)/shard_map/all_to_all | solution.py:307
  108.8 3.4 %attend.1 = bf16[4,64,384]{2,1,0:T(8,128)(2,1)S(1)} custom-call(s32[3]{0:T(128)S(1)} %pad_add_fusion.info_ref, bf16[4,64,256]{2,1,0:T(8,128)(2,1)S(1)} %all-to-all-done.query_ref, bf16[4,4,80,256]{3,2,1,0:T(8,128)(2,1)S(1)} %bitcast.45), custom_call_target="tpu_custom_call" | custom-call | tf_op jit(solution)/shard_map/attend/pallas_call | solution.py:256
  112.2 8.7 %all_to_all.30.parts_ref = bf16[4,64,384]{2,1,0:T(8,128)(2,1)S(1)} all-to-all(bf16[4,64,384]{2,1,0:T(8,128)(2,1)S(1)} %attend.1), channel_id=1, replica_groups=mesh['xh'=2,'y'=4,'core'=2,'k'=4,'zl'=2,'xl'=2] {'y'}, dimensions={0} | all-to-all | bytes 393216 | tf_op jit(solution)/shard_map/all_to_all | solution.py:307
  120.9 0.0 copy-start.1
  120.9 2.2 %copy-done.1 = bf16[256,8192]{1,0:T(8,128)(2,1)S(1)} copy-done((bf16[256,8192]{1,0:T(8,128)(2,1)S(1)}, bf16[256,8192]{1,0:T(8,128)(2,1)}, u32[]{:S(2)}) %copy-start.1) | copy-done | bytes 4194328
  123.1 2.8 %project.1 = bf16[16,64,512]{2,1,0:T(8,128)(2,1)} custom-call(bf16[4,64,384]{2,1,0:T(8,128)(2,1)S(1)} %all_to_all.30.parts_ref, bf16[256,8192]{1,0:T(8,128)(2,1)S(1)} %copy-done.1), custom_call_target="tpu_custom_call" | custom-call | tf_op jit(solution)/shard_map/project/pallas_call | solution.py:291
  125.9 8.3 %all-to-all-start.5 = ((bf16[16,64,512]{2,1,0:T(8,128)(2,1)}), bf16[16,64,512]{2,1,0:T(8,128)(2,1)S(1)}, u32[]{:S(2)}, u32[]{:S(2)}) async-start(bf16[16,64,512]{2,1,0:T(8,128)(2,1)} %project.1), calls=%async_computation.5 | async-start | bytes 2097152 | tf_op jit(solution)/shard_map/all_to_all | solution.py:307
  134.8 25.3 %all-to-all-done.5 = bf16[16,64,512]{2,1,0:T(8,128)(2,1)S(1)} async-done(((bf16[16,64,512]{2,1,0:T(8,128)(2,1)}), bf16[16,64,512]{2,1,0:T(8,128)(2,1)S(1)}, u32[]{:S(2)}, u32[]{:S(2)}) %all-to-all-start.5) | async-done | bytes 1048608 | tf_op jit(solution)/shard_map/all_to_all | solution.py:307
  160.1 0.1 convert_reduce_fusion
  160.3 0.7 select_convert_fusion
  (14 shorter events, 0.1 us)
Async XLA Ops:
  0.0 1.0 copy-start.2
  1.0 1.0 copy-start.3
  2.1 34.8 %copy-start.4 = (bf16[256,512]{1,0:T(8,128)(2,1)S(1)}, bf16[256,512]{1,0:T(8,128)(2,1)}, u32[]{:S(2)}) copy-start(bf16[256,512]{1,0:T(8,128)(2,1)} %prompt_ref.1) | copy-start | bytes 786436
  2.1 34.8 %copy-start.5 = (bf16[64,512]{1,0:T(8,128)(2,1)S(1)}, bf16[64,512]{1,0:T(8,128)(2,1)}, u32[]{:S(2)}) copy-start(bf16[64,512]{1,0:T(8,128)(2,1)} %resp_ref.1) | copy-start | bytes 196612
  3.3 25.3 %all-to-all-start.1 = ((bf16[16,32,512]{2,1,0:T(8,128)(2,1)}), bf16[16,32,512]{2,1,0:T(8,128)(2,1)S(1)}, u32[]{:S(2)}, u32[]{:S(2)}) async-start(bf16[16,32,512]{2,1,0:T(8,128)(2,1)} %pack_weights.1), calls=%async_computation.1 | async-start | bytes 1048576 | tf_op jit(solution)/shard_map/all_to_all | solution.py:307
  13.3 15.3 %collective-permute-start = (bf16[64,512]{1,0:T(8,128)(2,1)}, bf16[64,512]{1,0:T(8,128)(2,1)S(1)}, u32[]{:S(2)}, u32[]{:S(2)}) collective-permute-start(bf16[64,512]{1,0:T(8,128)(2,1)} %resp_ref.1), channel_id=1, source_target_pairs={{0,1},{1,0},{2,3},{3,2},{4,5},{5,4},{6,7},{7,6},{8,9},{9,8},{10,11... | collective-permute-start | bytes 196616 | tf_op jit(solution)/shard_map/ppermute | solution.py:315
  28.6 8.1 %collective-permute-start.8 = (bf16[16,32,512]{2,1,0:T(8,128)(2,1)S(1)}, bf16[16,32,512]{2,1,0:T(8,128)(2,1)S(1)}, u32[]{:S(2)}, u32[]{:S(2)}) collective-permute-start(bf16[16,32,512]{2,1,0:T(8,128)(2,1)S(1)} %all-to-all-done.1), channel_id=1, source_target_pairs={{0,16},{16,0},{1,17},{17,1},{2,18},{18,2},{3,19},{19,3},{4,20},{20... | collective-permute-start | bytes 1572872 | tf_op jit(solution)/shard_map/ppermute | solution.py:366
  29.5 7.2 %collective-permute-start.1 = (bf16[2,64,512]{2,1,0:T(8,128)(2,1)S(1)}, bf16[2,64,512]{2,1,0:T(8,128)(2,1)S(1)}, u32[]{:S(2)}, u32[]{:S(2)}) collective-permute-start(bf16[2,64,512]{2,1,0:T(8,128)(2,1)S(1)} %pad_maximum_fusion.1), channel_id=1, source_target_pairs={{0,2},{2,4},{4,6},{6,8},{8,10},{10,12},{12,14},{14,0},{1,3},{3,5},... | collective-permute-start | bytes 393224 | tf_op jit(solution)/shard_map/ppermute | solution.py:324
  31.2 15.5 %collective-permute-start.2 = (bf16[2,64,512]{2,1,0:T(8,128)(2,1)S(1)}, bf16[2,64,512]{2,1,0:T(8,128)(2,1)}, u32[]{:S(2)}, u32[]{:S(2)}) collective-permute-start(bf16[2,64,512]{2,1,0:T(8,128)(2,1)S(1)} %pad_maximum_fusion.1), channel_id=1, source_target_pairs={{0,14},{2,0},{4,2},{6,4},{8,6},{10,8},{12,10},{14,12},{1,15},{3,1}... | collective-permute-start | bytes 393224 | tf_op jit(solution)/shard_map/ppermute | solution.py:328
  36.7 13.8 %collective-permute-start.3 = (bf16[2,64,512]{2,1,0:T(8,128)(2,1)S(1)}, bf16[2,64,512]{2,1,0:T(8,128)(2,1)}, u32[]{:S(2)}, u32[]{:S(2)}) collective-permute-start(bf16[2,64,512]{2,1,0:T(8,128)(2,1)S(1)} %collective-permute-done.1), channel_id=1, source_target_pairs={{0,2},{2,4},{4,6},{6,8},{8,10},{10,12},{12,14},{14,0},{1,3},{3,5},... | collective-permute-start | bytes 393224 | tf_op jit(solution)/shard_map/ppermute | solution.py:324
  40.3 41.2 %all-to-all-start.2 = ((bf16[16,96,256]{2,1,0:T(8,128)(2,1)}), bf16[16,96,256]{2,1,0:T(8,128)(2,1)S(1)}, u32[]{:S(2)}, u32[]{:S(2)}) async-start(bf16[16,96,256]{2,1,0:T(8,128)(2,1)} %partial_products.1), calls=%async_computation.2 | async-start | bytes 1572864 | tf_op jit(solution)/shard_map/all_to_all | solution.py:307
  46.7 21.1 %collective-permute-start.4 = (bf16[2,64,512]{2,1,0:T(8,128)(2,1)}, bf16[2,64,512]{2,1,0:T(8,128)(2,1)S(1)}, u32[]{:S(2)}, u32[]{:S(2)}) collective-permute-start(bf16[2,64,512]{2,1,0:T(8,128)(2,1)} %collective-permute-done.2), channel_id=1, source_target_pairs={{0,14},{2,0},{4,2},{6,4},{8,6},{10,8},{12,10},{14,12},{1,15},{3,1}... | collective-permute-start | bytes 393224 | tf_op jit(solution)/shard_map/ppermute | solution.py:328
  50.4 20.0 %collective-permute-start.5 = (bf16[2,64,512]{2,1,0:T(8,128)(2,1)}, bf16[2,64,512]{2,1,0:T(8,128)(2,1)S(1)}, u32[]{:S(2)}, u32[]{:S(2)}) collective-permute-start(bf16[2,64,512]{2,1,0:T(8,128)(2,1)} %collective-permute-done.3), channel_id=1, source_target_pairs={{0,2},{2,4},{4,6},{6,8},{8,10},{10,12},{12,14},{14,0},{1,3},{3,5},... | collective-permute-start | bytes 393224 | tf_op jit(solution)/shard_map/ppermute | solution.py:324
  67.8 5.0 %collective-permute-start.6 = (bf16[2,64,512]{2,1,0:T(8,128)(2,1)S(1)}, bf16[2,64,512]{2,1,0:T(8,128)(2,1)S(1)}, u32[]{:S(2)}, u32[]{:S(2)}) collective-permute-start(bf16[2,64,512]{2,1,0:T(8,128)(2,1)S(1)} %collective-permute-done.4), channel_id=1, source_target_pairs={{0,14},{2,0},{4,2},{6,4},{8,6},{10,8},{12,10},{14,12},{1,15},{3,1}... | collective-permute-start | bytes 393224 | tf_op jit(solution)/shard_map/ppermute | solution.py:328
  70.5 6.3 %collective-permute-start.7 = (bf16[2,64,512]{2,1,0:T(8,128)(2,1)S(1)}, bf16[2,64,512]{2,1,0:T(8,128)(2,1)S(1)}, u32[]{:S(2)}, u32[]{:S(2)}) collective-permute-start(bf16[2,64,512]{2,1,0:T(8,128)(2,1)S(1)} %collective-permute-done.5), channel_id=1, source_target_pairs={{0,2},{2,4},{4,6},{6,8},{8,10},{10,12},{12,14},{14,0},{1,3},{3,5},... | collective-permute-start | bytes 393224 | tf_op jit(solution)/shard_map/ppermute | solution.py:324
  76.8 2.2 %copy-start = (bf16[8192,256]{1,0:T(8,128)(2,1)S(1)}, bf16[8192,256]{1,0:T(8,128)(2,1)}, u32[]{:S(2)}) copy-start(bf16[8192,256]{1,0:T(8,128)(2,1)} %weight_ref.2) | copy-start | bytes 12582916
  82.2 10.4 %all-to-all-start = ((bf16[4,64,256]{2,1,0:T(8,128)(2,1)}), bf16[4,64,256]{2,1,0:T(8,128)(2,1)S(1)}, u32[]{:S(2)}, u32[]{:S(2)}) async-start(bf16[4,64,256]{2,1,0:T(8,128)(2,1)} %broadcast_in_dim.39), calls=%async_computation | async-start | bytes 262144 | tf_op jit(solution)/shard_map/all_to_all | solution.py:307
  93.5 15.3 %all-to-all-start.3 = ((bf16[16,80,256]{2,1,0:T(8,128)(2,1)}), bf16[16,80,256]{2,1,0:T(8,128)(2,1)S(1)}, u32[]{:S(2)}, u32[]{:S(2)}) async-start(bf16[16,80,256]{2,1,0:T(8,128)(2,1)} %broadcast_in_dim.40), calls=%async_computation.3 | async-start | bytes 1310720 | tf_op jit(solution)/shard_map/all_to_all | solution.py:307
  120.9 2.2 %copy-start.1 = (bf16[256,8192]{1,0:T(8,128)(2,1)S(1)}, bf16[256,8192]{1,0:T(8,128)(2,1)}, u32[]{:S(2)}) copy-start(bf16[256,8192]{1,0:T(8,128)(2,1)} %weight_ref.3) | copy-start | bytes 12582916
  125.9 34.2 %all-to-all-start.5 = ((bf16[16,64,512]{2,1,0:T(8,128)(2,1)}), bf16[16,64,512]{2,1,0:T(8,128)(2,1)S(1)}, u32[]{:S(2)}, u32[]{:S(2)}) async-start(bf16[16,64,512]{2,1,0:T(8,128)(2,1)} %project.1), calls=%async_computation.5 | async-start | bytes 2097152 | tf_op jit(solution)/shard_map/all_to_all | solution.py:307

commit v2 on v1

v2 whole, which is shorter than its diff:
```python
import functools
import math

import jax
import jax.numpy as jnp
from jax import lax
from jax.experimental import pallas as pl
from jax.experimental.pallas import tpu as pltpu
from jax.sharding import Mesh
from jax.sharding import PartitionSpec as P

PARTS = (("xh", 2), ("y", 4), ("core", 2), ("k", 4), ("zl", 2), ("xl", 2))
SAMPLE = ("xh", "y", "core")
TENSOR = ("k", "zl", "xl")
ZRING = ("k", "zl")
OWN_HEAD = ("zl", "xl")
KEY_GROUP = ("xh", "core", "zl", "xl")

D = 8192
BLOCK = 512
HEAD_DIM = 128
HALF = 64
RESP = 64
PROMPT_ROWS = 256
ROWS = 80
SENT_ROWS = 2 * ROWS + 16
EPSILON = 1e-05
ROPE_BASE = 500000.0
NEG_BIG = -1e30
CORE_AT, XL_AT, T_AT, Y_AT, PLACE_AT, LENGTH_AT, Z_AT = 0, 1, 2, 3, 4, 5, 6
RING = (0, 7, 1, 6, 2, 5, 3, 4)
F32 = jnp.float32
BF16 = jnp.bfloat16
SMALL = 12 * 1024 * 1024


def iota(shape, dim):
    return lax.broadcasted_iota(jnp.int32, shape, dim)


def dot_t(a, b):
    return lax.dot_general(a, b, (((1,), (1,)), ((), ())), preferred_element_type=F32)


def dot(a, b):
    return lax.dot_general(a, b, (((1,), (0,)), ((), ())), preferred_element_type=F32)


def params(limit=None):
    return pltpu.CompilerParams(vmem_limit_bytes=limit)


def pack_kernel(info_ref, key_ref, value_ref, out_ref):
    row, col = iota((16, 64), 0), iota((16, 64), 1)
    source = (row >> 3) * 32 + (row & 7) * 4 + info_ref[0]
    pick = jnp.where(col == source, 1.0, 0.0).astype(BF16)
    both = jnp.concatenate([key_ref[...], value_ref[...]], axis=0)
    for i in range(out_ref.shape[0]):
        out_ref[i] = dot(pick, both[:, i * BLOCK : (i + 1) * BLOCK]).astype(BF16)


def pack_weights(head, key_rows, value_rows):
    steps = 2
    each = 16 // steps
    return pl.pallas_call(
        pack_kernel,
        grid=(steps,),
        in_specs=[
            pl.BlockSpec(memory_space=pltpu.SMEM),
            pl.BlockSpec((32, each * BLOCK), lambda i: (0, i)),
            pl.BlockSpec((32, each * BLOCK), lambda i: (0, i)),
        ],
        out_specs=pl.BlockSpec((each, 16, BLOCK), lambda i: (i, 0, 0)),
        out_shape=jax.ShapeDtypeStruct((16, 16, BLOCK), BF16),
        compiler_params=params(),
        name="pack_weights",
    )(head, key_rows, value_rows)


def scale_kernel(info_ref, prompt_ref, resp_ref, gain_ref, scaled, sums, high, low):
    gain = gain_ref[info_ref[T_AT]]
    high[320:384] = jnp.zeros((64, BLOCK), BF16)
    low[320:384] = jnp.zeros((64, BLOCK), BF16)

    def put(at, count, values):
        values = values.astype(F32)
        scaled[at : at + count] = (values * gain).astype(BF16)
        square = values * values
        top = square.astype(BF16)
        high[at : at + count] = top
        low[at : at + count] = (square - top.astype(F32)).astype(BF16)

    for c in range(4):
        put(80 * c, 64, prompt_ref[64 * c : 64 * c + 64])
        put(80 * c + 64, 16, resp_ref[16 * c : 16 * c + 16])
    ones = jnp.ones((16, BLOCK), BF16)
    row = iota((16, 128), 0)
    for c in range(4):
        total = dot_t(ones, high[80 * c : 80 * c + 128]) + dot_t(ones, low[80 * c : 80 * c + 128])
        top = total.astype(BF16).astype(F32)
        rest = total - top
        sums[c] = jnp.where(row == 0, top, jnp.where(row == 1, rest, 0.0)).astype(BF16)


def scale_rows(info, prompt, resp, gain):
    vmem = pl.BlockSpec(memory_space=pltpu.VMEM)
    return pl.pallas_call(
        scale_kernel,
        in_specs=[pl.BlockSpec(memory_space=pltpu.SMEM), vmem, vmem, vmem],
        out_shape=(jax.ShapeDtypeStruct((320, BLOCK), BF16), jax.ShapeDtypeStruct((4, 16, 128), BF16)),
        scratch_shapes=[pltpu.VMEM((384, BLOCK), BF16), pltpu.VMEM((384, BLOCK), BF16)],
        compiler_params=params(SMALL),
        name="scale_rows",
    )(info, prompt, resp, gain)


def partial_kernel(count, heads_ref, scaled_ref, sums_ref, *refs):
    pieces, out_ref = refs[:count], refs[-1]
    for i in range(count):

        @pl.when(pl.program_id(0) == i)
        def _(i=i):
            raw = dot_t(scaled_ref[...], pieces[i][...].reshape(256, BLOCK)).astype(BF16)
            for c in range(4):
                mine = raw[ROWS * c : ROWS * c + ROWS]
                out_ref[c, :ROWS] = mine[:, :128]
                out_ref[c, ROWS : 2 * ROWS] = mine[:, 128:]
                out_ref[c, 2 * ROWS :] = sums_ref[c]


def partial_products(heads, scaled, sums, pieces, before=None):
    def whole(shape):
        return pl.BlockSpec(shape, lambda i, heads: (0,) * len(shape))

    count = len(pieces)
    in_specs = [whole((320, BLOCK)), whole((4, 16, 128))] + [whole((16, 16, BLOCK))] * count
    operands = [heads, scaled, sums, *pieces]
    aliases = {}
    if before is not None:
        in_specs.append(pl.BlockSpec(memory_space=pl.ANY))
        operands.append(before)
        aliases = {len(operands) - 1: 0}
    return pl.pallas_call(
        functools.partial(partial_kernel, count),
        grid_spec=pltpu.PrefetchScalarGridSpec(
            num_scalar_prefetch=1,
            grid=(count,),
            in_specs=in_specs,
            out_specs=pl.BlockSpec((4, SENT_ROWS, 128), lambda i, heads: (heads[i], 0, 0)),
        ),
        out_shape=jax.ShapeDtypeStruct((16, SENT_ROWS, 128), BF16),
        input_output_aliases=aliases,
        compiler_params=params(SMALL),
        name="partial_products",
    )(*operands)


def turn(values, cosine, sine):
    return values * cosine + pltpu.roll(values, HALF, 1) * sine


def finish_kernel(parts_ref, cos_ref, sin_ref, out_ref):
    total = jnp.sum(parts_ref[...].astype(F32), axis=0)
    sums = total[2 * ROWS : 2 * ROWS + 1] + total[2 * ROWS + 1 : 2 * ROWS + 2]
    diagonal = iota((ROWS, 128), 0) == iota((ROWS, 128), 1)
    column = jnp.sum(jnp.where(diagonal, jnp.broadcast_to(sums, (ROWS, 128)), 0.0), axis=1, keepdims=True)
    factor = lax.rsqrt(column * (1.0 / D) + EPSILON)
    raw = jnp.concatenate([total[:ROWS] * factor, total[ROWS : 2 * ROWS] * factor], axis=1).astype(BF16)
    row, col = iota((256, 256), 0), iota((256, 256), 1)
    target = ((row >> 3) & 1) * 128 + (row >> 4) * 8 + (row & 7)
    ordered = dot(raw, jnp.where(col == target, 1.0, 0.0).astype(BF16))
    keys = turn(ordered[:, :HEAD_DIM], cos_ref[:ROWS], sin_ref[:ROWS]).astype(BF16)
    values = ordered[:, HEAD_DIM:].astype(BF16)
    for i in range(out_ref.shape[0]):
        out_ref[i, :, :HEAD_DIM] = keys
        out_ref[i, :, HEAD_DIM:] = values


def finish_keys(parts, cosine, sine):
    return pl.pallas_call(
        finish_kernel,
        out_shape=jax.ShapeDtypeStruct((16, ROWS, 256), BF16),
        compiler_params=params(SMALL),
        name="finish_keys",
    )(parts, cosine, sine)


def query_kernel(info_ref, gain_ref, cos_ref, sin_ref, weight_ref, *refs):
    blocks, (out_ref, weights, hiddens, weight_sems, hidden_sems) = refs[:8], refs[8:]
    xl = info_ref[XL_AT]
    places = [(info_ref[Z_AT] + step) % 8 for step in RING]
    copies = []
    for i, z in enumerate(places):
        rows = pl.ds(pl.multiple_of(z * 2 * BLOCK, 2 * BLOCK), 2 * BLOCK)
        copies.append(
            (
                pltpu.make_async_copy(weight_ref.at[rows], weights.at[i], weight_sems.at[i]),
                pltpu.make_async_copy(blocks[i], hiddens.at[i], hidden_sems.at[i]),
            )
        )
    for copy in copies:
        copy[0].start()
        copy[1].start()
    total = jnp.zeros((RESP, 256), F32)
    squares = jnp.zeros((RESP, 1), F32)
    for i, z in enumerate(places):
        copies[i][0].wait()
        copies[i][1].wait()
        for j in range(2):
            x = j ^ xl
            hidden = hiddens[i, j].astype(F32)
            scaled = (hidden * gain_ref[2 * z + x]).astype(BF16)
            total += dot(scaled, weights[i, pl.ds(pl.multiple_of(x * BLOCK, BLOCK), BLOCK)])
            squares += jnp.sum(hidden * hidden, axis=1, keepdims=True)
    factor = lax.rsqrt(squares * (1.0 / D) + EPSILON)
    for h in range(2):
        part = slice(h * HEAD_DIM, (h + 1) * HEAD_DIM)
        query = turn(total[:, part] * factor, cos_ref[ROWS:], sin_ref[ROWS:])
        out_ref[:, part] = query.astype(BF16)


def queries_of(info, gain, weight, cosine, sine, blocks):
    vmem, anywhere = pl.BlockSpec(memory_space=pltpu.VMEM), pl.BlockSpec(memory_space=pl.ANY)
    return pl.pallas_call(
        query_kernel,
        in_specs=[pl.BlockSpec(memory_space=pltpu.SMEM)] + [vmem] * 3 + [anywhere] * 9,
        out_shape=jax.ShapeDtypeStruct((RESP, 256), BF16),
        scratch_shapes=[
            pltpu.VMEM((8, 2 * BLOCK, 256), BF16),
            pltpu.VMEM((8, 2, RESP, BLOCK), BF16),
            pltpu.SemaphoreType.DMA((8,)),
            pltpu.SemaphoreType.DMA((8,)),
        ],
        compiler_params=params(SMALL),
        name="queries",
    )(info, gain, cosine, sine, weight, *blocks)


def attend_kernel(info_ref, rows_ref, *refs):
    queries, outs = refs[:4], refs[4:]
    own_y = info_ref[Y_AT]
    rows = rows_ref[...].reshape(16, ROWS, 256)
    prompt = rows[:, :64].reshape(1024, 256)
    prompt_keys, prompt_values = prompt[:, :HEAD_DIM], prompt[:, HEAD_DIM:]
    own = rows_ref[info_ref[PLACE_AT]]
    own = own[:, 64:].reshape(RESP, 256)
    own_keys, own_values = own[:, :HEAD_DIM], own[:, HEAD_DIM:]
    scale = HEAD_DIM ** (-0.5)
    power = scale * math.log2(math.e)

    column = iota((1, 1024), 1)
    place = column >> 8
    sample = (place >> 1) * 8 + own_y * 2 + (place & 1)
    live = sample * PROMPT_ROWS + (column & 255) < info_ref[LENGTH_AT]
    causal = iota((2 * RESP, RESP), 1) <= (iota((2 * RESP, RESP), 0) & (RESP - 1))
    lane = iota((RESP, 128), 1)

    for i in range(4):
        query = jnp.concatenate([queries[i][:, :HEAD_DIM], queries[i][:, HEAD_DIM:]], axis=0)
        far = jnp.where(live, dot_t(query, prompt_keys), NEG_BIG)
        top = jnp.max(far, axis=1, keepdims=True)
        if i == 0:
            near = jnp.where(causal, dot_t(query, own_keys), NEG_BIG)
            top = jnp.maximum(top, jnp.max(near, axis=1, keepdims=True))
        top = jnp.maximum(top, 0.5 * NEG_BIG)
        far = jnp.exp2((far - top) * power)
        total = jnp.sum(far, axis=1, keepdims=True)
        summed = dot(far.astype(BF16), prompt_values)
        if i == 0:
            near = jnp.exp2((near - top) * power)
            total += jnp.sum(near, axis=1, keepdims=True)
            summed += dot(near.astype(BF16), own_values)
        some = total > 0.0
        safe = jnp.where(some, total, 1.0)
        result = (summed / safe).astype(BF16)
        level = jnp.where(some, top * scale + jnp.log(safe), NEG_BIG)
        first = level.astype(BF16).astype(F32)
        rest = level - first
        second = rest.astype(BF16).astype(F32)
        third = rest - second
        extra = jnp.zeros((RESP, 128), F32)
        for h in range(2):
            mine = slice(h * RESP, (h + 1) * RESP)
            outs[i][:, h * HEAD_DIM : (h + 1) * HEAD_DIM] = result[mine]
            for n, piece in enumerate((first, second, third)):
                extra = jnp.where(lane == 3 * h + n, piece[mine], extra)
        outs[i][:, 256:] = extra.astype(BF16)


def attend(info, rows, queries):
    vmem = pl.BlockSpec(memory_space=pltpu.VMEM)
    return pl.pallas_call(
        attend_kernel,
        in_specs=[pl.BlockSpec(memory_space=pltpu.SMEM)] + [vmem] * 5,
        out_shape=(jax.ShapeDtypeStruct((RESP, 384), BF16),) * 4,
        compiler_params=params(SMALL),
        name="attend",
    )(info, rows, *queries)


def merge_kernel(*refs):
    parts, out_ref = refs[:4], refs[4]
    lane = iota((RESP, 128), 1)
    extras = [part[:, 256:].astype(F32) for part in parts]
    for h in range(2):
        head = slice(h * HEAD_DIM, (h + 1) * HEAD_DIM)
        mine = jnp.logical_and(lane >= 3 * h, lane < 3 * h + 3)
        levels = [jnp.sum(jnp.where(mine, e, 0.0), axis=1, keepdims=True) for e in extras]
        top = functools.reduce(jnp.maximum, levels)
        shares = [jnp.exp(level - top) for level in levels]
        total = functools.reduce(jnp.add, shares)
        pieces = [share * part[:, head].astype(F32) for share, part in zip(shares, parts)]
        out_ref[:, head] = (functools.reduce(jnp.add, pieces) / total).astype(BF16)


def merge(parts):
    vmem = pl.BlockSpec(memory_space=pltpu.VMEM)
    return pl.pallas_call(
        merge_kernel,
        in_specs=[vmem] * 4,
        out_shape=jax.ShapeDtypeStruct((RESP, 256), BF16),
        compiler_params=params(SMALL),
        name="merge",
    )(*parts)


def z_of(i, info):
    return (4 * info[CORE_AT] + 2 * (info[Y_AT] % 2)) ^ i


def project_kernel(info_ref, own_ref, other_ref, own_weight, *refs):
    cross, out_ref = refs[:4], refs[4]
    for i in range(8):
        result = dot(own_ref[...], own_weight[:, pl.ds(i * BLOCK, BLOCK)])
        result += dot(other_ref[...], cross[i // 2][:, pl.ds((i % 2) * BLOCK, BLOCK)])
        out_ref[z_of(i, info_ref)] = result.astype(BF16)


def project(info, own, other, own_weight, cross):
    vmem = pl.BlockSpec(memory_space=pltpu.VMEM)
    return pl.pallas_call(
        project_kernel,
        in_specs=[pl.BlockSpec(memory_space=pltpu.SMEM)] + [vmem] * 7,
        out_shape=jax.ShapeDtypeStruct((8, RESP, BLOCK), BF16),
        compiler_params=params(SMALL),
        name="project",
    )(info, own, other, own_weight, *cross)


def pick_kernel(info_ref, own_ref, other_ref, out_ref, sent_ref):
    out_ref[...] = own_ref[...]

    @pl.when(pl.program_id(0) < 2)
    def _():
        sent_ref[...] = other_ref[...]


def pick_columns(info, weight):
    def other_at(i, info):
        return 0, 2 * z_of(jnp.minimum(i, 1), info) + 1 - info[XL_AT]

    return pl.pallas_call(
        pick_kernel,
        grid_spec=pltpu.PrefetchScalarGridSpec(
            num_scalar_prefetch=1,
            grid=(8,),
            in_specs=[
                pl.BlockSpec((256, BLOCK), lambda i, info: (0, 2 * z_of(i, info) + info[XL_AT])),
                pl.BlockSpec((256, BLOCK), other_at),
            ],
            out_specs=[
                pl.BlockSpec((256, BLOCK), lambda i, info: (0, i)),
                pl.BlockSpec((256, BLOCK), lambda i, info: (0, jnp.minimum(i, 1))),
            ],
        ),
        out_shape=(
            jax.ShapeDtypeStruct((256, 8 * BLOCK), BF16),
            jax.ShapeDtypeStruct((256, 2 * BLOCK), BF16),
        ),
        compiler_params=params(SMALL),
        name="pick_columns",
    )(info, weight, weight)


def swap(values, axis):
    return lax.all_to_all(values, axis, 0, 0, tiled=False)


def body(
    response_hidden,
    prompt_hidden,
    norm_gain,
    query_weight,
    key_weight,
    value_weight,
    output_weight,
    response_lengths,
    prompt_length,
):
    length = prompt_length[0]
    core, y = lax.axis_index("core"), lax.axis_index("y")
    sample, quarter = lax.axis_index(SAMPLE), lax.axis_index(OWN_HEAD)
    gain = norm_gain.astype(F32).reshape(16, 1, BLOCK)

    row = jnp.arange(144, dtype=jnp.int32)
    positions = jnp.where(
        row < 64,
        sample * PROMPT_ROWS + quarter * 64 + row,
        jnp.where(row < 80, length + quarter * 16 + row - 64, length + row - 80),
    )
    lane = jnp.arange(HEAD_DIM, dtype=jnp.int32)
    inverse = ROPE_BASE ** (-((lane % HALF).astype(F32) * 2.0 / HEAD_DIM))
    angles = positions.astype(F32)[:, None] * inverse[None, :]
    cosine = jnp.cos(angles)
    sine = jnp.sin(angles) * jnp.where(lane < HALF, -1.0, 1.0)[None, :]

    xl, z = lax.axis_index("xl"), lax.axis_index(ZRING)
    info = jnp.stack(
        [core, xl, lax.axis_index(TENSOR), y, lax.axis_index(("xh", "core")), length, z]
    ).astype(jnp.int32)
    flip = [(0, 1), (1, 0)]
    onward = [(i, (i + 1) % 8) for i in range(8)]
    back = [(i, (i + 7) % 8) for i in range(8)]

    def up(values):
        return lax.ppermute(values, ZRING, onward)

    def down(values):
        return lax.ppermute(values, ZRING, back)

    packed = pack_weights(y.reshape(1), key_weight.T, value_weight.T)
    beside = lax.ppermute(response_hidden, "xl", flip)
    weights = swap(packed, TENSOR)
    pair = jnp.stack([response_hidden, beside])
    up1, down1 = up(pair), down(pair)
    four = lax.ppermute(pair, ZRING, [(i, (i + 4) % 8) for i in range(8)])
    scaled, sums = scale_rows(info, prompt_hidden, response_hidden, gain)
    own, sent = pick_columns(info, output_weight)
    weights, pair, scaled, sums, own, sent = lax.optimization_barrier((weights, pair, scaled, sums, own, sent))
    one, two, three = (
        lax.ppermute(weights, "y", [(i, i ^ step) for i in range(4)]) for step in (1, 2, 3)
    )
    first = lax.ppermute(sent, "xl", flip)
    up2, down2 = up(up1), down(down1)
    heads = jnp.stack([y, y ^ 1, y ^ 3]).astype(jnp.int32)
    products = partial_products(heads, scaled, sums, (weights, one, three))
    products = partial_products((y ^ 2).reshape(1), scaled, sums, (two,), products)
    products, up2, down2, first, four = lax.optimization_barrier((products, up2, down2, first, four))
    products = swap(products, TENSOR)
    up3, down3 = up(up2), down(down2)
    second = lax.ppermute(first, "y", [(i, i ^ 1) for i in range(4)])
    products, up3, down3, second = lax.optimization_barrier((products, up3, down3, second))
    blocks = (pair, up1, down1, up2, down2, up3, down3, four)
    queries = queries_of(info, gain, query_weight, cosine, sine, blocks)
    cross = (first, second, lax.ppermute(first, "core", flip), lax.ppermute(second, "core", flip))
    rows = finish_keys(products, cosine, sine)
    rows = swap(rows, KEY_GROUP).reshape(4, 4, ROWS, 256)

    def along(values, step):
        return lax.ppermute(values, "y", [(i, (i + step) % 4) for i in range(4)])

    pooled = [queries] + [along(queries, step) for step in (1, 2, 3)]
    rows, cross = lax.optimization_barrier((rows, cross))
    parts = attend(info, rows, pooled)
    attention = merge([parts[0]] + [along(parts[step], -step) for step in (1, 2, 3)])
    other = lax.ppermute(attention, "xl", flip)
    partial = project(info, attention, other, own, cross)
    summed = jnp.sum(swap(partial, ZRING).astype(F32), axis=0)
    live = jnp.arange(RESP, dtype=jnp.int32) < response_lengths[0]
    return jnp.where(live[:, None], summed, 0.0).astype(BF16)


def solution(mesh):
    names = tuple(name for name, _ in PARTS)
    sizes = tuple(size for _, size in PARTS)
    fine = Mesh(mesh.devices.reshape(sizes), names)
    return jax.shard_map(
        body,
        mesh=fine,
        in_specs=(
            P(SAMPLE, TENSOR),
            P(SAMPLE, TENSOR),
            P(),
            P(None, TENSOR),
            P(None, TENSOR),
            P(None, TENSOR),
            P(TENSOR, None),
            P(SAMPLE),
            P(),
        ),
        out_specs=P(SAMPLE, TENSOR),
        check_vma=False,
    )
```

time: 162 us -> 135 us (0.83)
  waiting for transfers between devices: 81.9 us -> 41.4 us
  starting transfers between devices: 42.2 us -> 52.4 us
  blocking collectives: 8.69 us -> 0 us
  local copies, waits for them, and re-layouts: 10 us -> 17.8 us
  Pallas kernels: 13.5 us -> 18.7 us
    all_to_all x5 -> x4, waiting for transfers between devices: 56.1 us -> 16.3 us  [swap(): return lax.all_to_all(values, axis, 0, 0, tiled=False)]
    ppermute x9 -> x22, starting transfers between devices: 8.46 us -> 27.4 us  [the longest x3 6.13 us: body(): lax.ppermute(weights, 'y', [(i, i ^ step) for i in range(4)])]
    unnamed x18 -> x42, local copies, waits for them, and re-layouts: 8.36 us -> 17.7 us
    all_to_all x1 -> x0, blocking collectives: 8.69 us -> none  [swap(): return lax.all_to_all(values, axis, 0, 0, tiled=False)]
    all_to_all x5 -> x4, starting transfers between devices: 33.7 us -> 25.1 us  [swap(): return lax.all_to_all(values, axis, 0, 0, tiled=False)]
    pallas_call x4 -> x8, Pallas kernels: 8.84 us -> 14.4 us  [the longest x2 4.39 us: partial_products(): pl.pallas_call(functools.partial(partial_kernel, count), grid_spec=pltpu....]
    ppermute x9 -> x22, waiting for transfers between devices: 25.7 us -> 25.1 us  [the longest x3 13.2 us: up(): return lax.ppermute(values, ZRING, onward)]
  transfers between devices with their start and end apart: 14 -> 26, of which waited for: 8 -> 10; matrix products, arithmetic and copies ran while one was open for 3% -> 1% of each run, Pallas kernels for 4% -> 8%
where the time goes in v2:
time: 135 us; the launch traced here: 134 us
  starting transfers between devices  52.4 us (39%)
  waiting for transfers between devices  41.4 us (31%)
  Pallas kernels  18.7 us (14%)
  local copies, waits for them, and re-layouts  17.8 us (13%)
  other arithmetic  1.95 us (1%)
  between operations  1.46 us (1%)
    all_to_all x4, starting transfers between devices, swap(): return lax.all_to_all(values, axis, 0, 0, tiled=False)  25.1 us
    unnamed x42, local copies, waits for them, and re-layouts  17.7 us
    all_to_all x4, waiting for transfers between devices, swap(): return lax.all_to_all(values, axis, 0, 0, tiled=False)  16.3 us
    ppermute x3, waiting for transfers between devices, up(): return lax.ppermute(values, ZRING, onward)  13.2 us
    ppermute x6, waiting for transfers between devices, along(): return lax.ppermute(values, 'y', [(i, (i + step) % 4) for i in range(4)])  8.25 us
    ppermute x3, starting transfers between devices, body(): lax.ppermute(weights, 'y', [(i, i ^ step) for i in range(4)])  6.13 us
    ppermute x6, starting transfers between devices, along(): return lax.ppermute(values, 'y', [(i, (i + step) % 4) for i in range(4)])  5.79 us
    ppermute x3, starting transfers between devices, up(): return lax.ppermute(values, ZRING, onward)  5.31 us
  transfers between devices with their start and end apart: 26, of which 10 were waited for; matrix products, arithmetic and copies ran while one was open for 1% of the time, Pallas kernels for 8%

profile of v2, /device:TPU:2, one launch (start us, length us, event | category | flops | bytes accessed | tf_op | source)
XLA Modules:
  0.0 133.7 jit_solution(437670816903564371)
XLA Ops:
  0.0 2.1 %pack_weights.1 = bf16[16,16,512]{2,1,0:T(8,128)(2,1)} custom-call(s32[1]{0:T(128)} %bitcast.4.info_ref, bf16[32,8192]{1,0:T(8,128)(2,1)} %bitcast.24, bf16[32,8192]{1,0:T(8,128)(2,1)} %bitcast.25), custom_call_target="tpu_custom_call" | custom-call | tf_op jit(solution)/shard_map/pack_weights/pallas_call | solution.py:65
  2.1 9.9 %all-to-all-start = ((bf16[16,16,512]{2,1,0:T(8,128)(2,1)}), bf16[16,16,512]{2,1,0:T(8,128)(2,1)S(1)}, u32[]{:S(2)}, u32[]{:S(2)}) async-start(bf16[16,16,512]{2,1,0:T(8,128)(2,1)} %pack_weights.1), calls=%async_computation | async-start | bytes 524288 | tf_op jit(solution)/shard_map/all_to_all | solution.py:386
  12.0 0.2 collective-permute-start
  12.9 0.7 reshape.55
  13.7 2.2 %copy-done = bf16[256,8192]{1,0:T(8,128)(2,1)S(1)} copy-done((bf16[256,8192]{1,0:T(8,128)(2,1)S(1)}, bf16[256,8192]{1,0:T(8,128)(2,1)}, u32[]{:S(2)}) %copy-start) | copy-done | bytes 4194328
  15.9 1.6 %pick_columns.1 = (bf16[256,4096]{1,0:T(8,128)(2,1)S(1)}, bf16[256,1024]{1,0:T(8,128)(2,1)S(1)}) custom-call(s32[7]{0:T(128)S(1)} %stack.46.info_ref, bf16[256,8192]{1,0:T(8,128)(2,1)S(1)} %copy-done, bf16[256,8192]{1,0:T(8,128)(2,1)S(1)} %copy-done), custom_call_target="tpu_custom_call" | custom-call | tf_op jit(solution)/shard_map/pick_columns/pallas_call | solution.py:362
  17.5 0.8 copy-done.20
  18.3 0.9 scale_rows.1
  19.3 3.3 %all-to-all-done.refs_0_ = bf16[16,16,512]{2,1,0:T(8,128)(2,1)S(1)} async-done(((bf16[16,16,512]{2,1,0:T(8,128)(2,1)}), bf16[16,16,512]{2,1,0:T(8,128)(2,1)S(1)}, u32[]{:S(2)}, u32[]{:S(2)}) %all-to-all-start) | async-done | bytes 262176 | tf_op jit(solution)/shard_map/all_to_all | solution.py:386
  22.6 1.6 %collective-permute-start.8 = (bf16[256,1024]{1,0:T(8,128)(2,1)}, bf16[256,1024]{1,0:T(8,128)(2,1)S(1)}, u32[]{:S(2)}, u32[]{:S(2)}) collective-permute-start(bf16[256,1024]{1,0:T(8,128)(2,1)} %copy-done.20), channel_id=1, source_target_pairs={{0,1},{1,0},{2,3},{3,2},{4,5},{5,4},{6,7},{7,6},{8,9},{9,8},{10,11... | collective-permute-start | bytes 1572872 | tf_op jit(solution)/shard_map/ppermute | solution.py:443
  24.2 0.3 collective-permute-start.6
  24.4 3.0 %collective-permute-start.3 = (bf16[16,16,512]{2,1,0:T(8,128)(2,1)S(1)}, bf16[16,16,512]{2,1,0:T(8,128)(2,1)S(1)}, u32[]{:S(2)}, u32[]{:S(2)}) collective-permute-start(bf16[16,16,512]{2,1,0:T(8,128)(2,1)S(1)} %all-to-all-done.refs_0_), channel_id=1, source_target_pairs={{0,96},{32,64},{64,32},{96,0},{1,97},{33,65},{65,33},{97,1},{2,98}... | collective-permute-start | bytes 786440 | tf_op jit(solution)/shard_map/ppermute | solution.py:441
  27.5 0.1 collective-permute-start.2
  27.6 1.7 %collective-permute-start.4 = (bf16[2,64,512]{2,1,0:T(8,128)(2,1)S(1)}, bf16[2,64,512]{2,1,0:T(8,128)(2,1)}, u32[]{:S(2)}, u32[]{:S(2)}) collective-permute-start(bf16[2,64,512]{2,1,0:T(8,128)(2,1)S(1)} %pad_maximum_fusion.refs_0_), channel_id=1, source_target_pairs={{0,2},{2,4},{4,6},{6,8},{8,10},{10,12},{12,14},{14,0},{1,3},{3,5},... | collective-permute-start | bytes 393224 | tf_op jit(solution)/shard_map/ppermute | solution.py:426
  29.3 3.0 %collective-permute-start.1 = (bf16[16,16,512]{2,1,0:T(8,128)(2,1)S(1)}, bf16[16,16,512]{2,1,0:T(8,128)(2,1)}, u32[]{:S(2)}, u32[]{:S(2)}) collective-permute-start(bf16[16,16,512]{2,1,0:T(8,128)(2,1)S(1)} %all-to-all-done.refs_0_), channel_id=1, source_target_pairs={{0,64},{32,96},{64,0},{96,32},{1,65},{33,97},{65,1},{97,33},{2,66}... | collective-permute-start | bytes 786440 | tf_op jit(solution)/shard_map/ppermute | solution.py:441
  32.3 1.6 %collective-permute-done.4.refs_1_ = bf16[2,64,512]{2,1,0:T(8,128)(2,1)} collective-permute-done((bf16[2,64,512]{2,1,0:T(8,128)(2,1)S(1)}, bf16[2,64,512]{2,1,0:T(8,128)(2,1)}, u32[]{:S(2)}, u32[]{:S(2)}) %collective-permute-start.4) | collective-permute-done | bytes 131104 | tf_op jit(solution)/shard_map/ppermute | solution.py:426
  33.9 3.6 %collective-permute-start.9 = (bf16[2,64,512]{2,1,0:T(8,128)(2,1)S(1)}, bf16[2,64,512]{2,1,0:T(8,128)(2,1)}, u32[]{:S(2)}, u32[]{:S(2)}) collective-permute-start(bf16[2,64,512]{2,1,0:T(8,128)(2,1)S(1)} %pad_maximum_fusion.refs_0_), channel_id=1, source_target_pairs={{0,8},{2,10},{4,12},{6,14},{8,0},{10,2},{12,4},{14,6},{1,9},{3,11}... | collective-permute-start | bytes 393224 | tf_op jit(solution)/shard_map/ppermute | solution.py:436
  37.5 0.7 copy-done.9
  38.2 0.6 copy-done.14
  38.8 0.7 copy-done.11
  39.5 2.0 %collective-permute-start.5 = (bf16[2,64,512]{2,1,0:T(8,128)(2,1)}, bf16[2,64,512]{2,1,0:T(8,128)(2,1)}, u32[]{:S(2)}, u32[]{:S(2)}) collective-permute-start(bf16[2,64,512]{2,1,0:T(8,128)(2,1)} %collective-permute-done.4.refs_1_), channel_id=1, source_target_pairs={{0,2},{2,4},{4,6},{6,8},{8,10},{10,12},{12,14},{14,0},{1,3},{3,5},... | collective-permute-start | bytes 393224 | tf_op jit(solution)/shard_map/ppermute | solution.py:426
  41.6 0.9 copy-done.10
  42.6 0.9 copy-done.12
  43.5 2.5 %partial_products.2.refs_1_ = bf16[16,176,128]{2,1,0:T(8,128)(2,1)} custom-call(s32[3]{0:T(128)S(1)} %pad_add_fusion.heads_ref, bf16[320,512]{1,0:T(8,128)(2,1)S(1)} %get-tuple-element.37.scaled_ref, bf16[4,16,128]{2,1,0:T(8,128)(2,1)S(1)} %get-tuple-element.38.sums_ref, bf16[16,16,512]{2,1,0:T(8,128)(2,1)S(1)} %all-to-all-done.refs_0_, ...), custom_call_target="tpu_custom_call" | custom-call | tf_op jit(solution)/shard_map/partial_products/pallas_call | solution.py:143
  46.0 1.9 %partial_products.3 = bf16[16,176,128]{2,1,0:T(8,128)(2,1)} custom-call(s32[1]{0:T(128)} %bitcast.7.heads_ref, bf16[320,512]{1,0:T(8,128)(2,1)S(1)} %get-tuple-element.37.scaled_ref, bf16[4,16,128]{2,1,0:T(8,128)(2,1)S(1)} %get-tuple-element.38.sums_ref, bf16[16,16,512]{2,1,0:T(8,128)(2,1)} %collective-permute-done.1.refs_0_, ...), custom_call_target="tpu_custom_call", output_to_operand_aliasing={{}: (4, {})} | custom-call | tf_op jit(solution)/shard_map/partial_products/pallas_call | solution.py:143
  48.0 5.1 %all-to-all-start.1 = ((bf16[16,176,128]{2,1,0:T(8,128)(2,1)}), bf16[16,176,128]{2,1,0:T(8,128)(2,1)S(1)}, u32[]{:S(2)}, u32[]{:S(2)}) async-start(bf16[16,176,128]{2,1,0:T(8,128)(2,1)} %partial_products.3), calls=%async_computation.1 | async-start | bytes 1441792 | tf_op jit(solution)/shard_map/all_to_all | solution.py:386
  53.1 1.9 %collective-permute-start.12 = (bf16[256,1024]{1,0:T(8,128)(2,1)S(1)}, bf16[256,1024]{1,0:T(8,128)(2,1)}, u32[]{:S(2)}, u32[]{:S(2)}) collective-permute-start(bf16[256,1024]{1,0:T(8,128)(2,1)S(1)} %collective-permute-done.8.refs_0_), channel_id=1, source_target_pairs={{0,32},{32,0},{64,96},{96,64},{1,33},{33,1},{65,97},{97,65},{2,34}... | collective-permute-start | bytes 1572872 | tf_op jit(solution)/shard_map/ppermute | solution.py:451
  55.0 1.5 %collective-permute-start.10 = (bf16[2,64,512]{2,1,0:T(8,128)(2,1)}, bf16[2,64,512]{2,1,0:T(8,128)(2,1)S(1)}, u32[]{:S(2)}, u32[]{:S(2)}) collective-permute-start(bf16[2,64,512]{2,1,0:T(8,128)(2,1)} %collective-permute-done.5.refs_3_), channel_id=1, source_target_pairs={{0,2},{2,4},{4,6},{6,8},{8,10},{10,12},{12,14},{14,0},{1,3},{3,5},... | collective-permute-start | bytes 393224 | tf_op jit(solution)/shard_map/ppermute | solution.py:426
  56.5 1.8 %collective-permute-start.11 = (bf16[2,64,512]{2,1,0:T(8,128)(2,1)}, bf16[2,64,512]{2,1,0:T(8,128)(2,1)S(1)}, u32[]{:S(2)}, u32[]{:S(2)}) collective-permute-start(bf16[2,64,512]{2,1,0:T(8,128)(2,1)} %collective-permute-done.7.refs_4_), channel_id=1, source_target_pairs={{0,14},{2,0},{4,2},{6,4},{8,6},{10,8},{12,10},{14,12},{1,15},{3,1}... | collective-permute-start | bytes 393224 | tf_op jit(solution)/shard_map/ppermute | solution.py:429
  58.3 0.3 fusion
  58.6 11.6 %collective-permute-done.10.refs_5_ = bf16[2,64,512]{2,1,0:T(8,128)(2,1)S(1)} collective-permute-done((bf16[2,64,512]{2,1,0:T(8,128)(2,1)}, bf16[2,64,512]{2,1,0:T(8,128)(2,1)S(1)}, u32[]{:S(2)}, u32[]{:S(2)}) %collective-permute-start.10) | collective-permute-done | bytes 131104 | tf_op jit(solution)/shard_map/ppermute | solution.py:426
  70.2 0.7 copy-done.16
  70.9 0.7 copy-done.18
  71.5 1.2 finish_keys.1
  72.7 4.6 %all-to-all-start.2 = ((bf16[16,80,256]{2,1,0:T(8,128)(2,1)}), bf16[16,80,256]{2,1,0:T(8,128)(2,1)S(1)}, u32[]{:S(2)}, u32[]{:S(2)}) async-start(bf16[16,80,256]{2,1,0:T(8,128)(2,1)} %finish_keys.1), calls=%async_computation.2 | async-start | bytes 1310720 | tf_op jit(solution)/shard_map/all_to_all | solution.py:386
  77.3 0.1 collective-permute-start.13
  77.5 0.4 collective-permute-start.14
  77.8 2.2 %copy-done.1 = bf16[8192,256]{1,0:T(8,128)(2,1)S(1)} copy-done((bf16[8192,256]{1,0:T(8,128)(2,1)S(1)}, bf16[8192,256]{1,0:T(8,128)(2,1)}, u32[]{:S(2)}) %copy-start.1) | copy-done | bytes 4194328
  80.0 0.9 copy-done.7
  80.9 0.9 copy-done.15
  81.8 0.9 copy-done.17
  82.7 0.9 copy-done.19
  83.6 3.3 %queries.1.refs_0_ = bf16[64,256]{1,0:T(8,128)(2,1)S(1)} custom-call(s32[7]{0:T(128)S(1)} %stack.46.info_ref, f32[16,1,512]{2,1,0:T(1,128)S(1)} %bitcast.22, f32[144,128]{1,0:T(8,128)S(1)} %get-tuple-element.62.cos_ref, f32[144,128]{1,0:T(8,128)S(1)} %get-tuple-element.61.sin_ref, bf16[8192,256]{1,0:T(8,128)(2,1)S(1)} %copy-done.1, ...), custom_call_target="tpu_custom_call" | custom-call | tf_op jit(solution)/shard_map/queries/pallas_call | solution.py:224
  87.0 1.5 %collective-permute-start.17 = (bf16[64,256]{1,0:T(8,128)(2,1)S(1)}, bf16[64,256]{1,0:T(8,128)(2,1)S(1)}, u32[]{:S(2)}, u32[]{:S(2)}) collective-permute-start(bf16[64,256]{1,0:T(8,128)(2,1)S(1)} %queries.1.refs_0_), channel_id=1, source_target_pairs={{0,96},{32,0},{64,32},{96,64},{1,97},{33,1},{65,33},{97,65},{2,98}... | collective-permute-start | bytes 98312 | tf_op jit(solution)/shard_map/ppermute | solution.py:460
  88.4 2.2 %collective-permute-start.16 = (bf16[64,256]{1,0:T(8,128)(2,1)S(1)}, bf16[64,256]{1,0:T(8,128)(2,1)S(1)}, u32[]{:S(2)}, u32[]{:S(2)}) collective-permute-start(bf16[64,256]{1,0:T(8,128)(2,1)S(1)} %queries.1.refs_0_), channel_id=1, source_target_pairs={{0,64},{32,96},{64,0},{96,32},{1,65},{33,97},{65,1},{97,33},{2,66}... | collective-permute-start | bytes 98312 | tf_op jit(solution)/shard_map/ppermute | solution.py:460
  90.7 0.8 copy-done.2
  91.5 0.8 copy-done.4
  92.3 1.9 %collective-permute-done.16.refs_2_ = bf16[64,256]{1,0:T(8,128)(2,1)S(1)} collective-permute-done((bf16[64,256]{1,0:T(8,128)(2,1)S(1)}, bf16[64,256]{1,0:T(8,128)(2,1)S(1)}, u32[]{:S(2)}, u32[]{:S(2)}) %collective-permute-start.16) | collective-permute-done | bytes 32800 | tf_op jit(solution)/shard_map/ppermute | solution.py:460
  94.2 1.6 %collective-permute-done.15.refs_1_ = bf16[64,256]{1,0:T(8,128)(2,1)S(1)} collective-permute-done((bf16[64,256]{1,0:T(8,128)(2,1)S(1)}, bf16[64,256]{1,0:T(8,128)(2,1)S(1)}, u32[]{:S(2)}, u32[]{:S(2)}) %collective-permute-start.15) | collective-permute-done | bytes 32800 | tf_op jit(solution)/shard_map/ppermute | solution.py:460
  95.8 2.2 %attend.1 = (bf16[64,384]{1,0:T(8,128)(2,1)S(1)}, bf16[64,384]{1,0:T(8,128)(2,1)S(1)}, bf16[64,384]{1,0:T(8,128)(2,1)S(1)}, bf16[64,384]{1,0:T(8,128)(2,1)S(1)}) custom-call(s32[7]{0:T(128)S(1)} %stack.46.info_ref, bf16[4,4,80,256]{3,2,1,0:T(8,128)(2,1)S(1)} %bitcast.20, bf16[64,256]{1,0:T(8,128)(2,1)S(1)} %queries.1.refs_0_, ...), custom_call_target="tpu_custom_call" | custom-call | tf_op jit(solution)/shard_map/attend/pallas_call | solution.py:292
  98.1 1.2 collective-permute-start.19
  99.3 0.8 collective-permute-start.20
  100.1 2.1 %collective-permute-done.18.refs_1_ = bf16[64,384]{1,0:T(8,128)(2,1)S(1)} collective-permute-done((bf16[64,384]{1,0:T(8,128)(2,1)S(1)}, bf16[64,384]{1,0:T(8,128)(2,1)S(1)}, u32[]{:S(2)}, u32[]{:S(2)}) %collective-permute-start.18) | collective-permute-done | bytes 49184 | tf_op jit(solution)/shard_map/ppermute | solution.py:460
  102.2 1.7 %collective-permute-done.19.refs_2_ = bf16[64,384]{1,0:T(8,128)(2,1)S(1)} collective-permute-done((bf16[64,384]{1,0:T(8,128)(2,1)S(1)}, bf16[64,384]{1,0:T(8,128)(2,1)S(1)}, u32[]{:S(2)}, u32[]{:S(2)}) %collective-permute-start.19) | collective-permute-done | bytes 49184 | tf_op jit(solution)/shard_map/ppermute | solution.py:460
  103.9 1.0 collective-permute-done.20.refs_3_
  104.8 0.2 merge.1.own_ref
  105.0 0.4 collective-permute-start.21
  105.4 3.6 %collective-permute-done.21.other_ref = bf16[64,256]{1,0:T(8,128)(2,1)S(1)} collective-permute-done((bf16[64,256]{1,0:T(8,128)(2,1)S(1)}, bf16[64,256]{1,0:T(8,128)(2,1)S(1)}, u32[]{:S(2)}, u32[]{:S(2)}) %collective-permute-start.21) | collective-permute-done | bytes 32800 | tf_op jit(solution)/shard_map/ppermute | solution.py:466
  109.0 1.0 copy-done.3
  110.1 1.0 copy-done.5
  111.1 2.7 %project.1 = bf16[8,64,512]{2,1,0:T(8,128)(2,1)} custom-call(s32[7]{0:T(128)S(1)} %stack.46.info_ref, bf16[64,256]{1,0:T(8,128)(2,1)S(1)} %merge.1.own_ref, bf16[64,256]{1,0:T(8,128)(2,1)S(1)} %collective-permute-done.21.other_ref, bf16[256,4096]{1,0:T(8,128)(2,1)S(1)} %get-tuple-element.56.own_weight, bf16[256,1024]{1,0:T(8,128)(2,1)S(1)} %collective-permute-done.8.refs_0_, ...), custom_call_target="tpu_custom_call" | custom-call | tf_op jit(solution)/shard_map/project/pallas_call | solution.py:341
  113.8 5.4 %all-to-all-start.3 = ((bf16[8,64,512]{2,1,0:T(8,128)(2,1)}), bf16[8,64,512]{2,1,0:T(8,128)(2,1)S(1)}, u32[]{:S(2)}, u32[]{:S(2)}) async-start(bf16[8,64,512]{2,1,0:T(8,128)(2,1)} %project.1), calls=%async_computation.3 | async-start | bytes 1048576 | tf_op jit(solution)/shard_map/all_to_all | solution.py:386
  119.9 13.0 %all-to-all-done.3 = bf16[8,64,512]{2,1,0:T(8,128)(2,1)S(1)} async-done(((bf16[8,64,512]{2,1,0:T(8,128)(2,1)}), bf16[8,64,512]{2,1,0:T(8,128)(2,1)S(1)}, u32[]{:S(2)}, u32[]{:S(2)}) %all-to-all-start.3) | async-done | bytes 524320 | tf_op jit(solution)/shard_map/all_to_all | solution.py:386
  133.0 0.7 select_convert_fusion
  (50 shorter events, 0.4 us)
Async XLA Ops:
  2.1 20.5 %all-to-all-start = ((bf16[16,16,512]{2,1,0:T(8,128)(2,1)}), bf16[16,16,512]{2,1,0:T(8,128)(2,1)S(1)}, u32[]{:S(2)}, u32[]{:S(2)}) async-start(bf16[16,16,512]{2,1,0:T(8,128)(2,1)} %pack_weights.1), calls=%async_computation | async-start | bytes 524288 | tf_op jit(solution)/shard_map/all_to_all | solution.py:386
  12.0 7.3 %collective-permute-start = (bf16[64,512]{1,0:T(8,128)(2,1)}, bf16[64,512]{1,0:T(8,128)(2,1)S(1)}, u32[]{:S(2)}, u32[]{:S(2)}) collective-permute-start(bf16[64,512]{1,0:T(8,128)(2,1)} %resp_ref.1), channel_id=1, source_target_pairs={{0,1},{1,0},{2,3},{3,2},{4,5},{5,4},{6,7},{7,6},{8,9},{9,8},{10,11... | collective-permute-start | bytes 196616 | tf_op jit(solution)/shard_map/ppermute | solution.py:432
  13.7 2.2 %copy-start = (bf16[256,8192]{1,0:T(8,128)(2,1)S(1)}, bf16[256,8192]{1,0:T(8,128)(2,1)}, u32[]{:S(2)}) copy-start(bf16[256,8192]{1,0:T(8,128)(2,1)} %other_ref.1) | copy-start | bytes 12582916
  15.9 2.5 %copy-start.8 = (bf16[256,512]{1,0:T(8,128)(2,1)S(1)}, bf16[256,512]{1,0:T(8,128)(2,1)}, u32[]{:S(2)}) copy-start(bf16[256,512]{1,0:T(8,128)(2,1)} %prompt_ref.1) | copy-start | bytes 786436
  15.9 2.5 %copy-start.13 = (bf16[64,512]{1,0:T(8,128)(2,1)S(1)}, bf16[64,512]{1,0:T(8,128)(2,1)}, u32[]{:S(2)}) copy-start(bf16[64,512]{1,0:T(8,128)(2,1)} %resp_ref.1) | copy-start | bytes 196612
  17.5 0.8 copy-start.20
  19.3 28.7 %copy-start.6 = (bf16[2,64,512]{2,1,0:T(8,128)(2,1)}, bf16[2,64,512]{2,1,0:T(8,128)(2,1)S(1)}, u32[]{:S(2)}) copy-start(bf16[2,64,512]{2,1,0:T(8,128)(2,1)S(1)} %pad_maximum_fusion.refs_0_) | copy-start | bytes 393220
  22.6 25.4 %collective-permute-start.8 = (bf16[256,1024]{1,0:T(8,128)(2,1)}, bf16[256,1024]{1,0:T(8,128)(2,1)S(1)}, u32[]{:S(2)}, u32[]{:S(2)}) collective-permute-start(bf16[256,1024]{1,0:T(8,128)(2,1)} %copy-done.20), channel_id=1, source_target_pairs={{0,1},{1,0},{2,3},{3,2},{4,5},{5,4},{6,7},{7,6},{8,9},{9,8},{10,11... | collective-permute-start | bytes 1572872 | tf_op jit(solution)/shard_map/ppermute | solution.py:443
  24.2 5.2 %collective-permute-start.6 = (bf16[2,64,512]{2,1,0:T(8,128)(2,1)S(1)}, bf16[2,64,512]{2,1,0:T(8,128)(2,1)S(1)}, u32[]{:S(2)}, u32[]{:S(2)}) collective-permute-start(bf16[2,64,512]{2,1,0:T(8,128)(2,1)S(1)} %pad_maximum_fusion.refs_0_), channel_id=1, source_target_pairs={{0,14},{2,0},{4,2},{6,4},{8,6},{10,8},{12,10},{14,12},{1,15},{3,1}... | collective-permute-start | bytes 393224 | tf_op jit(solution)/shard_map/ppermute | solution.py:429
  24.4 13.0 %collective-permute-start.3 = (bf16[16,16,512]{2,1,0:T(8,128)(2,1)S(1)}, bf16[16,16,512]{2,1,0:T(8,128)(2,1)S(1)}, u32[]{:S(2)}, u32[]{:S(2)}) collective-permute-start(bf16[16,16,512]{2,1,0:T(8,128)(2,1)S(1)} %all-to-all-done.refs_0_), channel_id=1, source_target_pairs={{0,96},{32,64},{64,32},{96,0},{1,97},{33,65},{65,33},{97,1},{2,98}... | collective-permute-start | bytes 786440 | tf_op jit(solution)/shard_map/ppermute | solution.py:441
  27.5 11.4 %collective-permute-start.2 = (bf16[16,16,512]{2,1,0:T(8,128)(2,1)S(1)}, bf16[16,16,512]{2,1,0:T(8,128)(2,1)S(1)}, u32[]{:S(2)}, u32[]{:S(2)}) collective-permute-start(bf16[16,16,512]{2,1,0:T(8,128)(2,1)S(1)} %all-to-all-done.refs_0_), channel_id=1, source_target_pairs={{0,32},{32,0},{64,96},{96,64},{1,33},{33,1},{65,97},{97,65},{2,34}... | collective-permute-start | bytes 786440 | tf_op jit(solution)/shard_map/ppermute | solution.py:441
  27.6 6.3 %collective-permute-start.4 = (bf16[2,64,512]{2,1,0:T(8,128)(2,1)S(1)}, bf16[2,64,512]{2,1,0:T(8,128)(2,1)}, u32[]{:S(2)}, u32[]{:S(2)}) collective-permute-start(bf16[2,64,512]{2,1,0:T(8,128)(2,1)S(1)} %pad_maximum_fusion.refs_0_), channel_id=1, source_target_pairs={{0,2},{2,4},{4,6},{6,8},{8,10},{10,12},{12,14},{14,0},{1,3},{3,5},... | collective-permute-start | bytes 393224 | tf_op jit(solution)/shard_map/ppermute | solution.py:426
  29.3 16.7 %collective-permute-start.1 = (bf16[16,16,512]{2,1,0:T(8,128)(2,1)S(1)}, bf16[16,16,512]{2,1,0:T(8,128)(2,1)}, u32[]{:S(2)}, u32[]{:S(2)}) collective-permute-start(bf16[16,16,512]{2,1,0:T(8,128)(2,1)S(1)} %all-to-all-done.refs_0_), channel_id=1, source_target_pairs={{0,64},{32,96},{64,0},{96,32},{1,65},{33,97},{65,1},{97,33},{2,66}... | collective-permute-start | bytes 786440 | tf_op jit(solution)/shard_map/ppermute | solution.py:441
  33.9 14.1 %collective-permute-start.9 = (bf16[2,64,512]{2,1,0:T(8,128)(2,1)S(1)}, bf16[2,64,512]{2,1,0:T(8,128)(2,1)}, u32[]{:S(2)}, u32[]{:S(2)}) collective-permute-start(bf16[2,64,512]{2,1,0:T(8,128)(2,1)S(1)} %pad_maximum_fusion.refs_0_), channel_id=1, source_target_pairs={{0,8},{2,10},{4,12},{6,14},{8,0},{10,2},{12,4},{14,6},{1,9},{3,11}... | collective-permute-start | bytes 393224 | tf_op jit(solution)/shard_map/ppermute | solution.py:436
  37.5 0.7 copy-start.9
  38.2 9.8 %collective-permute-start.7 = (bf16[2,64,512]{2,1,0:T(8,128)(2,1)S(1)}, bf16[2,64,512]{2,1,0:T(8,128)(2,1)}, u32[]{:S(2)}, u32[]{:S(2)}) collective-permute-start(bf16[2,64,512]{2,1,0:T(8,128)(2,1)S(1)} %collective-permute-done.6.refs_2_), channel_id=1, source_target_pairs={{0,14},{2,0},{4,2},{6,4},{8,6},{10,8},{12,10},{14,12},{1,15},{3,1}... | collective-permute-start | bytes 393224 | tf_op jit(solution)/shard_map/ppermute | solution.py:429
  38.2 0.7 copy-start.14
  38.8 0.7 copy-start.11
  39.5 8.4 %collective-permute-start.5 = (bf16[2,64,512]{2,1,0:T(8,128)(2,1)}, bf16[2,64,512]{2,1,0:T(8,128)(2,1)}, u32[]{:S(2)}, u32[]{:S(2)}) collective-permute-start(bf16[2,64,512]{2,1,0:T(8,128)(2,1)} %collective-permute-done.4.refs_1_), channel_id=1, source_target_pairs={{0,2},{2,4},{4,6},{6,8},{8,10},{10,12},{12,14},{14,0},{1,3},{3,5},... | collective-permute-start | bytes 393224 | tf_op jit(solution)/shard_map/ppermute | solution.py:426
  41.6 1.0 copy-start.10
  42.6 0.9 copy-start.12
  48.0 23.6 %all-to-all-start.1 = ((bf16[16,176,128]{2,1,0:T(8,128)(2,1)}), bf16[16,176,128]{2,1,0:T(8,128)(2,1)S(1)}, u32[]{:S(2)}, u32[]{:S(2)}) async-start(bf16[16,176,128]{2,1,0:T(8,128)(2,1)} %partial_products.3), calls=%async_computation.1 | async-start | bytes 1441792 | tf_op jit(solution)/shard_map/all_to_all | solution.py:386
  53.1 18.5 %collective-permute-start.12 = (bf16[256,1024]{1,0:T(8,128)(2,1)S(1)}, bf16[256,1024]{1,0:T(8,128)(2,1)}, u32[]{:S(2)}, u32[]{:S(2)}) collective-permute-start(bf16[256,1024]{1,0:T(8,128)(2,1)S(1)} %collective-permute-done.8.refs_0_), channel_id=1, source_target_pairs={{0,32},{32,0},{64,96},{96,64},{1,33},{33,1},{65,97},{97,65},{2,34}... | collective-permute-start | bytes 1572872 | tf_op jit(solution)/shard_map/ppermute | solution.py:451
  55.0 15.3 %collective-permute-start.10 = (bf16[2,64,512]{2,1,0:T(8,128)(2,1)}, bf16[2,64,512]{2,1,0:T(8,128)(2,1)S(1)}, u32[]{:S(2)}, u32[]{:S(2)}) collective-permute-start(bf16[2,64,512]{2,1,0:T(8,128)(2,1)} %collective-permute-done.5.refs_3_), channel_id=1, source_target_pairs={{0,2},{2,4},{4,6},{6,8},{8,10},{10,12},{12,14},{14,0},{1,3},{3,5},... | collective-permute-start | bytes 393224 | tf_op jit(solution)/shard_map/ppermute | solution.py:426
  56.5 14.4 %collective-permute-start.11 = (bf16[2,64,512]{2,1,0:T(8,128)(2,1)}, bf16[2,64,512]{2,1,0:T(8,128)(2,1)S(1)}, u32[]{:S(2)}, u32[]{:S(2)}) collective-permute-start(bf16[2,64,512]{2,1,0:T(8,128)(2,1)} %collective-permute-done.7.refs_4_), channel_id=1, source_target_pairs={{0,14},{2,0},{4,2},{6,4},{8,6},{10,8},{12,10},{14,12},{1,15},{3,1}... | collective-permute-start | bytes 393224 | tf_op jit(solution)/shard_map/ppermute | solution.py:429
  70.2 0.7 copy-start.16
  70.9 0.7 copy-start.18
  72.7 19.5 %all-to-all-start.2 = ((bf16[16,80,256]{2,1,0:T(8,128)(2,1)}), bf16[16,80,256]{2,1,0:T(8,128)(2,1)S(1)}, u32[]{:S(2)}, u32[]{:S(2)}) async-start(bf16[16,80,256]{2,1,0:T(8,128)(2,1)} %finish_keys.1), calls=%async_computation.2 | async-start | bytes 1310720 | tf_op jit(solution)/shard_map/all_to_all | solution.py:386
  77.3 13.3 %collective-permute-start.13 = (bf16[256,1024]{1,0:T(8,128)(2,1)S(1)}, bf16[256,1024]{1,0:T(8,128)(2,1)S(1)}, u32[]{:S(2)}, u32[]{:S(2)}) collective-permute-start(bf16[256,1024]{1,0:T(8,128)(2,1)S(1)} %collective-permute-done.8.refs_0_), channel_id=1, source_target_pairs={{0,16},{16,0},{1,17},{17,1},{2,18},{18,2},{3,19},{19,3},{4,20},{20... | collective-permute-start | bytes 1572872 | tf_op jit(solution)/shard_map/ppermute | solution.py:455
  77.5 14.0 %collective-permute-start.14 = (bf16[256,1024]{1,0:T(8,128)(2,1)}, bf16[256,1024]{1,0:T(8,128)(2,1)S(1)}, u32[]{:S(2)}, u32[]{:S(2)}) collective-permute-start(bf16[256,1024]{1,0:T(8,128)(2,1)} %collective-permute-done.12.refs_1_), channel_id=1, source_target_pairs={{0,16},{16,0},{1,17},{17,1},{2,18},{18,2},{3,19},{19,3},{4,20},{20... | collective-permute-start | bytes 1572872 | tf_op jit(solution)/shard_map/ppermute | solution.py:455
  77.8 2.2 %copy-start.1 = (bf16[8192,256]{1,0:T(8,128)(2,1)S(1)}, bf16[8192,256]{1,0:T(8,128)(2,1)}, u32[]{:S(2)}) copy-start(bf16[8192,256]{1,0:T(8,128)(2,1)} %weight_ref.1) | copy-start | bytes 12582916
  80.0 0.9 copy-start.7
  80.9 0.9 copy-start.15
  81.8 0.9 copy-start.17
  82.7 0.9 copy-start.19
  87.0 5.3 %collective-permute-start.17 = (bf16[64,256]{1,0:T(8,128)(2,1)S(1)}, bf16[64,256]{1,0:T(8,128)(2,1)S(1)}, u32[]{:S(2)}, u32[]{:S(2)}) collective-permute-start(bf16[64,256]{1,0:T(8,128)(2,1)S(1)} %queries.1.refs_0_), channel_id=1, source_target_pairs={{0,96},{32,0},{64,32},{96,64},{1,97},{33,1},{65,33},{97,65},{2,98}... | collective-permute-start | bytes 98312 | tf_op jit(solution)/shard_map/ppermute | solution.py:460
  88.4 5.8 %collective-permute-start.16 = (bf16[64,256]{1,0:T(8,128)(2,1)S(1)}, bf16[64,256]{1,0:T(8,128)(2,1)S(1)}, u32[]{:S(2)}, u32[]{:S(2)}) collective-permute-start(bf16[64,256]{1,0:T(8,128)(2,1)S(1)} %queries.1.refs_0_), channel_id=1, source_target_pairs={{0,64},{32,96},{64,0},{96,32},{1,65},{33,97},{65,1},{97,33},{2,66}... | collective-permute-start | bytes 98312 | tf_op jit(solution)/shard_map/ppermute | solution.py:460
  90.7 5.1 %collective-permute-start.15 = (bf16[64,256]{1,0:T(8,128)(2,1)S(1)}, bf16[64,256]{1,0:T(8,128)(2,1)S(1)}, u32[]{:S(2)}, u32[]{:S(2)}) collective-permute-start(bf16[64,256]{1,0:T(8,128)(2,1)S(1)} %queries.1.refs_0_), channel_id=1, source_target_pairs={{0,32},{32,64},{64,96},{96,0},{1,33},{33,65},{65,97},{97,1},{2,34}... | collective-permute-start | bytes 98312 | tf_op jit(solution)/shard_map/ppermute | solution.py:460
  90.7 0.8 copy-start.2
  91.5 0.8 copy-start.4
  98.0 4.2 %collective-permute-start.18 = (bf16[64,384]{1,0:T(8,128)(2,1)S(1)}, bf16[64,384]{1,0:T(8,128)(2,1)S(1)}, u32[]{:S(2)}, u32[]{:S(2)}) collective-permute-start(bf16[64,384]{1,0:T(8,128)(2,1)S(1)} %get-tuple-element.53), channel_id=1, source_target_pairs={{0,96},{32,0},{64,32},{96,64},{1,97},{33,1},{65,33},{97,65},{2,98}... | collective-permute-start | bytes 147464 | tf_op jit(solution)/shard_map/ppermute | solution.py:460
  98.1 5.8 %collective-permute-start.19 = (bf16[64,384]{1,0:T(8,128)(2,1)S(1)}, bf16[64,384]{1,0:T(8,128)(2,1)S(1)}, u32[]{:S(2)}, u32[]{:S(2)}) collective-permute-start(bf16[64,384]{1,0:T(8,128)(2,1)S(1)} %get-tuple-element.54), channel_id=1, source_target_pairs={{0,64},{32,96},{64,0},{96,32},{1,65},{33,97},{65,1},{97,33},{2,66}... | collective-permute-start | bytes 147464 | tf_op jit(solution)/shard_map/ppermute | solution.py:460
  99.3 5.6 %collective-permute-start.20 = (bf16[64,384]{1,0:T(8,128)(2,1)S(1)}, bf16[64,384]{1,0:T(8,128)(2,1)S(1)}, u32[]{:S(2)}, u32[]{:S(2)}) collective-permute-start(bf16[64,384]{1,0:T(8,128)(2,1)S(1)} %get-tuple-element.55), channel_id=1, source_target_pairs={{0,32},{32,64},{64,96},{96,0},{1,33},{33,65},{65,97},{97,1},{2,34}... | collective-permute-start | bytes 147464 | tf_op jit(solution)/shard_map/ppermute | solution.py:460
  105.0 4.0 %collective-permute-start.21 = (bf16[64,256]{1,0:T(8,128)(2,1)S(1)}, bf16[64,256]{1,0:T(8,128)(2,1)S(1)}, u32[]{:S(2)}, u32[]{:S(2)}) collective-permute-start(bf16[64,256]{1,0:T(8,128)(2,1)S(1)} %merge.1.own_ref), channel_id=1, source_target_pairs={{0,1},{1,0},{2,3},{3,2},{4,5},{5,4},{6,7},{7,6},{8,9},{9,8},{10,11... | collective-permute-start | bytes 98312 | tf_op jit(solution)/shard_map/ppermute | solution.py:466
  109.0 1.0 copy-start.3
  110.1 1.0 copy-start.5
  113.8 19.1 %all-to-all-start.3 = ((bf16[8,64,512]{2,1,0:T(8,128)(2,1)}), bf16[8,64,512]{2,1,0:T(8,128)(2,1)S(1)}, u32[]{:S(2)}, u32[]{:S(2)}) async-start(bf16[8,64,512]{2,1,0:T(8,128)(2,1)} %project.1), calls=%async_computation.3 | async-start | bytes 1048576 | tf_op jit(solution)/shard_map/all_to_all | solution.py:386

commit v3 on v2

v3 whole, which is shorter than its diff:
```python
import functools
import math

import jax
import jax.numpy as jnp
from jax import lax
from jax.experimental import pallas as pl
from jax.experimental.pallas import tpu as pltpu
from jax.sharding import Mesh
from jax.sharding import PartitionSpec as P

PARTS = (("xh", 2), ("y", 4), ("core", 2), ("k", 4), ("zl", 2), ("xl", 2))
SAMPLE = ("xh", "y", "core")
TENSOR = ("k", "zl", "xl")
ZRING = ("k", "zl")
KEY_GROUP = ("xh", "core", "zl", "xl")

D = 8192
BLOCK = 512
HEAD_DIM = 128
HALF = 64
RESP = 64
PROMPT_ROWS = 256
ROWS = 160
SENT_ROWS = ROWS + 16
PACKED = 64 + RESP
EPSILON = 1e-05
ROPE_BASE = 500000.0
NEG_BIG = -1e30
CORE_AT, XL_AT, T_AT, Y_AT, PLACE_AT, LENGTH_AT = 0, 1, 2, 3, 4, 5
F32 = jnp.float32
BF16 = jnp.bfloat16
SMALL = 12 * 1024 * 1024


def iota(shape, dim):
    return lax.broadcasted_iota(jnp.int32, shape, dim)


def dot_t(a, b):
    return lax.dot_general(a, b, (((1,), (1,)), ((), ())), preferred_element_type=F32)


def dot(a, b):
    return lax.dot_general(a, b, (((1,), (0,)), ((), ())), preferred_element_type=F32)


LONG = pl.CostEstimate(flops=30_000_000_000, bytes_accessed=1_000_000, transcendentals=0)


def params(limit=None):
    return pltpu.CompilerParams(vmem_limit_bytes=limit)


def pack_kernel(core_ref, key_ref, value_ref, hidden_ref, out_ref):
    row, col = iota((32, 64), 0), iota((32, 64), 1)
    source = ((row >> 3) & 1) * 32 + (row & 7) * 4 + 2 * core_ref[0] + (row >> 4)
    pick = jnp.where(col == source, 1.0, 0.0).astype(BF16)
    both = jnp.concatenate([key_ref[...], value_ref[...]], axis=0)
    for i in range(out_ref.shape[0]):
        for x in range(2):
            at = (2 * i + x) * BLOCK
            rows = dot(pick, both[:, at : at + BLOCK]).astype(BF16)
            for head in range(2):
                out_ref[i, (2 * head + x) * 16 : (2 * head + x) * 16 + 16] = rows[head * 16 : head * 16 + 16]
        out_ref[i, 64:] = hidden_ref[...]


def pack(core, key_rows, value_rows, hidden):
    steps = 2
    each = 8 // steps
    return pl.pallas_call(
        pack_kernel,
        grid=(steps,),
        in_specs=[
            pl.BlockSpec(memory_space=pltpu.SMEM),
            pl.BlockSpec((32, 2 * each * BLOCK), lambda i: (0, i)),
            pl.BlockSpec((32, 2 * each * BLOCK), lambda i: (0, i)),
            pl.BlockSpec((RESP, BLOCK), lambda i: (0, 0)),
        ],
        out_specs=pl.BlockSpec((each, PACKED, BLOCK), lambda i: (i, 0, 0)),
        out_shape=jax.ShapeDtypeStruct((8, PACKED, BLOCK), BF16),
        compiler_params=params(),
        name="pack",
    )(core, key_rows, value_rows, hidden)


def scale_kernel(info_ref, prompt_ref, resp_ref, gain_ref, out_ref, high, low):
    gain = gain_ref[info_ref[T_AT]]

    def put(at, count, values):
        values = values.astype(F32)
        out_ref[at : at + count] = (values * gain).astype(BF16)
        square = values * values
        top = square.astype(BF16)
        high[at : at + count] = top
        low[at : at + count] = (square - top.astype(F32)).astype(BF16)

    for half in range(2):
        put(ROWS * half, 128, prompt_ref[128 * half : 128 * half + 128])
        put(ROWS * half + 128, 32, resp_ref[32 * half : 32 * half + 32])
    high[320:448] = jnp.zeros((128, BLOCK), BF16)
    low[320:448] = jnp.zeros((128, BLOCK), BF16)
    ones = jnp.ones((16, BLOCK), BF16)
    row = iota((16, 128), 0)
    rows = jnp.zeros((16, 128), F32)
    for n, at in enumerate((0, 128, ROWS, ROWS + 128)):
        total = dot_t(ones, high[at : at + 128]) + dot_t(ones, low[at : at + 128])
        top = total.astype(BF16).astype(F32)
        rows = jnp.where(row == 2 * n, top, jnp.where(row == 2 * n + 1, total - top, rows))
    out_ref[320:, :128] = rows.astype(BF16)
    out_ref[320:, 128:] = jnp.zeros((16, BLOCK - 128), BF16)


def scale_rows(info, prompt, resp, gain):
    vmem = pl.BlockSpec(memory_space=pltpu.VMEM)
    return pl.pallas_call(
        scale_kernel,
        in_specs=[pl.BlockSpec(memory_space=pltpu.SMEM), vmem, vmem, vmem],
        out_shape=jax.ShapeDtypeStruct((2 * ROWS + 16, BLOCK), BF16),
        scratch_shapes=[pltpu.VMEM((448, BLOCK), BF16), pltpu.VMEM((448, BLOCK), BF16)],
        compiler_params=params(SMALL),
        name="scale_rows",
    )(info, prompt, resp, gain)


def partial_kernel(scalars_ref, weight_ref, own_ref, other_ref, *refs):
    out_ref = refs[-1]
    is_first = scalars_ref[1] == 0
    own, other = own_ref[: 2 * ROWS], other_ref[: 2 * ROWS]
    rows = (jnp.where(is_first, own, other), jnp.where(is_first, other, own))
    total = jnp.zeros((2 * ROWS, 256), F32)
    for x in range(2):
        weights = [weight_ref[:, (2 * head + x) * 16 : (2 * head + x) * 16 + 16] for head in range(2)]
        weights = [piece.reshape(128, BLOCK) for piece in weights]
        total += dot_t(rows[x], jnp.concatenate(weights, axis=0))
    total = total.astype(BF16)
    own_sums, other_sums = own_ref[2 * ROWS :, :128], other_ref[2 * ROWS :, :128]
    for head in range(2):
        for half in range(2):
            to = 2 * head + half
            out_ref[to, :ROWS] = total[ROWS * half : ROWS * half + ROWS, head * 128 : head * 128 + 128]
            sums = jnp.concatenate(
                [own_sums[4 * half : 4 * half + 4], other_sums[4 * half : 4 * half + 4], jnp.zeros((8, 128), BF16)],
                axis=0,
            )
            out_ref[to, ROWS:] = sums


def split_kernel(got_ref, *refs):
    weights_ref, hidden_ref = refs[-2:]
    weights_ref[...] = got_ref[:, :64]
    hidden_ref[...] = got_ref[:, 64:]


def split(got, after):
    return pl.pallas_call(
        split_kernel,
        in_specs=[pl.BlockSpec(memory_space=pltpu.VMEM)] * (1 + len(after)),
        out_shape=(jax.ShapeDtypeStruct((8, 64, BLOCK), BF16), jax.ShapeDtypeStruct((8, RESP, BLOCK), BF16)),
        compiler_params=params(SMALL),
        name="split",
    )(got, *after)


def partial_products(scalars, weights, own, other, before=None, after=None):
    def whole(shape):
        return pl.BlockSpec(shape, lambda i, scalars: (0,) * len(shape))

    rows = (2 * ROWS + 16, BLOCK)
    in_specs = [whole((8, 64, BLOCK)), whole(rows), whole(rows)]
    operands = [scalars, weights, own, other]
    aliases = {}
    if before is not None:
        in_specs.append(pl.BlockSpec(memory_space=pl.ANY))
        operands.append(before)
        aliases = {len(operands) - 1: 0}
    if after is not None:
        in_specs.append(pl.BlockSpec((16, 128), lambda i, scalars: (0, 0)))
        operands.append(after)
    return pl.pallas_call(
        partial_kernel,
        grid_spec=pltpu.PrefetchScalarGridSpec(
            num_scalar_prefetch=1,
            grid=(1,),
            in_specs=in_specs,
            out_specs=pl.BlockSpec((4, SENT_ROWS, 128), lambda i, scalars: (scalars[0], 0, 0)),
        ),
        out_shape=jax.ShapeDtypeStruct((8, SENT_ROWS, 128), BF16),
        input_output_aliases=aliases,
        compiler_params=params(SMALL),
        name="partial_products",
    )(*operands)


def turn(values, cosine, sine):
    return values * cosine + pltpu.roll(values, HALF, 1) * sine


def finish_kernel(parts_ref, trig_ref, *refs):
    out_ref = refs[-1]
    total = jnp.sum(parts_ref[...].astype(F32), axis=0)
    sums = total[ROWS:]
    column = []
    for n, count in enumerate((128, ROWS - 128)):
        line = sums[2 * n : 2 * n + 1] + sums[2 * n + 1 : 2 * n + 2] + sums[2 * n + 4 : 2 * n + 5]
        line += sums[2 * n + 5 : 2 * n + 6]
        diagonal = iota((count, 128), 0) == iota((count, 128), 1)
        spread = jnp.where(diagonal, jnp.broadcast_to(line, (count, 128)), 0.0)
        column.append(jnp.sum(spread, axis=1, keepdims=True))
    factor = lax.rsqrt(jnp.concatenate(column, axis=0) * (1.0 / D) + EPSILON)
    raw = (total[:ROWS] * factor).astype(BF16)
    row, col = iota((128, 128), 0), iota((128, 128), 1)
    target = ((row >> 3) & 1) * 64 + (row >> 4) * 8 + (row & 7)
    ordered = dot(raw, jnp.where(col == target, 1.0, 0.0).astype(BF16))
    beside = dot(raw, jnp.where(col == (target ^ 32), 1.0, 0.0).astype(BF16))
    result = (ordered * trig_ref[0, :ROWS] + beside * trig_ref[1, :ROWS]).astype(BF16)
    for i in range(out_ref.shape[0]):
        out_ref[i] = result


def finish_keys(parts, trig, *after):
    return pl.pallas_call(
        finish_kernel,
        in_specs=[pl.BlockSpec(memory_space=pltpu.VMEM)] * (2 + len(after)),
        out_shape=jax.ShapeDtypeStruct((16, ROWS, 128), BF16),
        compiler_params=params(SMALL),
        cost_estimate=LONG,
        name="finish_keys",
    )(parts, trig, *after)


def by_xl(natural):
    return ((natural >> 3) & 1) * 64 + (natural >> 4) * 8 + (natural & 7)


def query_kernel(info_ref, gain_ref, trig_ref, weight_ref, own_ref, other_ref, out_ref):
    xl = info_ref[XL_AT]
    total = jnp.zeros((RESP, 256), F32)
    squares = jnp.zeros((RESP, 1), F32)
    for z in range(8):
        for j, ref in enumerate((own_ref, other_ref)):
            x = j ^ xl
            hidden = ref[z].astype(F32)
            scaled = (hidden * gain_ref[2 * z + x]).astype(BF16)
            total += dot(scaled, weight_ref[pl.ds(pl.multiple_of((2 * z + x) * BLOCK, BLOCK), BLOCK)])
            squares += jnp.sum(hidden * hidden, axis=1, keepdims=True)
    factor = lax.rsqrt(squares * (1.0 / D) + EPSILON)
    row, col = iota((128, 128), 0), iota((128, 128), 1)
    order = jnp.where(col == by_xl(row), 1.0, 0.0).astype(BF16)
    for h in range(2):
        part = slice(h * HEAD_DIM, (h + 1) * HEAD_DIM)
        query = turn(total[:, part] * factor, trig_ref[0, ROWS:], trig_ref[1, ROWS:])
        out_ref[:, part] = dot(query.astype(BF16), order).astype(BF16)


def queries_of(info, gain, weight, trig, own, other):
    vmem = pl.BlockSpec(memory_space=pltpu.VMEM)
    return pl.pallas_call(
        query_kernel,
        in_specs=[pl.BlockSpec(memory_space=pltpu.SMEM)] + [vmem] * 5,
        out_shape=jax.ShapeDtypeStruct((RESP, 256), BF16),
        compiler_params=params(SMALL),
        cost_estimate=LONG,
        name="queries",
    )(info, gain, trig, weight, own, other)


def attend_kernel(info_ref, rows_ref, *refs):
    queries, outs = refs[:4], refs[4:]
    own_y = info_ref[Y_AT]

    def joined(block, at, count):
        first, second = rows_ref[block, pl.ds(at, count)], rows_ref[block + 1, pl.ds(at, count)]
        keys = jnp.concatenate([first[:, :HALF], second[:, :HALF]], axis=1)
        return keys, jnp.concatenate([first[:, HALF:], second[:, HALF:]], axis=1)

    prompt = [joined(2 * i, 0, 128) for i in range(8)]
    prompt_keys, prompt_values = (jnp.concatenate([p[n] for p in prompt], axis=0) for n in range(2))
    place = info_ref[PLACE_AT] * 4
    own = [joined(place + 2 * half, 128, 32) for half in range(2)]
    own_keys, own_values = (jnp.concatenate([o[n] for o in own], axis=0) for n in range(2))
    scale = HEAD_DIM ** (-0.5)
    power = scale * math.log2(math.e)

    column = iota((1, 1024), 1)
    sample = (column >> 9) * 8 + own_y * 2 + ((column >> 8) & 1)
    live = sample * PROMPT_ROWS + (column & 255) < info_ref[LENGTH_AT]
    causal = iota((2 * RESP, RESP), 1) <= (iota((2 * RESP, RESP), 0) & (RESP - 1))
    lane = iota((RESP, 128), 1)

    for i in range(4):
        query = jnp.concatenate([queries[i][:, :HEAD_DIM], queries[i][:, HEAD_DIM:]], axis=0)
        far = jnp.where(live, dot_t(query, prompt_keys), NEG_BIG)
        top = jnp.max(far, axis=1, keepdims=True)
        if i == 0:
            near = jnp.where(causal, dot_t(query, own_keys), NEG_BIG)
            top = jnp.maximum(top, jnp.max(near, axis=1, keepdims=True))
        top = jnp.maximum(top, 0.5 * NEG_BIG)
        far = jnp.exp2((far - top) * power)
        total = jnp.sum(far, axis=1, keepdims=True)
        summed = dot(far.astype(BF16), prompt_values)
        if i == 0:
            near = jnp.exp2((near - top) * power)
            total += jnp.sum(near, axis=1, keepdims=True)
            summed += dot(near.astype(BF16), own_values)
        some = total > 0.0
        safe = jnp.where(some, total, 1.0)
        result = (summed / safe).astype(BF16)
        level = jnp.where(some, top * scale + jnp.log(safe), NEG_BIG)
        first = level.astype(BF16).astype(F32)
        rest = level - first
        second = rest.astype(BF16).astype(F32)
        third = rest - second
        extra = jnp.zeros((RESP, 128), F32)
        for h in range(2):
            mine = slice(h * RESP, (h + 1) * RESP)
            outs[i][:, h * HEAD_DIM : (h + 1) * HEAD_DIM] = result[mine]
            for n, piece in enumerate((first, second, third)):
                extra = jnp.where(lane == 3 * h + n, piece[mine], extra)
        outs[i][:, 256:] = extra.astype(BF16)


def attend(info, rows, queries):
    vmem = pl.BlockSpec(memory_space=pltpu.VMEM)
    return pl.pallas_call(
        attend_kernel,
        in_specs=[pl.BlockSpec(memory_space=pltpu.SMEM)] + [vmem] * 5,
        out_shape=(jax.ShapeDtypeStruct((RESP, 384), BF16),) * 4,
        compiler_params=params(SMALL),
        name="attend",
    )(info, rows, *queries)


def merge_kernel(*refs):
    parts, out_ref = refs[:4], refs[4]
    lane = iota((RESP, 128), 1)
    row, col = iota((128, 128), 0), iota((128, 128), 1)
    order = jnp.where(row == by_xl(col), 1.0, 0.0).astype(BF16)
    extras = [part[:, 256:].astype(F32) for part in parts]
    for h in range(2):
        head = slice(h * HEAD_DIM, (h + 1) * HEAD_DIM)
        mine = jnp.logical_and(lane >= 3 * h, lane < 3 * h + 3)
        levels = [jnp.sum(jnp.where(mine, e, 0.0), axis=1, keepdims=True) for e in extras]
        top = functools.reduce(jnp.maximum, levels)
        shares = [jnp.exp(level - top) for level in levels]
        total = functools.reduce(jnp.add, shares)
        pieces = [share * part[:, head].astype(F32) for share, part in zip(shares, parts)]
        mean = (functools.reduce(jnp.add, pieces) / total).astype(BF16)
        out_ref[:, head] = dot(mean, order).astype(BF16)


def merge(parts):
    vmem = pl.BlockSpec(memory_space=pltpu.VMEM)
    return pl.pallas_call(
        merge_kernel,
        in_specs=[vmem] * 4,
        out_shape=jax.ShapeDtypeStruct((RESP, 256), BF16),
        compiler_params=params(SMALL),
        name="merge",
    )(*parts)


def z_of(i, info):
    return (4 * info[CORE_AT] + 2 * (info[Y_AT] % 2)) ^ i


def project_own_kernel(own_ref, *refs):
    weights, out_ref = refs[:4], refs[4]
    for i in range(8):
        out_ref[i] = dot(own_ref[...], weights[i // 2][:, pl.ds((i % 2) * BLOCK, BLOCK)])


def project_own(own, weights):
    vmem = pl.BlockSpec(memory_space=pltpu.VMEM)
    return pl.pallas_call(
        project_own_kernel,
        in_specs=[vmem] * 5,
        out_shape=jax.ShapeDtypeStruct((8, RESP, BLOCK), F32),
        compiler_params=params(SMALL),
        cost_estimate=LONG,
        name="project_own",
    )(own, *weights)


def project_kernel(info_ref, started_ref, other_ref, *refs):
    cross, out_ref = refs[:4], refs[4]
    for i in range(8):
        result = started_ref[i] + dot(other_ref[...], cross[i // 2][:, pl.ds((i % 2) * BLOCK, BLOCK)])
        out_ref[z_of(i, info_ref)] = result.astype(BF16)


def project(info, started, other, cross):
    vmem = pl.BlockSpec(memory_space=pltpu.VMEM)
    return pl.pallas_call(
        project_kernel,
        in_specs=[pl.BlockSpec(memory_space=pltpu.SMEM)] + [vmem] * 6,
        out_shape=jax.ShapeDtypeStruct((8, RESP, BLOCK), BF16),
        compiler_params=params(SMALL),
        name="project",
    )(info, started, other, *cross)


def pick_kernel(info_ref, weight_ref, *refs):
    own_refs, sent_ref = refs[:4], refs[4]

    def columns(i, x):
        at = (2 * z_of(i, info_ref) + x) * BLOCK
        return weight_ref[:, pl.ds(pl.multiple_of(at, BLOCK), BLOCK)]

    xl = info_ref[XL_AT]
    for i in range(8):
        own_refs[i // 2][:, (i % 2) * BLOCK : (i % 2) * BLOCK + BLOCK] = columns(i, xl)
    for i in range(2):
        sent_ref[:, i * BLOCK : (i + 1) * BLOCK] = columns(i, 1 - xl)


def pick_columns(info, weight):
    return pl.pallas_call(
        pick_kernel,
        in_specs=[pl.BlockSpec(memory_space=pltpu.SMEM), pl.BlockSpec(memory_space=pltpu.VMEM)],
        out_shape=(jax.ShapeDtypeStruct((256, 2 * BLOCK), BF16),) * 5,
        compiler_params=params(SMALL),
        name="pick_columns",
    )(info, weight)


def swap(values, axis):
    return lax.all_to_all(values, axis, 0, 0, tiled=False)


def body(
    response_hidden,
    prompt_hidden,
    norm_gain,
    query_weight,
    key_weight,
    value_weight,
    output_weight,
    response_lengths,
    prompt_length,
):
    length = prompt_length[0]
    core, y = lax.axis_index("core"), lax.axis_index("y")
    sample, half, xl = lax.axis_index(SAMPLE), lax.axis_index("zl"), lax.axis_index("xl")
    gain = norm_gain.astype(F32).reshape(16, 1, BLOCK)

    row = jnp.arange(ROWS + RESP, dtype=jnp.int32)[:, None]
    positions = jnp.where(
        row < 128,
        sample * PROMPT_ROWS + half * 128 + row,
        jnp.where(row < ROWS, length + half * 32 + row - 128, length + row - ROWS),
    )
    lane = jnp.arange(HEAD_DIM, dtype=jnp.int32)[None, :]
    entry = ((lane >> 3) * 2 + xl) * 8 + (lane & 7)
    entry = jnp.where(row < ROWS, entry, lane)
    still = (row < ROWS) & (lane >= HALF)
    inverse = ROPE_BASE ** (-((entry % HALF).astype(F32) * 2.0 / HEAD_DIM))
    angles = jnp.where(still, 0.0, positions.astype(F32) * inverse)
    trig = jnp.stack([jnp.cos(angles), jnp.sin(angles) * jnp.where(entry < HALF, -1.0, 1.0)])

    info = jnp.stack(
        [core, xl, lax.axis_index(TENSOR), y, lax.axis_index(("xh", "core")), length]
    ).astype(jnp.int32)
    flip = [(0, 1), (1, 0)]

    packed = pack(core.reshape(1), key_weight.T, value_weight.T, response_hidden)
    got = swap(packed, ZRING)
    scaled = scale_rows(info, prompt_hidden, response_hidden, gain)
    beside = lax.ppermute(scaled, "xl", flip)
    *own, sent = pick_columns(info, output_weight)
    first = lax.ppermute(sent, "xl", flip)
    weights, own_hidden = split(got, (beside, sent))
    other_weights = lax.ppermute(weights, "core", flip)
    products = partial_products(jnp.stack([core, xl]), weights, scaled, beside)
    products = partial_products(jnp.stack([1 - core, xl]), other_weights, scaled, beside, products, first)
    products = swap(products, ZRING)
    other_hidden = lax.ppermute(own_hidden, "xl", flip)
    second = lax.ppermute(first, "y", [(i, i ^ 1) for i in range(4)])
    queries = queries_of(info, gain, query_weight, trig, own_hidden, other_hidden)
    cross = (first, second, lax.ppermute(first, "core", flip), lax.ppermute(second, "core", flip))
    rows = finish_keys(products, trig, queries, second)
    rows = swap(rows, KEY_GROUP)

    def along(values, step):
        return lax.ppermute(values, "y", [(i, (i + step) % 4) for i in range(4)])

    pooled = [queries] + [along(queries, step) for step in (1, 2, 3)]
    parts = attend(info, rows, pooled)
    attention = merge([parts[0]] + [along(parts[step], -step) for step in (1, 2, 3)])
    partner = lax.ppermute(attention, "xl", flip)
    partial = project(info, project_own(attention, own), partner, cross)
    summed = jnp.sum(swap(partial, ZRING).astype(F32), axis=0)
    live = jnp.arange(RESP, dtype=jnp.int32) < response_lengths[0]
    return jnp.where(live[:, None], summed, 0.0).astype(BF16)


def solution(mesh):
    names = tuple(name for name, _ in PARTS)
    sizes = tuple(size for _, size in PARTS)
    fine = Mesh(mesh.devices.reshape(sizes), names)
    return jax.shard_map(
        body,
        mesh=fine,
        in_specs=(
            P(SAMPLE, TENSOR),
            P(SAMPLE, TENSOR),
            P(),
            P(None, TENSOR),
            P(None, TENSOR),
            P(None, TENSOR),
            P(TENSOR, None),
            P(SAMPLE),
            P(),
        ),
        out_specs=P(SAMPLE, TENSOR),
        check_vma=False,
    )
```

time: 135 us -> 119 us (0.88)
  starting transfers between devices: 52.4 us -> 37.1 us
  waiting for transfers between devices: 41.4 us -> 52.5 us
  local copies, waits for them, and re-layouts: 17.8 us -> 8.94 us
  Pallas kernels: 18.7 us -> 16.5 us
    all_to_all x4, waiting for transfers between devices: 16.3 us -> 38.4 us  [swap(): return lax.all_to_all(values, axis, 0, 0, tiled=False)]
    ppermute x12 -> x4, starting transfers between devices: 17.6 us -> 2.63 us  [the longest x1 1.53 us: body(): partner = lax.ppermute(attention, 'xl', flip)]
    unnamed x42 -> x22, local copies, waits for them, and re-layouts: 17.7 us -> 8.85 us
    ppermute x12 -> x4, waiting for transfers between devices: 16.8 us -> 8.61 us  [the longest x1 5.11 us: body(): other_hidden = lax.ppermute(own_hidden, 'xl', flip)]
    ppermute x6, starting transfers between devices: 5.79 us -> 9.92 us  [along(): return lax.ppermute(values, 'y', [(i, (i + step) % 4) for i in range(4)])]
    all_to_all x4, starting transfers between devices: 25.1 us -> 20.9 us  [swap(): return lax.all_to_all(values, axis, 0, 0, tiled=False)]
    ppermute x6, waiting for transfers between devices: 8.25 us -> 5.49 us  [along(): return lax.ppermute(values, 'y', [(i, (i + step) % 4) for i in range(4)])]
    pallas_call x5 -> x7, Pallas kernels: 9.31 us -> 8.81 us  [the longest x2 3.18 us: partial_products(): pl.pallas_call(partial_kernel, grid_spec=pltpu.PrefetchScalarGridSpec(num...]
  transfers between devices with their start and end apart: 26 -> 18, of which waited for: 10 -> 10; matrix products, arithmetic and copies ran while one was open for 1% -> 1% of each run, Pallas kernels for 8% -> 8%
where the time goes in v3:
time: 119 us; the launch traced here: 118 us
  waiting for transfers between devices  52.5 us (44%)
  starting transfers between devices  37.1 us (31%)
  Pallas kernels  16.5 us (14%)
  local copies, waits for them, and re-layouts  8.94 us (8%)
  other arithmetic  1.56 us (1%)
  between operations  1.49 us (1%)
    all_to_all x4, waiting for transfers between devices, swap(): return lax.all_to_all(values, axis, 0, 0, tiled=False)  38.4 us
    all_to_all x4, starting transfers between devices, swap(): return lax.all_to_all(values, axis, 0, 0, tiled=False)  20.9 us
    ppermute x6, starting transfers between devices, along(): return lax.ppermute(values, 'y', [(i, (i + step) % 4) for i in range(4)])  9.92 us
    unnamed x22, local copies, waits for them, and re-layouts  8.85 us
    ppermute x6, waiting for transfers between devices, along(): return lax.ppermute(values, 'y', [(i, (i + step) % 4) for i in range(4)])  5.49 us
    ppermute x1, waiting for transfers between devices, body(): other_hidden = lax.ppermute(own_hidden, 'xl', flip)  5.11 us
    ppermute x1, waiting for transfers between devices, body(): beside = lax.ppermute(scaled, 'xl', flip)  3.5 us
    pallas_call x2, Pallas kernels, partial_products(): pl.pallas_call(partial_kernel, grid_spec=pltpu.PrefetchScalarGridSpec(num...  3.18 us
  transfers between devices with their start and end apart: 18, of which 10 were waited for; matrix products, arithmetic and copies ran while one was open for 1% of the time, Pallas kernels for 8%

profile of v3, /device:TPU:2, one launch (start us, length us, event | category | flops | bytes accessed | tf_op | source)
XLA Modules:
  0.0 118.1 jit_solution(3838711059275759969)
XLA Ops:
  0.0 2.3 %pack.1 = bf16[8,128,512]{2,1,0:T(8,128)(2,1)} custom-call(s32[1]{0:T(128)} %bitcast.1.core_ref, bf16[32,8192]{1,0:T(8,128)(2,1)} %bitcast.16, bf16[32,8192]{1,0:T(8,128)(2,1)} %bitcast.17, bf16[64,512]{1,0:T(8,128)(2,1)} %resp_ref.1), custom_call_target="tpu_custom_call" | custom-call | tf_op jit(solution)/shard_map/pack/pallas_call | solution.py:72
  2.4 8.5 %all-to-all-start = ((bf16[8,128,512]{2,1,0:T(8,128)(2,1)}), bf16[8,128,512]{2,1,0:T(8,128)(2,1)S(1)}, u32[]{:S(2)}, u32[]{:S(2)}) async-start(bf16[8,128,512]{2,1,0:T(8,128)(2,1)} %pack.1), calls=%async_computation | async-start | bytes 2097152 | tf_op jit(solution)/shard_map/all_to_all | solution.py:429
  11.5 0.0 copy-done.10
  11.5 0.1 stack.40.info_ref
  11.6 0.0 copy-done.1
  11.6 1.0 scale_rows.1.own_ref
  12.6 0.6 collective-permute-start
  13.1 2.2 %copy-done = bf16[256,8192]{1,0:T(8,128)(2,1)S(1)} copy-done((bf16[256,8192]{1,0:T(8,128)(2,1)S(1)}, bf16[256,8192]{1,0:T(8,128)(2,1)}, u32[]{:S(2)}) %copy-start) | copy-done | bytes 4194328
  15.3 0.8 pick_columns.1
  16.1 0.8 copy-done.4
  16.9 0.8 copy-done.6
  17.7 0.8 copy-done.8
  18.5 1.5 %collective-permute-start.2 = (bf16[256,1024]{1,0:T(8,128)(2,1)S(1)}, bf16[256,1024]{1,0:T(8,128)(2,1)S(1)}, u32[]{:S(2)}, u32[]{:S(2)}) collective-permute-start(bf16[256,1024]{1,0:T(8,128)(2,1)S(1)} %get-tuple-element.16.refs_1_), channel_id=1, source_target_pairs={{0,1},{1,0},{2,3},{3,2},{4,5},{5,4},{6,7},{7,6},{8,9},{9,8},{10,11... | collective-permute-start | bytes 1572872 | tf_op jit(solution)/shard_map/ppermute | solution.py:472
  20.0 0.1 pad_add_fusion.1.scalars_ref
  20.1 3.5 %collective-permute-done.refs_0_.other_ref = bf16[336,512]{1,0:T(8,128)(2,1)S(1)} collective-permute-done((bf16[336,512]{1,0:T(8,128)(2,1)S(1)}, bf16[336,512]{1,0:T(8,128)(2,1)S(1)}, u32[]{:S(2)}, u32[]{:S(2)}) %collective-permute-start) | collective-permute-done | bytes 344096 | tf_op jit(solution)/shard_map/ppermute | solution.py:470
  23.6 16.0 %all-to-all-done.got_ref = bf16[8,128,512]{2,1,0:T(8,128)(2,1)S(1)} async-done(((bf16[8,128,512]{2,1,0:T(8,128)(2,1)}), bf16[8,128,512]{2,1,0:T(8,128)(2,1)S(1)}, u32[]{:S(2)}, u32[]{:S(2)}) %all-to-all-start) | async-done | bytes 1048608 | tf_op jit(solution)/shard_map/all_to_all | solution.py:429
  39.6 0.9 split.1
  40.4 0.0 collective-permute-start.1
  40.4 0.5 collective-permute-start.3
  41.0 0.1 pad_add_fusion.scalars_ref
  41.1 0.6 fusion.11
  41.7 0.0 collective-permute-done.2.refs_1_.refs_0_
  41.7 1.7 %collective-permute-start.4 = (bf16[256,1024]{1,0:T(8,128)(2,1)S(1)}, bf16[256,1024]{1,0:T(8,128)(2,1)S(1)}, u32[]{:S(2)}, u32[]{:S(2)}) collective-permute-start(bf16[256,1024]{1,0:T(8,128)(2,1)S(1)} %collective-permute-done.2.refs_1_.refs_0_), channel_id=1, source_target_pairs={{0,32},{32,0},{64,96},{96,64},{1,33},{33,1},{65,97},{97,65},{2,34}... | collective-permute-start | bytes 1572872 | tf_op jit(solution)/shard_map/ppermute | solution.py:479
  43.3 1.6 %partial_products.2.refs_0_ = bf16[8,176,128]{2,1,0:T(8,128)(2,1)} custom-call(s32[2]{0:T(128)S(1)} %pad_add_fusion.1.scalars_ref, bf16[8,64,512]{2,1,0:T(8,128)(2,1)S(1)} %get-tuple-element.17.weight_ref, bf16[336,512]{1,0:T(8,128)(2,1)S(1)} %scale_rows.1.own_ref, bf16[336,512]{1,0:T(8,128)(2,1)S(1)} %collective-permute-done.refs_0_.other_ref), custom_call_target="tpu_custom_call" | custom-call | tf_op jit(solution)/shard_map/partial_products/pallas_call | solution.py:181
  44.9 0.0 collective-permute-done.1.weight_ref
  44.9 1.6 %partial_products.3 = bf16[8,176,128]{2,1,0:T(8,128)(2,1)} custom-call(s32[2]{0:T(128)S(1)} %pad_add_fusion.scalars_ref, bf16[8,64,512]{2,1,0:T(8,128)(2,1)S(1)} %collective-permute-done.1.weight_ref, bf16[336,512]{1,0:T(8,128)(2,1)S(1)} %scale_rows.1.own_ref, ...), custom_call_target="tpu_custom_call", output_to_operand_aliasing={{}: (4, {})} | custom-call | tf_op jit(solution)/shard_map/partial_products/pallas_call | solution.py:181
  46.5 3.4 %all-to-all-start.1 = ((bf16[8,176,128]{2,1,0:T(8,128)(2,1)}), bf16[8,176,128]{2,1,0:T(8,128)(2,1)S(1)}, u32[]{:S(2)}, u32[]{:S(2)}) async-start(bf16[8,176,128]{2,1,0:T(8,128)(2,1)} %partial_products.3), calls=%async_computation.1 | async-start | bytes 720896 | tf_op jit(solution)/shard_map/all_to_all | solution.py:429
  50.0 5.1 %collective-permute-done.3.other_ref = bf16[8,64,512]{2,1,0:T(8,128)(2,1)} collective-permute-done((bf16[8,64,512]{2,1,0:T(8,128)(2,1)}, bf16[8,64,512]{2,1,0:T(8,128)(2,1)}, u32[]{:S(2)}, u32[]{:S(2)}) %collective-permute-start.3) | collective-permute-done | bytes 524320 | tf_op jit(solution)/shard_map/ppermute | solution.py:478
  55.1 2.2 %copy-done.3 = bf16[8192,256]{1,0:T(8,128)(2,1)S(1)} copy-done((bf16[8192,256]{1,0:T(8,128)(2,1)S(1)}, bf16[8192,256]{1,0:T(8,128)(2,1)}, u32[]{:S(2)}) %copy-start.3) | copy-done | bytes 4194328
  57.3 2.3 %queries.1.refs_0_ = bf16[64,256]{1,0:T(8,128)(2,1)S(1)} custom-call(s32[6]{0:T(128)S(1)} %stack.40.info_ref, f32[16,1,512]{2,1,0:T(1,128)S(1)} %bitcast.15, f32[2,224,128]{2,1,0:T(8,128)S(1)} %pad_maximum_fusion.trig_ref, bf16[8192,256]{1,0:T(8,128)(2,1)S(1)} %copy-done.3, bf16[8,64,512]{2,1,0:T(8,128)(2,1)} %get-tuple-element.18.own_ref, ...), custom_call_target="tpu_custom_call" | custom-call | flops 30000001024 | bytes 1000000 | tf_op jit(solution)/shard_map/queries/pallas_call | solution.py:259
  59.6 0.0 collective-permute-done.4.refs_1_
  59.6 4.6 %all-to-all-done.1.parts_ref = bf16[8,176,128]{2,1,0:T(8,128)(2,1)S(1)} async-done(((bf16[8,176,128]{2,1,0:T(8,128)(2,1)}), bf16[8,176,128]{2,1,0:T(8,128)(2,1)S(1)}, u32[]{:S(2)}, u32[]{:S(2)}) %all-to-all-start.1) | async-done | bytes 360480 | tf_op jit(solution)/shard_map/all_to_all | solution.py:429
  64.3 1.2 finish_keys.1
  65.4 5.5 %all-to-all-start.2 = ((bf16[16,160,128]{2,1,0:T(8,128)(2,1)}), bf16[16,160,128]{2,1,0:T(8,128)(2,1)S(1)}, u32[]{:S(2)}, u32[]{:S(2)}) async-start(bf16[16,160,128]{2,1,0:T(8,128)(2,1)} %finish_keys.1), calls=%async_computation.2 | async-start | bytes 1310720 | tf_op jit(solution)/shard_map/all_to_all | solution.py:429
  71.0 0.4 collective-permute-start.5
  71.4 3.2 %collective-permute-start.6 = (bf16[64,256]{1,0:T(8,128)(2,1)S(1)}, bf16[64,256]{1,0:T(8,128)(2,1)S(1)}, u32[]{:S(2)}, u32[]{:S(2)}) collective-permute-start(bf16[64,256]{1,0:T(8,128)(2,1)S(1)} %queries.1.refs_0_), channel_id=1, source_target_pairs={{0,64},{32,96},{64,0},{96,32},{1,65},{33,97},{65,1},{97,33},{2,66}... | collective-permute-start | bytes 98312 | tf_op jit(solution)/shard_map/ppermute | solution.py:486
  74.6 1.9 %collective-permute-start.7 = (bf16[64,256]{1,0:T(8,128)(2,1)S(1)}, bf16[64,256]{1,0:T(8,128)(2,1)S(1)}, u32[]{:S(2)}, u32[]{:S(2)}) collective-permute-start(bf16[64,256]{1,0:T(8,128)(2,1)S(1)} %queries.1.refs_0_), channel_id=1, source_target_pairs={{0,96},{32,0},{64,32},{96,64},{1,97},{33,1},{65,33},{97,65},{2,98}... | collective-permute-start | bytes 98312 | tf_op jit(solution)/shard_map/ppermute | solution.py:486
  76.5 0.0 collective-permute-done.5.refs_1_
  76.5 0.3 collective-permute-done.6.refs_2_
  76.8 1.7 %collective-permute-done.7.refs_3_ = bf16[64,256]{1,0:T(8,128)(2,1)S(1)} collective-permute-done((bf16[64,256]{1,0:T(8,128)(2,1)S(1)}, bf16[64,256]{1,0:T(8,128)(2,1)S(1)}, u32[]{:S(2)}, u32[]{:S(2)}) %collective-permute-start.7) | collective-permute-done | bytes 32800 | tf_op jit(solution)/shard_map/ppermute | solution.py:486
  78.5 3.2 %all-to-all-done.2.rows_ref = bf16[16,160,128]{2,1,0:T(8,128)(2,1)S(1)} async-done(((bf16[16,160,128]{2,1,0:T(8,128)(2,1)}), bf16[16,160,128]{2,1,0:T(8,128)(2,1)S(1)}, u32[]{:S(2)}, u32[]{:S(2)}) %all-to-all-start.2) | async-done | bytes 655392 | tf_op jit(solution)/shard_map/all_to_all | solution.py:429
  81.7 2.2 %attend.1 = (bf16[64,384]{1,0:T(8,128)(2,1)S(1)}, bf16[64,384]{1,0:T(8,128)(2,1)S(1)}, bf16[64,384]{1,0:T(8,128)(2,1)S(1)}, bf16[64,384]{1,0:T(8,128)(2,1)S(1)}) custom-call(s32[6]{0:T(128)S(1)} %stack.40.info_ref, bf16[16,160,128]{2,1,0:T(8,128)(2,1)S(1)} %all-to-all-done.2.rows_ref, bf16[64,256]{1,0:T(8,128)(2,1)S(1)} %queries.1.refs_0_, ...), custom_call_target="tpu_custom_call" | custom-call | tf_op jit(solution)/shard_map/attend/pallas_call | solution.py:326
  83.9 2.3 %collective-permute-start.8 = (bf16[64,384]{1,0:T(8,128)(2,1)S(1)}, bf16[64,384]{1,0:T(8,128)(2,1)S(1)}, u32[]{:S(2)}, u32[]{:S(2)}) collective-permute-start(bf16[64,384]{1,0:T(8,128)(2,1)S(1)} %get-tuple-element.20), channel_id=1, source_target_pairs={{0,96},{32,0},{64,32},{96,64},{1,97},{33,1},{65,33},{97,65},{2,98}... | collective-permute-start | bytes 147464 | tf_op jit(solution)/shard_map/ppermute | solution.py:486
  86.2 0.8 collective-permute-start.9
  87.0 1.3 %collective-permute-start.10 = (bf16[64,384]{1,0:T(8,128)(2,1)S(1)}, bf16[64,384]{1,0:T(8,128)(2,1)S(1)}, u32[]{:S(2)}, u32[]{:S(2)}) collective-permute-start(bf16[64,384]{1,0:T(8,128)(2,1)S(1)} %get-tuple-element.22), channel_id=1, source_target_pairs={{0,32},{32,64},{64,96},{96,0},{1,33},{33,65},{65,97},{97,1},{2,34}... | collective-permute-start | bytes 147464 | tf_op jit(solution)/shard_map/ppermute | solution.py:486
  88.3 0.0 collective-permute-start.12
  88.3 0.5 collective-permute-start.13
  88.8 0.0 collective-permute-done.8.refs_1_
  88.8 2.9 %collective-permute-done.9.refs_2_ = bf16[64,384]{1,0:T(8,128)(2,1)S(1)} collective-permute-done((bf16[64,384]{1,0:T(8,128)(2,1)S(1)}, bf16[64,384]{1,0:T(8,128)(2,1)S(1)}, u32[]{:S(2)}, u32[]{:S(2)}) %collective-permute-start.9) | collective-permute-done | bytes 49184 | tf_op jit(solution)/shard_map/ppermute | solution.py:486
  91.8 0.5 collective-permute-done.10.refs_3_
  92.3 0.3 merge.1.own_ref
  92.6 1.5 %collective-permute-start.11 = (bf16[64,256]{1,0:T(8,128)(2,1)S(1)}, bf16[64,256]{1,0:T(8,128)(2,1)S(1)}, u32[]{:S(2)}, u32[]{:S(2)}) collective-permute-start(bf16[64,256]{1,0:T(8,128)(2,1)S(1)} %merge.1.own_ref), channel_id=1, source_target_pairs={{0,1},{1,0},{2,3},{3,2},{4,5},{5,4},{6,7},{7,6},{8,9},{9,8},{10,11... | collective-permute-start | bytes 98312 | tf_op jit(solution)/shard_map/ppermute | solution.py:491
  94.1 0.0 copy-done.5
  94.1 1.0 copy-done.7
  95.2 1.0 copy-done.9
  96.2 0.5 project_own.1.started_ref
  96.7 0.0 collective-permute-done.12.refs_2_
  96.7 0.0 collective-permute-done.13.refs_3_
  96.7 0.0 collective-permute-done.11.other_ref
  96.7 1.8 %project.1 = bf16[8,64,512]{2,1,0:T(8,128)(2,1)} custom-call(s32[6]{0:T(128)S(1)} %stack.40.info_ref, f32[8,64,512]{2,1,0:T(8,128)S(1)} %project_own.1.started_ref, bf16[64,256]{1,0:T(8,128)(2,1)S(1)} %collective-permute-done.11.other_ref, bf16[256,1024]{1,0:T(8,128)(2,1)S(1)} %collective-permute-done.2.refs_1_.refs_0_, ...), custom_call_target="tpu_custom_call" | custom-call | tf_op jit(solution)/shard_map/project/pallas_call | solution.py:395
  98.5 3.5 %all-to-all-start.3 = ((bf16[8,64,512]{2,1,0:T(8,128)(2,1)}), bf16[8,64,512]{2,1,0:T(8,128)(2,1)S(1)}, u32[]{:S(2)}, u32[]{:S(2)}) async-start(bf16[8,64,512]{2,1,0:T(8,128)(2,1)} %project.1), calls=%async_computation.3 | async-start | bytes 1048576 | tf_op jit(solution)/shard_map/all_to_all | solution.py:429
  102.7 14.6 %all-to-all-done.3 = bf16[8,64,512]{2,1,0:T(8,128)(2,1)S(1)} async-done(((bf16[8,64,512]{2,1,0:T(8,128)(2,1)}), bf16[8,64,512]{2,1,0:T(8,128)(2,1)S(1)}, u32[]{:S(2)}, u32[]{:S(2)}) %all-to-all-start.3) | async-done | bytes 524320 | tf_op jit(solution)/shard_map/all_to_all | solution.py:429
  117.3 0.1 convert_reduce_fusion
  117.4 0.7 select_convert_fusion
  (19 shorter events, 0.1 us)
Async XLA Ops:
  0.0 11.6 %copy-start.1 = (bf16[64,512]{1,0:T(8,128)(2,1)S(1)}, bf16[64,512]{1,0:T(8,128)(2,1)}, u32[]{:S(2)}) copy-start(bf16[64,512]{1,0:T(8,128)(2,1)} %resp_ref.1) | copy-start | bytes 196612
  0.0 11.5 %copy-start.10 = (bf16[8192]{0:T(1024)(128)(2,1)S(1)}, bf16[8192]{0:T(1024)(128)(2,1)}, u32[]{:S(2)}) copy-start(bf16[8192]{0:T(1024)(128)(2,1)} %param.11) | copy-start | bytes 49156
  0.0 11.6 %copy-start.2 = (bf16[256,512]{1,0:T(8,128)(2,1)S(1)}, bf16[256,512]{1,0:T(8,128)(2,1)}, u32[]{:S(2)}) copy-start(bf16[256,512]{1,0:T(8,128)(2,1)} %prompt_ref.1) | copy-start | bytes 786436
  2.4 37.2 %all-to-all-start = ((bf16[8,128,512]{2,1,0:T(8,128)(2,1)}), bf16[8,128,512]{2,1,0:T(8,128)(2,1)S(1)}, u32[]{:S(2)}, u32[]{:S(2)}) async-start(bf16[8,128,512]{2,1,0:T(8,128)(2,1)} %pack.1), calls=%async_computation | async-start | bytes 2097152 | tf_op jit(solution)/shard_map/all_to_all | solution.py:429
  12.6 11.0 %collective-permute-start = (bf16[336,512]{1,0:T(8,128)(2,1)S(1)}, bf16[336,512]{1,0:T(8,128)(2,1)S(1)}, u32[]{:S(2)}, u32[]{:S(2)}) collective-permute-start(bf16[336,512]{1,0:T(8,128)(2,1)S(1)} %scale_rows.1.own_ref), channel_id=1, source_target_pairs={{0,1},{1,0},{2,3},{3,2},{4,5},{5,4},{6,7},{7,6},{8,9},{9,8},{10,11... | collective-permute-start | bytes 1032200 | tf_op jit(solution)/shard_map/ppermute | solution.py:470
  13.1 2.2 %copy-start = (bf16[256,8192]{1,0:T(8,128)(2,1)S(1)}, bf16[256,8192]{1,0:T(8,128)(2,1)}, u32[]{:S(2)}) copy-start(bf16[256,8192]{1,0:T(8,128)(2,1)} %weight_ref.2) | copy-start | bytes 12582916
  16.1 0.8 copy-start.4
  16.9 0.8 copy-start.6
  17.7 0.8 copy-start.8
  18.5 23.2 %collective-permute-start.2 = (bf16[256,1024]{1,0:T(8,128)(2,1)S(1)}, bf16[256,1024]{1,0:T(8,128)(2,1)S(1)}, u32[]{:S(2)}, u32[]{:S(2)}) collective-permute-start(bf16[256,1024]{1,0:T(8,128)(2,1)S(1)} %get-tuple-element.16.refs_1_), channel_id=1, source_target_pairs={{0,1},{1,0},{2,3},{3,2},{4,5},{5,4},{6,7},{7,6},{8,9},{9,8},{10,11... | collective-permute-start | bytes 1572872 | tf_op jit(solution)/shard_map/ppermute | solution.py:472
  40.4 4.5 %collective-permute-start.1 = (bf16[8,64,512]{2,1,0:T(8,128)(2,1)S(1)}, bf16[8,64,512]{2,1,0:T(8,128)(2,1)S(1)}, u32[]{:S(2)}, u32[]{:S(2)}) collective-permute-start(bf16[8,64,512]{2,1,0:T(8,128)(2,1)S(1)} %get-tuple-element.17.weight_ref), channel_id=1, source_target_pairs={{0,16},{16,0},{1,17},{17,1},{2,18},{18,2},{3,19},{19,3},{4,20},{20... | collective-permute-start | bytes 1572872 | tf_op jit(solution)/shard_map/ppermute | solution.py:474
  40.4 14.6 %collective-permute-start.3 = (bf16[8,64,512]{2,1,0:T(8,128)(2,1)}, bf16[8,64,512]{2,1,0:T(8,128)(2,1)}, u32[]{:S(2)}, u32[]{:S(2)}) collective-permute-start(bf16[8,64,512]{2,1,0:T(8,128)(2,1)} %get-tuple-element.18.own_ref), channel_id=1, source_target_pairs={{0,1},{1,0},{2,3},{3,2},{4,5},{5,4},{6,7},{7,6},{8,9},{9,8},{10,11... | collective-permute-start | bytes 1572872 | tf_op jit(solution)/shard_map/ppermute | solution.py:478
  41.7 17.9 %collective-permute-start.4 = (bf16[256,1024]{1,0:T(8,128)(2,1)S(1)}, bf16[256,1024]{1,0:T(8,128)(2,1)S(1)}, u32[]{:S(2)}, u32[]{:S(2)}) collective-permute-start(bf16[256,1024]{1,0:T(8,128)(2,1)S(1)} %collective-permute-done.2.refs_1_.refs_0_), channel_id=1, source_target_pairs={{0,32},{32,0},{64,96},{96,64},{1,33},{33,1},{65,97},{97,65},{2,34}... | collective-permute-start | bytes 1572872 | tf_op jit(solution)/shard_map/ppermute | solution.py:479
  46.5 17.7 %all-to-all-start.1 = ((bf16[8,176,128]{2,1,0:T(8,128)(2,1)}), bf16[8,176,128]{2,1,0:T(8,128)(2,1)S(1)}, u32[]{:S(2)}, u32[]{:S(2)}) async-start(bf16[8,176,128]{2,1,0:T(8,128)(2,1)} %partial_products.3), calls=%async_computation.1 | async-start | bytes 720896 | tf_op jit(solution)/shard_map/all_to_all | solution.py:429
  55.1 2.2 %copy-start.3 = (bf16[8192,256]{1,0:T(8,128)(2,1)S(1)}, bf16[8192,256]{1,0:T(8,128)(2,1)}, u32[]{:S(2)}) copy-start(bf16[8192,256]{1,0:T(8,128)(2,1)} %weight_ref.3) | copy-start | bytes 12582916
  59.6 34.5 %copy-start.5 = (bf16[256,1024]{1,0:T(8,128)(2,1)S(1)}, bf16[256,1024]{1,0:T(8,128)(2,1)}, u32[]{:S(2)}) copy-start(bf16[256,1024]{1,0:T(8,128)(2,1)} %copy-done.4) | copy-start | bytes 1572868
  65.4 16.2 %all-to-all-start.2 = ((bf16[16,160,128]{2,1,0:T(8,128)(2,1)}), bf16[16,160,128]{2,1,0:T(8,128)(2,1)S(1)}, u32[]{:S(2)}, u32[]{:S(2)}) async-start(bf16[16,160,128]{2,1,0:T(8,128)(2,1)} %finish_keys.1), calls=%async_computation.2 | async-start | bytes 1310720 | tf_op jit(solution)/shard_map/all_to_all | solution.py:429
  71.0 5.5 %collective-permute-start.5 = (bf16[64,256]{1,0:T(8,128)(2,1)S(1)}, bf16[64,256]{1,0:T(8,128)(2,1)S(1)}, u32[]{:S(2)}, u32[]{:S(2)}) collective-permute-start(bf16[64,256]{1,0:T(8,128)(2,1)S(1)} %queries.1.refs_0_), channel_id=1, source_target_pairs={{0,32},{32,64},{64,96},{96,0},{1,33},{33,65},{65,97},{97,1},{2,34}... | collective-permute-start | bytes 98312 | tf_op jit(solution)/shard_map/ppermute | solution.py:486
  71.4 5.4 %collective-permute-start.6 = (bf16[64,256]{1,0:T(8,128)(2,1)S(1)}, bf16[64,256]{1,0:T(8,128)(2,1)S(1)}, u32[]{:S(2)}, u32[]{:S(2)}) collective-permute-start(bf16[64,256]{1,0:T(8,128)(2,1)S(1)} %queries.1.refs_0_), channel_id=1, source_target_pairs={{0,64},{32,96},{64,0},{96,32},{1,65},{33,97},{65,1},{97,33},{2,66}... | collective-permute-start | bytes 98312 | tf_op jit(solution)/shard_map/ppermute | solution.py:486
  74.6 3.9 %collective-permute-start.7 = (bf16[64,256]{1,0:T(8,128)(2,1)S(1)}, bf16[64,256]{1,0:T(8,128)(2,1)S(1)}, u32[]{:S(2)}, u32[]{:S(2)}) collective-permute-start(bf16[64,256]{1,0:T(8,128)(2,1)S(1)} %queries.1.refs_0_), channel_id=1, source_target_pairs={{0,96},{32,0},{64,32},{96,64},{1,97},{33,1},{65,33},{97,65},{2,98}... | collective-permute-start | bytes 98312 | tf_op jit(solution)/shard_map/ppermute | solution.py:486
  83.9 4.9 %collective-permute-start.8 = (bf16[64,384]{1,0:T(8,128)(2,1)S(1)}, bf16[64,384]{1,0:T(8,128)(2,1)S(1)}, u32[]{:S(2)}, u32[]{:S(2)}) collective-permute-start(bf16[64,384]{1,0:T(8,128)(2,1)S(1)} %get-tuple-element.20), channel_id=1, source_target_pairs={{0,96},{32,0},{64,32},{96,64},{1,97},{33,1},{65,33},{97,65},{2,98}... | collective-permute-start | bytes 147464 | tf_op jit(solution)/shard_map/ppermute | solution.py:486
  86.2 5.6 %collective-permute-start.9 = (bf16[64,384]{1,0:T(8,128)(2,1)S(1)}, bf16[64,384]{1,0:T(8,128)(2,1)S(1)}, u32[]{:S(2)}, u32[]{:S(2)}) collective-permute-start(bf16[64,384]{1,0:T(8,128)(2,1)S(1)} %get-tuple-element.21), channel_id=1, source_target_pairs={{0,64},{32,96},{64,0},{96,32},{1,65},{33,97},{65,1},{97,33},{2,66}... | collective-permute-start | bytes 147464 | tf_op jit(solution)/shard_map/ppermute | solution.py:486
  87.0 5.3 %collective-permute-start.10 = (bf16[64,384]{1,0:T(8,128)(2,1)S(1)}, bf16[64,384]{1,0:T(8,128)(2,1)S(1)}, u32[]{:S(2)}, u32[]{:S(2)}) collective-permute-start(bf16[64,384]{1,0:T(8,128)(2,1)S(1)} %get-tuple-element.22), channel_id=1, source_target_pairs={{0,32},{32,64},{64,96},{96,0},{1,33},{33,65},{65,97},{97,1},{2,34}... | collective-permute-start | bytes 147464 | tf_op jit(solution)/shard_map/ppermute | solution.py:486
  88.3 8.4 %collective-permute-start.12 = (bf16[256,1024]{1,0:T(8,128)(2,1)S(1)}, bf16[256,1024]{1,0:T(8,128)(2,1)S(1)}, u32[]{:S(2)}, u32[]{:S(2)}) collective-permute-start(bf16[256,1024]{1,0:T(8,128)(2,1)S(1)} %collective-permute-done.2.refs_1_.refs_0_), channel_id=1, source_target_pairs={{0,16},{16,0},{1,17},{17,1},{2,18},{18,2},{3,19},{19,3},{4,20},{20... | collective-permute-start | bytes 1572872 | tf_op jit(solution)/shard_map/ppermute | solution.py:481
  88.3 8.4 %collective-permute-start.13 = (bf16[256,1024]{1,0:T(8,128)(2,1)S(1)}, bf16[256,1024]{1,0:T(8,128)(2,1)S(1)}, u32[]{:S(2)}, u32[]{:S(2)}) collective-permute-start(bf16[256,1024]{1,0:T(8,128)(2,1)S(1)} %collective-permute-done.4.refs_1_), channel_id=1, source_target_pairs={{0,16},{16,0},{1,17},{17,1},{2,18},{18,2},{3,19},{19,3},{4,20},{20... | collective-permute-start | bytes 1572872 | tf_op jit(solution)/shard_map/ppermute | solution.py:481
  92.6 4.1 %collective-permute-start.11 = (bf16[64,256]{1,0:T(8,128)(2,1)S(1)}, bf16[64,256]{1,0:T(8,128)(2,1)S(1)}, u32[]{:S(2)}, u32[]{:S(2)}) collective-permute-start(bf16[64,256]{1,0:T(8,128)(2,1)S(1)} %merge.1.own_ref), channel_id=1, source_target_pairs={{0,1},{1,0},{2,3},{3,2},{4,5},{5,4},{6,7},{7,6},{8,9},{9,8},{10,11... | collective-permute-start | bytes 98312 | tf_op jit(solution)/shard_map/ppermute | solution.py:491
  94.1 1.0 copy-start.7
  95.2 1.0 copy-start.9
  98.5 18.8 %all-to-all-start.3 = ((bf16[8,64,512]{2,1,0:T(8,128)(2,1)}), bf16[8,64,512]{2,1,0:T(8,128)(2,1)S(1)}, u32[]{:S(2)}, u32[]{:S(2)}) async-start(bf16[8,64,512]{2,1,0:T(8,128)(2,1)} %project.1), calls=%async_computation.3 | async-start | bytes 1048576 | tf_op jit(solution)/shard_map/all_to_all | solution.py:429

commit v4 on v3

--- a/solution.py
+++ b/solution.py
@@ -22,6 +22,7 @@
 RESP = 64
 PROMPT_ROWS = 256
 ROWS = 160
+SHARED_ROWS = 144
 SENT_ROWS = ROWS + 16
 PACKED = 64 + RESP
 EPSILON = 1e-05
@@ -54,15 +55,13 @@
 
 def pack_kernel(core_ref, key_ref, value_ref, hidden_ref, out_ref):
     row, col = iota((32, 64), 0), iota((32, 64), 1)
-    source = ((row >> 3) & 1) * 32 + (row & 7) * 4 + 2 * core_ref[0] + (row >> 4)
+    source = ((row >> 2) & 1) * 32 + (4 * core_ref[0] + (row & 3)) * 4 + (row >> 3)
     pick = jnp.where(col == source, 1.0, 0.0).astype(BF16)
     both = jnp.concatenate([key_ref[...], value_ref[...]], axis=0)
     for i in range(out_ref.shape[0]):
         for x in range(2):
             at = (2 * i + x) * BLOCK
-            rows = dot(pick, both[:, at : at + BLOCK]).astype(BF16)
-            for head in range(2):
-                out_ref[i, (2 * head + x) * 16 : (2 * head + x) * 16 + 16] = rows[head * 16 : head * 16 + 16]
+            out_ref[i, 32 * x : 32 * x + 32] = dot(pick, both[:, at : at + BLOCK]).astype(BF16)
         out_ref[i, 64:] = hidden_ref[...]
 
 
@@ -124,73 +123,53 @@
     )(info, prompt, resp, gain)
 
 
-def partial_kernel(scalars_ref, weight_ref, own_ref, other_ref, *refs):
-    out_ref = refs[-1]
-    is_first = scalars_ref[1] == 0
-    own, other = own_ref[: 2 * ROWS], other_ref[: 2 * ROWS]
-    rows = (jnp.where(is_first, own, other), jnp.where(is_first, other, own))
-    total = jnp.zeros((2 * ROWS, 256), F32)
-    for x in range(2):
-        weights = [weight_ref[:, (2 * head + x) * 16 : (2 * head + x) * 16 + 16] for head in range(2)]
-        weights = [piece.reshape(128, BLOCK) for piece in weights]
-        total += dot_t(rows[x], jnp.concatenate(weights, axis=0))
+def split_kernel(got_ref, *refs):
+    refs[-1][...] = got_ref[:, 64:]
+
+
+def split(got, after):
+    return pl.pallas_call(
+        split_kernel,
+        in_specs=[pl.BlockSpec(memory_space=pltpu.VMEM)] * (1 + len(after)),
+        out_shape=jax.ShapeDtypeStruct((8, RESP, BLOCK), BF16),
+        compiler_params=params(SMALL),
+        name="split",
+    )(got, *after)
+
+
+def partial_kernel(info_ref, got_ref, *refs):
+    out_ref = refs[4]
+    xl, core = info_ref[XL_AT], info_ref[CORE_AT]
+    weights = [got_ref[:, pl.ds(pl.multiple_of(32 * x, 32), 32)].reshape(256, BLOCK) for x in (xl, 1 - xl)]
+    row, col = iota((256, 512), 0), iota((256, 512), 1)
+    target = ((row >> 3) & 3) * 128 + (row >> 5) * 8 + (row & 7)
+    total = jnp.zeros((2 * ROWS, 512), F32)
+    sums = []
+    for n, at in enumerate((core, 1 - core)):
+        here, there = refs[2 * n], refs[2 * n + 1]
+        raw = dot_t(here[: 2 * ROWS], weights[0]) + dot_t(there[: 2 * ROWS], weights[1])
+        pick = jnp.where(col == target + 64 * at, 1.0, 0.0).astype(BF16)
+        total += dot(raw.astype(BF16), pick)
+        sums.append((here[2 * ROWS :, :128], there[2 * ROWS :, :128]))
     total = total.astype(BF16)
-    own_sums, other_sums = own_ref[2 * ROWS :, :128], other_ref[2 * ROWS :, :128]
-    for head in range(2):
-        for half in range(2):
+    for half in range(2):
+        lines = [[piece[4 * half : 4 * half + 4] for piece in pair] for pair in sums]
+        lines = [jnp.concatenate(lines[0] + lines[1], axis=0), jnp.concatenate(lines[1] + lines[0], axis=0)]
+        for head in range(4):
             to = 2 * head + half
             out_ref[to, :ROWS] = total[ROWS * half : ROWS * half + ROWS, head * 128 : head * 128 + 128]
-            sums = jnp.concatenate(
-                [own_sums[4 * half : 4 * half + 4], other_sums[4 * half : 4 * half + 4], jnp.zeros((8, 128), BF16)],
-                axis=0,
-            )
-            out_ref[to, ROWS:] = sums
-
-
-def split_kernel(got_ref, *refs):
-    weights_ref, hidden_ref = refs[-2:]
-    weights_ref[...] = got_ref[:, :64]
-    hidden_ref[...] = got_ref[:, 64:]
-
-
-def split(got, after):
-    return pl.pallas_call(
-        split_kernel,
-        in_specs=[pl.BlockSpec(memory_space=pltpu.VMEM)] * (1 + len(after)),
-        out_shape=(jax.ShapeDtypeStruct((8, 64, BLOCK), BF16), jax.ShapeDtypeStruct((8, RESP, BLOCK), BF16)),
-        compiler_params=params(SMALL),
-        name="split",
-    )(got, *after)
-
-
-def partial_products(scalars, weights, own, other, before=None, after=None):
-    def whole(shape):
-        return pl.BlockSpec(shape, lambda i, scalars: (0,) * len(shape))
-
-    rows = (2 * ROWS + 16, BLOCK)
-    in_specs = [whole((8, 64, BLOCK)), whole(rows), whole(rows)]
-    operands = [scalars, weights, own, other]
-    aliases = {}
-    if before is not None:
-        in_specs.append(pl.BlockSpec(memory_space=pl.ANY))
-        operands.append(before)
-        aliases = {len(operands) - 1: 0}
-    if after is not None:
-        in_specs.append(pl.BlockSpec((16, 128), lambda i, scalars: (0, 0)))
-        operands.append(after)
+            out_ref[to, ROWS:] = jnp.where(core == 0, lines[0], lines[1])
+
+
+def partial_products(info, got, blocks):
+    vmem = pl.BlockSpec(memory_space=pltpu.VMEM)
     return pl.pallas_call(
         partial_kernel,
-        grid_spec=pltpu.PrefetchScalarGridSpec(
-            num_scalar_prefetch=1,
-            grid=(1,),
-            in_specs=in_specs,
-            out_specs=pl.BlockSpec((4, SENT_ROWS, 128), lambda i, scalars: (scalars[0], 0, 0)),
-        ),
+        in_specs=[pl.BlockSpec(memory_space=pltpu.SMEM)] + [vmem] * 5,
         out_shape=jax.ShapeDtypeStruct((8, SENT_ROWS, 128), BF16),
-        input_output_aliases=aliases,
         compiler_params=params(SMALL),
         name="partial_products",
-    )(*operands)
+    )(info, got, *blocks)
 
 
 def turn(values, cosine, sine):
@@ -201,37 +180,48 @@
     out_ref = refs[-1]
     total = jnp.sum(parts_ref[...].astype(F32), axis=0)
     sums = total[ROWS:]
-    column = []
-    for n, count in enumerate((128, ROWS - 128)):
-        line = sums[2 * n : 2 * n + 1] + sums[2 * n + 1 : 2 * n + 2] + sums[2 * n + 4 : 2 * n + 5]
-        line += sums[2 * n + 5 : 2 * n + 6]
-        diagonal = iota((count, 128), 0) == iota((count, 128), 1)
-        spread = jnp.where(diagonal, jnp.broadcast_to(line, (count, 128)), 0.0)
-        column.append(jnp.sum(spread, axis=1, keepdims=True))
-    factor = lax.rsqrt(jnp.concatenate(column, axis=0) * (1.0 / D) + EPSILON)
+    factors = []
+    for core in range(2):
+        column = []
+        for n, count in enumerate((128, ROWS - 128)):
+            at = 8 * core + 2 * n
+            line = sums[at : at + 1] + sums[at + 1 : at + 2] + sums[at + 4 : at + 5] + sums[at + 5 : at + 6]
+            diagonal = iota((count, 128), 0) == iota((count, 128), 1)
+            spread = jnp.where(diagonal, jnp.broadcast_to(line, (count, 128)), 0.0)
+            column.append(jnp.sum(spread, axis=1, keepdims=True))
+        factors.append(lax.rsqrt(jnp.concatenate(column, axis=0) * (1.0 / D) + EPSILON))
+    factor = jnp.where(iota((ROWS, 128), 1) < 64, factors[0], factors[1])
     raw = (total[:ROWS] * factor).astype(BF16)
     row, col = iota((128, 128), 0), iota((128, 128), 1)
-    target = ((row >> 3) & 1) * 64 + (row >> 4) * 8 + (row & 7)
+    target = (row & 64) + ((row >> 2) & 1) * 32 + ((row >> 3) & 7) * 4 + (row & 3)
     ordered = dot(raw, jnp.where(col == target, 1.0, 0.0).astype(BF16))
-    beside = dot(raw, jnp.where(col == (target ^ 32), 1.0, 0.0).astype(BF16))
-    result = (ordered * trig_ref[0, :ROWS] + beside * trig_ref[1, :ROWS]).astype(BF16)
+    beside = dot(raw, jnp.where(col == (target ^ 16), 1.0, 0.0).astype(BF16))
+    result = ordered * trig_ref[0, :ROWS] + beside * trig_ref[1, :ROWS]
+    prompt = result[:128].astype(BF16)
+    first, second = result[128:144], result[144:160]
+    left = iota((16, 128), 1) < 64
+    resp = (
+        jnp.where(left, first, pltpu.roll(second, 64, 1)).astype(BF16),
+        jnp.where(left, pltpu.roll(first, 64, 1), second).astype(BF16),
+    )
     for i in range(out_ref.shape[0]):
-        out_ref[i] = result
+        out_ref[i, :128] = prompt
+        out_ref[i, 128:] = resp[(i >> 2) & 1]
 
 
 def finish_keys(parts, trig, *after):
     return pl.pallas_call(
         finish_kernel,
         in_specs=[pl.BlockSpec(memory_space=pltpu.VMEM)] * (2 + len(after)),
-        out_shape=jax.ShapeDtypeStruct((16, ROWS, 128), BF16),
+        out_shape=jax.ShapeDtypeStruct((16, SHARED_ROWS, 128), BF16),
         compiler_params=params(SMALL),
         cost_estimate=LONG,
         name="finish_keys",
     )(parts, trig, *after)
 
 
-def by_xl(natural):
-    return ((natural >> 3) & 1) * 64 + (natural >> 4) * 8 + (natural & 7)
+def by_device(natural):
+    return ((natural >> 3) & 1) * 64 + ((natural >> 2) & 1) * 32 + (natural >> 4) * 4 + (natural & 3)
 
 
 def query_kernel(info_ref, gain_ref, trig_ref, weight_ref, own_ref, other_ref, out_ref):
@@ -247,7 +237,7 @@
             squares += jnp.sum(hidden * hidden, axis=1, keepdims=True)
     factor = lax.rsqrt(squares * (1.0 / D) + EPSILON)
     row, col = iota((128, 128), 0), iota((128, 128), 1)
-    order = jnp.where(col == by_xl(row), 1.0, 0.0).astype(BF16)
+    order = jnp.where(col == by_device(row), 1.0, 0.0).astype(BF16)
     for h in range(2):
         part = slice(h * HEAD_DIM, (h + 1) * HEAD_DIM)
         query = turn(total[:, part] * factor, trig_ref[0, ROWS:], trig_ref[1, ROWS:])
@@ -270,16 +260,37 @@
     queries, outs = refs[:4], refs[4:]
     own_y = info_ref[Y_AT]
 
-    def joined(block, at, count):
-        first, second = rows_ref[block, pl.ds(at, count)], rows_ref[block + 1, pl.ds(at, count)]
-        keys = jnp.concatenate([first[:, :HALF], second[:, :HALF]], axis=1)
-        return keys, jnp.concatenate([first[:, HALF:], second[:, HALF:]], axis=1)
-
-    prompt = [joined(2 * i, 0, 128) for i in range(8)]
-    prompt_keys, prompt_values = (jnp.concatenate([p[n] for p in prompt], axis=0) for n in range(2))
-    place = info_ref[PLACE_AT] * 4
-    own = [joined(place + 2 * half, 128, 32) for half in range(2)]
-    own_keys, own_values = (jnp.concatenate([o[n] for o in own], axis=0) for n in range(2))
+    row, col = iota((512, 512), 0), iota((512, 512), 1)
+    target = ((row >> 5) & 3) * 128 + ((row >> 7) & 1) * 64 + (row >> 8) * 32 + (row & 31)
+    pick = jnp.where(col == target, 1.0, 0.0).astype(BF16)
+
+    def joined(xh, zl, at, count):
+        pieces = [rows_ref[xh * 8 + core * 4 + zl * 2 + x, at : at + count] for core in range(2) for x in range(2)]
+        return dot(jnp.concatenate(pieces, axis=1), pick).astype(BF16)
+
+    prompt = [[joined(xh, zl, 0, 128) for zl in range(2)] for xh in range(2)]
+
+    def prompt_rows(kv):
+        return jnp.concatenate(
+            [
+                prompt[xh][zl][:, (2 * core + kv) * 128 : (2 * core + kv) * 128 + 128]
+                for xh in range(2)
+                for core in range(2)
+                for zl in range(2)
+            ],
+            axis=0,
+        )
+
+    prompt_keys, prompt_values = prompt_rows(0), prompt_rows(1)
+    own_xh = info_ref[PLACE_AT] // 2
+    own = [joined(own_xh, zl, 128, 16) for zl in range(2)]
+
+    def own_rows(kv):
+        return jnp.concatenate(
+            [o[:, (2 * n + kv) * 128 : (2 * n + kv) * 128 + 128] for o in own for n in range(2)], axis=0
+        )
+
+    own_keys, own_values = own_rows(0), own_rows(1)
     scale = HEAD_DIM ** (-0.5)
     power = scale * math.log2(math.e)
 
@@ -336,7 +347,7 @@
     parts, out_ref = refs[:4], refs[4]
     lane = iota((RESP, 128), 1)
     row, col = iota((128, 128), 0), iota((128, 128), 1)
-    order = jnp.where(row == by_xl(col), 1.0, 0.0).astype(BF16)
+    order = jnp.where(row == by_device(col), 1.0, 0.0).astype(BF16)
     extras = [part[:, 256:].astype(F32) for part in parts]
     for h in range(2):
         head = slice(h * HEAD_DIM, (h + 1) * HEAD_DIM)
@@ -362,25 +373,25 @@
 
 
 def z_of(i, info):
-    return (4 * info[CORE_AT] + 2 * (info[Y_AT] % 2)) ^ i
-
-
-def project_own_kernel(own_ref, *refs):
-    weights, out_ref = refs[:4], refs[4]
+    return (4 * info[CORE_AT]) ^ i
+
+
+def project_own_kernel(info_ref, own_ref, weight_ref, out_ref):
     for i in range(8):
-        out_ref[i] = dot(own_ref[...], weights[i // 2][:, pl.ds((i % 2) * BLOCK, BLOCK)])
-
-
-def project_own(own, weights):
+        at = (2 * z_of(i, info_ref) + info_ref[XL_AT]) * BLOCK
+        out_ref[i] = dot(own_ref[...], weight_ref[:, pl.ds(pl.multiple_of(at, BLOCK), BLOCK)])
+
+
+def project_own(info, own, weight):
     vmem = pl.BlockSpec(memory_space=pltpu.VMEM)
     return pl.pallas_call(
         project_own_kernel,
-        in_specs=[vmem] * 5,
+        in_specs=[pl.BlockSpec(memory_space=pltpu.SMEM)] + [vmem] * 2,
         out_shape=jax.ShapeDtypeStruct((8, RESP, BLOCK), F32),
         compiler_params=params(SMALL),
         cost_estimate=LONG,
         name="project_own",
-    )(own, *weights)
+    )(info, own, weight)
 
 
 def project_kernel(info_ref, started_ref, other_ref, *refs):
@@ -401,28 +412,22 @@
     )(info, started, other, *cross)
 
 
-def pick_kernel(info_ref, weight_ref, *refs):
-    own_refs, sent_ref = refs[:4], refs[4]
-
-    def columns(i, x):
-        at = (2 * z_of(i, info_ref) + x) * BLOCK
-        return weight_ref[:, pl.ds(pl.multiple_of(at, BLOCK), BLOCK)]
-
-    xl = info_ref[XL_AT]
-    for i in range(8):
-        own_refs[i // 2][:, (i % 2) * BLOCK : (i % 2) * BLOCK + BLOCK] = columns(i, xl)
-    for i in range(2):
-        sent_ref[:, i * BLOCK : (i + 1) * BLOCK] = columns(i, 1 - xl)
-
-
-def pick_columns(info, weight):
+def pick_kernel(info_ref, weight_ref, after_ref, *out_refs):
+    for i in range(4):
+        at = (2 * z_of(i, info_ref) + 1 - info_ref[XL_AT]) * BLOCK
+        columns = weight_ref[:, pl.ds(pl.multiple_of(at, BLOCK), BLOCK)]
+        out_refs[i // 2][:, (i % 2) * BLOCK : (i % 2) * BLOCK + BLOCK] = columns
+
+
+def pick_columns(info, weight, after):
+    vmem = pl.BlockSpec(memory_space=pltpu.VMEM)
     return pl.pallas_call(
         pick_kernel,
-        in_specs=[pl.BlockSpec(memory_space=pltpu.SMEM), pl.BlockSpec(memory_space=pltpu.VMEM)],
-        out_shape=(jax.ShapeDtypeStruct((256, 2 * BLOCK), BF16),) * 5,
+        in_specs=[pl.BlockSpec(memory_space=pltpu.SMEM)] + [vmem] * 2,
+        out_shape=(jax.ShapeDtypeStruct((256, 2 * BLOCK), BF16),) * 2,
         compiler_params=params(SMALL),
         name="pick_columns",
-    )(info, weight)
+    )(info, weight, after)
 
 
 def swap(values, axis):
@@ -446,15 +451,16 @@
     gain = norm_gain.astype(F32).reshape(16, 1, BLOCK)
 
     row = jnp.arange(ROWS + RESP, dtype=jnp.int32)[:, None]
+    lane = jnp.arange(HEAD_DIM, dtype=jnp.int32)[None, :]
+    sample_of = sample - core + (lane >> 6)
     positions = jnp.where(
         row < 128,
-        sample * PROMPT_ROWS + half * 128 + row,
+        sample_of * PROMPT_ROWS + half * 128 + row,
         jnp.where(row < ROWS, length + half * 32 + row - 128, length + row - ROWS),
     )
-    lane = jnp.arange(HEAD_DIM, dtype=jnp.int32)[None, :]
-    entry = ((lane >> 3) * 2 + xl) * 8 + (lane & 7)
+    entry = (2 * ((lane >> 2) & 7) + xl) * 8 + 4 * core + (lane & 3)
     entry = jnp.where(row < ROWS, entry, lane)
-    still = (row < ROWS) & (lane >= HALF)
+    still = (row < ROWS) & ((lane & 32) > 0)
     inverse = ROPE_BASE ** (-((entry % HALF).astype(F32) * 2.0 / HEAD_DIM))
     angles = jnp.where(still, 0.0, positions.astype(F32) * inverse)
     trig = jnp.stack([jnp.cos(angles), jnp.sin(angles) * jnp.where(entry < HALF, -1.0, 1.0)])
@@ -468,18 +474,16 @@
     got = swap(packed, ZRING)
     scaled = scale_rows(info, prompt_hidden, response_hidden, gain)
     beside = lax.ppermute(scaled, "xl", flip)
-    *own, sent = pick_columns(info, output_weight)
-    first = lax.ppermute(sent, "xl", flip)
-    weights, own_hidden = split(got, (beside, sent))
-    other_weights = lax.ppermute(weights, "core", flip)
-    products = partial_products(jnp.stack([core, xl]), weights, scaled, beside)
-    products = partial_products(jnp.stack([1 - core, xl]), other_weights, scaled, beside, products, first)
+    crossed = lax.ppermute(scaled, "core", flip), lax.ppermute(beside, "core", flip)
+    sent = pick_columns(info, output_weight, scaled)
+    early, late = (lax.ppermute(piece, "xl", flip) for piece in sent)
+    own_hidden = split(got, (*crossed, early, sent[1], trig))
+    other_hidden = lax.ppermute(own_hidden, "xl", flip)
+    products = partial_products(info, got, (scaled, beside, *crossed))
     products = swap(products, ZRING)
-    other_hidden = lax.ppermute(own_hidden, "xl", flip)
-    second = lax.ppermute(first, "y", [(i, i ^ 1) for i in range(4)])
     queries = queries_of(info, gain, query_weight, trig, own_hidden, other_hidden)
-    cross = (first, second, lax.ppermute(first, "core", flip), lax.ppermute(second, "core", flip))
-    rows = finish_keys(products, trig, queries, second)
+    cross = (early, late, lax.ppermute(early, "core", flip), lax.ppermute(late, "core", flip))
+    rows = finish_keys(products, trig, queries)
     rows = swap(rows, KEY_GROUP)
 
     def along(values, step):
@@ -489,7 +493,7 @@
     parts = attend(info, rows, pooled)
     attention = merge([parts[0]] + [along(parts[step], -step) for step in (1, 2, 3)])
     partner = lax.ppermute(attention, "xl", flip)
-    partial = project(info, project_own(attention, own), partner, cross)
+    partial = project(info, project_own(info, attention, output_weight), partner, cross)
     summed = jnp.sum(swap(partial, ZRING).astype(F32), axis=0)
     live = jnp.arange(RESP, dtype=jnp.int32) < response_lengths[0]
     return jnp.where(live[:, None], summed, 0.0).astype(BF16)

time: 119 us -> 117 us (0.983)
  local copies, waits for them, and re-layouts: 8.94 us -> 6.66 us
  starting transfers between devices: 37.1 us -> 35.7 us
    all_to_all x4, waiting for transfers between devices: 38.4 us -> 24.3 us  [swap(): return lax.all_to_all(values, axis, 0, 0, tiled=False)]
    ppermute x5 -> x6, waiting for transfers between devices: 0.01 us -> 10.6 us  [the longest x2 10.6 us: body(): early, late = (lax.ppermute(piece, 'xl', flip) for piece in sent)]
    ppermute x1, waiting for transfers between devices: 5.11 us -> 7.67 us  [body(): other_hidden = lax.ppermute(own_hidden, 'xl', flip)]
    unnamed x22 -> x12, local copies, waits for them, and re-layouts: 8.85 us -> 6.57 us
    ppermute x5 -> x6, starting transfers between devices: 3.68 us -> 1.69 us  [the longest x2 1.68 us: body(): early, late = (lax.ppermute(piece, 'xl', flip) for piece in sent)]
    ppermute x1, waiting for transfers between devices: 3.5 us -> 5.39 us  [body(): beside = lax.ppermute(scaled, 'xl', flip)]
    pallas_call x3 -> x2, Pallas kernels: 3.66 us -> 3.53 us  [the longest x1 2.51 us: partial_products(): pl.pallas_call(partial_kernel, in_specs=[pl.BlockSpec(memory_space=pltpu....]
  transfers between devices with their start and end apart: 18 -> 19, of which waited for: 10 -> 12; matrix products, arithmetic and copies ran while one was open for 1% -> 1% of each run, Pallas kernels for 8% -> 10%
where the time goes in v4:
time: 117 us; the launch traced here: 116 us
  waiting for transfers between devices  53.4 us (46%)
  starting transfers between devices  35.7 us (31%)
  Pallas kernels  17.6 us (15%)
  local copies, waits for them, and re-layouts  6.66 us (6%)
  other arithmetic  1.47 us (1%)
  between operations  1.46 us (1%)
    all_to_all x4, waiting for transfers between devices, swap(): return lax.all_to_all(values, axis, 0, 0, tiled=False)  24.3 us
    all_to_all x4, starting transfers between devices, swap(): return lax.all_to_all(values, axis, 0, 0, tiled=False)  20.9 us
    ppermute x2, waiting for transfers between devices, body(): early, late = (lax.ppermute(piece, 'xl', flip) for piece in sent)  10.6 us
    ppermute x6, starting transfers between devices, along(): return lax.ppermute(values, 'y', [(i, (i + step) % 4) for i in range(4)])  10.5 us
    ppermute x1, waiting for transfers between devices, body(): other_hidden = lax.ppermute(own_hidden, 'xl', flip)  7.67 us
    unnamed x12, local copies, waits for them, and re-layouts  6.57 us
    ppermute x6, waiting for transfers between devices, along(): return lax.ppermute(values, 'y', [(i, (i + step) % 4) for i in range(4)])  5.48 us
    ppermute x1, waiting for transfers between devices, body(): beside = lax.ppermute(scaled, 'xl', flip)  5.39 us
  transfers between devices with their start and end apart: 19, of which 12 were waited for; matrix products, arithmetic and copies ran while one was open for 1% of the time, Pallas kernels for 10%

profile of v4, /device:TPU:2, one launch (start us, length us, event | category | flops | bytes accessed | tf_op | source)
XLA Modules:
  0.0 116.4 jit_solution(6394070779567162693)
XLA Ops:
  0.0 0.0 copy-start.2
  0.0 0.0 copy-start.5
  0.0 0.0 copy-start.3
  0.0 2.4 %pack.1 = bf16[8,128,512]{2,1,0:T(8,128)(2,1)} custom-call(s32[1]{0:T(128)} %bitcast.1.core_ref, bf16[32,8192]{1,0:T(8,128)(2,1)} %bitcast.15, bf16[32,8192]{1,0:T(8,128)(2,1)} %bitcast.16, bf16[64,512]{1,0:T(8,128)(2,1)} %resp_ref.1), custom_call_target="tpu_custom_call" | custom-call | tf_op jit(solution)/shard_map/pack/pallas_call | solution.py:71
  2.4 8.5 %all-to-all-start = ((bf16[8,128,512]{2,1,0:T(8,128)(2,1)}), bf16[8,128,512]{2,1,0:T(8,128)(2,1)S(1)}, u32[]{:S(2)}, u32[]{:S(2)}) async-start(bf16[8,128,512]{2,1,0:T(8,128)(2,1)} %pack.1), calls=%async_computation | async-start | bytes 2097152 | tf_op jit(solution)/shard_map/all_to_all | solution.py:434
  11.5 0.0 copy-done.5
  11.5 0.1 stack.28.info_ref
  11.6 0.0 copy-done.2
  11.6 0.0 copy-done.3
  11.6 1.0 scale_rows.1.refs_0_.after_ref
  12.6 0.6 collective-permute-start
  13.1 0.0 collective-permute-start.1
  13.1 0.0 copy-start
  13.1 2.2 %copy-done = bf16[256,8192]{1,0:T(8,128)(2,1)S(1)} copy-done((bf16[256,8192]{1,0:T(8,128)(2,1)S(1)}, bf16[256,8192]{1,0:T(8,128)(2,1)}, u32[]{:S(2)}) %copy-start) | copy-done | bytes 4194328
  15.3 1.4 %pick_columns.1 = (bf16[256,1024]{1,0:T(8,128)(2,1)}, bf16[256,1024]{1,0:T(8,128)(2,1)S(1)}) custom-call(s32[6]{0:T(128)S(1)} %stack.28.info_ref, bf16[256,8192]{1,0:T(8,128)(2,1)S(1)} %copy-done, bf16[336,512]{1,0:T(8,128)(2,1)S(1)} %scale_rows.1.refs_0_.after_ref), custom_call_target="tpu_custom_call" | custom-call | tf_op jit(solution)/shard_map/pick_columns/pallas_call | solution.py:424
  16.8 1.5 %collective-permute-start.3 = (bf16[256,1024]{1,0:T(8,128)(2,1)}, bf16[256,1024]{1,0:T(8,128)(2,1)S(1)}, u32[]{:S(2)}, u32[]{:S(2)}) collective-permute-start(bf16[256,1024]{1,0:T(8,128)(2,1)} %get-tuple-element.11), channel_id=1, source_target_pairs={{0,1},{1,0},{2,3},{3,2},{4,5},{5,4},{6,7},{7,6},{8,9},{9,8},{10,11... | collective-permute-start | bytes 1572872 | tf_op jit(solution)/shard_map/ppermute | solution.py:479
  18.3 5.4 %collective-permute-done.refs_1_ = bf16[336,512]{1,0:T(8,128)(2,1)} collective-permute-done((bf16[336,512]{1,0:T(8,128)(2,1)S(1)}, bf16[336,512]{1,0:T(8,128)(2,1)}, u32[]{:S(2)}, u32[]{:S(2)}) %collective-permute-start) | collective-permute-done | bytes 344096 | tf_op jit(solution)/shard_map/ppermute | solution.py:476
  23.7 0.0 collective-permute-start.2
  23.7 0.6 fusion.11
  24.4 0.0 collective-permute-done.1.refs_2_.refs_0_
  24.4 9.0 %collective-permute-done.3.refs_2_.refs_0_ = bf16[256,1024]{1,0:T(8,128)(2,1)S(1)} collective-permute-done((bf16[256,1024]{1,0:T(8,128)(2,1)}, bf16[256,1024]{1,0:T(8,128)(2,1)S(1)}, u32[]{:S(2)}, u32[]{:S(2)}) %collective-permute-start.3) | collective-permute-done | bytes 524320 | tf_op jit(solution)/shard_map/ppermute | solution.py:479
  33.4 0.0 collective-permute-done.2.refs_3_.refs_1_
  33.4 6.2 %all-to-all-done.got_ref = bf16[8,128,512]{2,1,0:T(8,128)(2,1)S(1)} async-done(((bf16[8,128,512]{2,1,0:T(8,128)(2,1)}), bf16[8,128,512]{2,1,0:T(8,128)(2,1)S(1)}, u32[]{:S(2)}, u32[]{:S(2)}) %all-to-all-start) | async-done | bytes 1048608 | tf_op jit(solution)/shard_map/all_to_all | solution.py:434
  39.6 0.8 split.1.own_ref
  40.4 0.5 collective-permute-start.4
  41.0 2.5 %partial_products.1 = bf16[8,176,128]{2,1,0:T(8,128)(2,1)} custom-call(s32[6]{0:T(128)S(1)} %stack.28.info_ref, bf16[8,128,512]{2,1,0:T(8,128)(2,1)S(1)} %all-to-all-done.got_ref, bf16[336,512]{1,0:T(8,128)(2,1)S(1)} %scale_rows.1.refs_0_.after_ref, bf16[336,512]{1,0:T(8,128)(2,1)} %collective-permute-done.refs_1_, ...), custom_call_target="tpu_custom_call" | custom-call | tf_op jit(solution)/shard_map/partial_products/pallas_call | solution.py:166
  43.5 3.4 %all-to-all-start.1 = ((bf16[8,176,128]{2,1,0:T(8,128)(2,1)}), bf16[8,176,128]{2,1,0:T(8,128)(2,1)S(1)}, u32[]{:S(2)}, u32[]{:S(2)}) async-start(bf16[8,176,128]{2,1,0:T(8,128)(2,1)} %partial_products.1), calls=%async_computation.1 | async-start | bytes 720896 | tf_op jit(solution)/shard_map/all_to_all | solution.py:434
  46.9 7.7 %collective-permute-done.4.other_ref = bf16[8,64,512]{2,1,0:T(8,128)(2,1)} collective-permute-done((bf16[8,64,512]{2,1,0:T(8,128)(2,1)}, bf16[8,64,512]{2,1,0:T(8,128)(2,1)}, u32[]{:S(2)}, u32[]{:S(2)}) %collective-permute-start.4) | collective-permute-done | bytes 524320 | tf_op jit(solution)/shard_map/ppermute | solution.py:481
  54.6 0.0 copy-start.4
  54.6 2.2 %copy-done.4 = bf16[8192,256]{1,0:T(8,128)(2,1)S(1)} copy-done((bf16[8192,256]{1,0:T(8,128)(2,1)S(1)}, bf16[8192,256]{1,0:T(8,128)(2,1)}, u32[]{:S(2)}) %copy-start.4) | copy-done | bytes 4194328
  56.8 2.3 %queries.1.refs_0_ = bf16[64,256]{1,0:T(8,128)(2,1)S(1)} custom-call(s32[6]{0:T(128)S(1)} %stack.28.info_ref, f32[16,1,512]{2,1,0:T(1,128)S(1)} %bitcast.14, f32[2,224,128]{2,1,0:T(8,128)S(1)} %pad_maximum_fusion.refs_4_.trig_ref, bf16[8192,256]{1,0:T(8,128)(2,1)S(1)} %copy-done.4, bf16[8,64,512]{2,1,0:T(8,128)(2,1)} %split.1.own_ref, ...), custom_call_target="tpu_custom_call" | custom-call | flops 30000001024 | bytes 1000000 | tf_op jit(solution)/shard_map/queries/pallas_call | solution.py:249
  59.1 1.9 %all-to-all-done.1.parts_ref = bf16[8,176,128]{2,1,0:T(8,128)(2,1)S(1)} async-done(((bf16[8,176,128]{2,1,0:T(8,128)(2,1)}), bf16[8,176,128]{2,1,0:T(8,128)(2,1)S(1)}, u32[]{:S(2)}, u32[]{:S(2)}) %all-to-all-start.1) | async-done | bytes 360480 | tf_op jit(solution)/shard_map/all_to_all | solution.py:434
  61.0 1.2 %finish_keys.1 = bf16[16,144,128]{2,1,0:T(8,128)(2,1)} custom-call(bf16[8,176,128]{2,1,0:T(8,128)(2,1)S(1)} %all-to-all-done.1.parts_ref, f32[2,224,128]{2,1,0:T(8,128)S(1)} %pad_maximum_fusion.refs_4_.trig_ref, bf16[64,256]{1,0:T(8,128)(2,1)S(1)} %queries.1.refs_0_), custom_call_target="tpu_custom_call" | custom-call | flops 30000001024 | bytes 1000000 | tf_op jit(solution)/shard_map/finish_keys/pallas_call | solution.py:213
  62.2 5.5 %all-to-all-start.2 = ((bf16[16,144,128]{2,1,0:T(8,128)(2,1)}), bf16[16,144,128]{2,1,0:T(8,128)(2,1)S(1)}, u32[]{:S(2)}, u32[]{:S(2)}) async-start(bf16[16,144,128]{2,1,0:T(8,128)(2,1)} %finish_keys.1), calls=%async_computation.2 | async-start | bytes 1179648 | tf_op jit(solution)/shard_map/all_to_all | solution.py:434
  67.7 0.2 collective-permute-start.12
  67.9 1.6 %collective-permute-start.5 = (bf16[64,256]{1,0:T(8,128)(2,1)S(1)}, bf16[64,256]{1,0:T(8,128)(2,1)S(1)}, u32[]{:S(2)}, u32[]{:S(2)}) collective-permute-start(bf16[64,256]{1,0:T(8,128)(2,1)S(1)} %queries.1.refs_0_), channel_id=1, source_target_pairs={{0,32},{32,64},{64,96},{96,0},{1,33},{33,65},{65,97},{97,1},{2,34}... | collective-permute-start | bytes 98312 | tf_op jit(solution)/shard_map/ppermute | solution.py:490
  69.5 2.9 %collective-permute-start.6 = (bf16[64,256]{1,0:T(8,128)(2,1)S(1)}, bf16[64,256]{1,0:T(8,128)(2,1)S(1)}, u32[]{:S(2)}, u32[]{:S(2)}) collective-permute-start(bf16[64,256]{1,0:T(8,128)(2,1)S(1)} %queries.1.refs_0_), channel_id=1, source_target_pairs={{0,64},{32,96},{64,0},{96,32},{1,65},{33,97},{65,1},{97,33},{2,66}... | collective-permute-start | bytes 98312 | tf_op jit(solution)/shard_map/ppermute | solution.py:490
  72.4 1.3 %collective-permute-start.7 = (bf16[64,256]{1,0:T(8,128)(2,1)S(1)}, bf16[64,256]{1,0:T(8,128)(2,1)S(1)}, u32[]{:S(2)}, u32[]{:S(2)}) collective-permute-start(bf16[64,256]{1,0:T(8,128)(2,1)S(1)} %queries.1.refs_0_), channel_id=1, source_target_pairs={{0,96},{32,0},{64,32},{96,64},{1,97},{33,1},{65,33},{97,65},{2,98}... | collective-permute-start | bytes 98312 | tf_op jit(solution)/shard_map/ppermute | solution.py:490
  73.8 0.0 collective-permute-done.5.refs_1_
  73.8 1.2 %collective-permute-done.6.refs_2_ = bf16[64,256]{1,0:T(8,128)(2,1)S(1)} collective-permute-done((bf16[64,256]{1,0:T(8,128)(2,1)S(1)}, bf16[64,256]{1,0:T(8,128)(2,1)S(1)}, u32[]{:S(2)}, u32[]{:S(2)}) %collective-permute-start.6) | collective-permute-done | bytes 32800 | tf_op jit(solution)/shard_map/ppermute | solution.py:490
  74.9 1.4 %collective-permute-done.7.refs_3_ = bf16[64,256]{1,0:T(8,128)(2,1)S(1)} collective-permute-done((bf16[64,256]{1,0:T(8,128)(2,1)S(1)}, bf16[64,256]{1,0:T(8,128)(2,1)S(1)}, u32[]{:S(2)}, u32[]{:S(2)}) %collective-permute-start.7) | collective-permute-done | bytes 32800 | tf_op jit(solution)/shard_map/ppermute | solution.py:490
  76.3 1.5 %all-to-all-done.2.rows_ref = bf16[16,144,128]{2,1,0:T(8,128)(2,1)S(1)} async-done(((bf16[16,144,128]{2,1,0:T(8,128)(2,1)}), bf16[16,144,128]{2,1,0:T(8,128)(2,1)S(1)}, u32[]{:S(2)}, u32[]{:S(2)}) %all-to-all-start.2) | async-done | bytes 589856 | tf_op jit(solution)/shard_map/all_to_all | solution.py:434
  77.8 2.8 %attend.1 = (bf16[64,384]{1,0:T(8,128)(2,1)S(1)}, bf16[64,384]{1,0:T(8,128)(2,1)S(1)}, bf16[64,384]{1,0:T(8,128)(2,1)S(1)}, bf16[64,384]{1,0:T(8,128)(2,1)S(1)}) custom-call(s32[6]{0:T(128)S(1)} %stack.28.info_ref, bf16[16,144,128]{2,1,0:T(8,128)(2,1)S(1)} %all-to-all-done.2.rows_ref, bf16[64,256]{1,0:T(8,128)(2,1)S(1)} %queries.1.refs_0_, ...), custom_call_target="tpu_custom_call" | custom-call | tf_op jit(solution)/shard_map/attend/pallas_call | solution.py:337
  80.6 3.1 %collective-permute-start.8 = (bf16[64,384]{1,0:T(8,128)(2,1)S(1)}, bf16[64,384]{1,0:T(8,128)(2,1)S(1)}, u32[]{:S(2)}, u32[]{:S(2)}) collective-permute-start(bf16[64,384]{1,0:T(8,128)(2,1)S(1)} %get-tuple-element.14), channel_id=1, source_target_pairs={{0,96},{32,0},{64,32},{96,64},{1,97},{33,1},{65,33},{97,65},{2,98}... | collective-permute-start | bytes 147464 | tf_op jit(solution)/shard_map/ppermute | solution.py:490
  83.7 0.6 collective-permute-start.9
  84.3 1.0 collective-permute-start.10
  85.3 0.0 collective-permute-start.13
  85.3 1.6 %collective-permute-done.12.refs_1_ = bf16[256,1024]{1,0:T(8,128)(2,1)S(1)} collective-permute-done((bf16[256,1024]{1,0:T(8,128)(2,1)S(1)}, bf16[256,1024]{1,0:T(8,128)(2,1)S(1)}, u32[]{:S(2)}, u32[]{:S(2)}) %collective-permute-start.12) | collective-permute-done | bytes 524320 | tf_op jit(solution)/shard_map/ppermute | solution.py:479
  86.9 0.0 collective-permute-start.14
  86.9 0.0 collective-permute-done.8.refs_1_
  86.9 2.4 %collective-permute-done.9.refs_2_ = bf16[64,384]{1,0:T(8,128)(2,1)S(1)} collective-permute-done((bf16[64,384]{1,0:T(8,128)(2,1)S(1)}, bf16[64,384]{1,0:T(8,128)(2,1)S(1)}, u32[]{:S(2)}, u32[]{:S(2)}) %collective-permute-start.9) | collective-permute-done | bytes 49184 | tf_op jit(solution)/shard_map/ppermute | solution.py:490
  89.3 0.5 collective-permute-done.10.refs_3_
  89.8 0.3 merge.1.own_ref
  90.1 1.5 %collective-permute-start.11 = (bf16[64,256]{1,0:T(8,128)(2,1)S(1)}, bf16[64,256]{1,0:T(8,128)(2,1)S(1)}, u32[]{:S(2)}, u32[]{:S(2)}) collective-permute-start(bf16[64,256]{1,0:T(8,128)(2,1)S(1)} %merge.1.own_ref), channel_id=1, source_target_pairs={{0,1},{1,0},{2,3},{3,2},{4,5},{5,4},{6,7},{7,6},{8,9},{9,8},{10,11... | collective-permute-start | bytes 98312 | tf_op jit(solution)/shard_map/ppermute | solution.py:495
  91.7 2.2 %copy-done.1 = bf16[256,8192]{1,0:T(8,128)(2,1)S(1)} copy-done((bf16[256,8192]{1,0:T(8,128)(2,1)S(1)}, bf16[256,8192]{1,0:T(8,128)(2,1)}, u32[]{:S(2)}) %copy-start.1) | copy-done | bytes 4194328
  93.8 1.0 project_own.1.started_ref
  94.9 0.0 collective-permute-done.13.refs_2_
  94.9 0.0 collective-permute-done.14.refs_3_
  94.9 0.0 collective-permute-done.11.other_ref
  94.9 1.8 %project.1 = bf16[8,64,512]{2,1,0:T(8,128)(2,1)} custom-call(s32[6]{0:T(128)S(1)} %stack.28.info_ref, f32[8,64,512]{2,1,0:T(8,128)S(1)} %project_own.1.started_ref, bf16[64,256]{1,0:T(8,128)(2,1)S(1)} %collective-permute-done.11.other_ref, bf16[256,1024]{1,0:T(8,128)(2,1)S(1)} %collective-permute-done.3.refs_2_.refs_0_, ...), custom_call_target="tpu_custom_call" | custom-call | tf_op jit(solution)/shard_map/project/pallas_call | solution.py:406
  96.7 3.5 %all-to-all-start.3 = ((bf16[8,64,512]{2,1,0:T(8,128)(2,1)}), bf16[8,64,512]{2,1,0:T(8,128)(2,1)S(1)}, u32[]{:S(2)}, u32[]{:S(2)}) async-start(bf16[8,64,512]{2,1,0:T(8,128)(2,1)} %project.1), calls=%async_computation.3 | async-start | bytes 1048576 | tf_op jit(solution)/shard_map/all_to_all | solution.py:434
  100.9 14.7 %all-to-all-done.3 = bf16[8,64,512]{2,1,0:T(8,128)(2,1)S(1)} async-done(((bf16[8,64,512]{2,1,0:T(8,128)(2,1)}), bf16[8,64,512]{2,1,0:T(8,128)(2,1)S(1)}, u32[]{:S(2)}, u32[]{:S(2)}) %all-to-all-start.3) | async-done | bytes 524320 | tf_op jit(solution)/shard_map/all_to_all | solution.py:434
  115.6 0.1 convert_reduce_fusion
  115.7 0.7 select_convert_fusion
  (8 shorter events, 0.1 us)
Async XLA Ops:
  0.0 11.6 %copy-start.2 = (bf16[64,512]{1,0:T(8,128)(2,1)S(1)}, bf16[64,512]{1,0:T(8,128)(2,1)}, u32[]{:S(2)}) copy-start(bf16[64,512]{1,0:T(8,128)(2,1)} %resp_ref.1) | copy-start | bytes 196612
  0.0 11.5 %copy-start.5 = (bf16[8192]{0:T(1024)(128)(2,1)S(1)}, bf16[8192]{0:T(1024)(128)(2,1)}, u32[]{:S(2)}) copy-start(bf16[8192]{0:T(1024)(128)(2,1)} %param.11) | copy-start | bytes 49156
  0.0 11.6 %copy-start.3 = (bf16[256,512]{1,0:T(8,128)(2,1)S(1)}, bf16[256,512]{1,0:T(8,128)(2,1)}, u32[]{:S(2)}) copy-start(bf16[256,512]{1,0:T(8,128)(2,1)} %prompt_ref.1) | copy-start | bytes 786436
  2.4 37.2 %all-to-all-start = ((bf16[8,128,512]{2,1,0:T(8,128)(2,1)}), bf16[8,128,512]{2,1,0:T(8,128)(2,1)S(1)}, u32[]{:S(2)}, u32[]{:S(2)}) async-start(bf16[8,128,512]{2,1,0:T(8,128)(2,1)} %pack.1), calls=%async_computation | async-start | bytes 2097152 | tf_op jit(solution)/shard_map/all_to_all | solution.py:434
  12.6 11.1 %collective-permute-start = (bf16[336,512]{1,0:T(8,128)(2,1)S(1)}, bf16[336,512]{1,0:T(8,128)(2,1)}, u32[]{:S(2)}, u32[]{:S(2)}) collective-permute-start(bf16[336,512]{1,0:T(8,128)(2,1)S(1)} %scale_rows.1.refs_0_.after_ref), channel_id=1, source_target_pairs={{0,1},{1,0},{2,3},{3,2},{4,5},{5,4},{6,7},{7,6},{8,9},{9,8},{10,11... | collective-permute-start | bytes 1032200 | tf_op jit(solution)/shard_map/ppermute | solution.py:476
  13.1 11.2 %collective-permute-start.1 = (bf16[336,512]{1,0:T(8,128)(2,1)S(1)}, bf16[336,512]{1,0:T(8,128)(2,1)S(1)}, u32[]{:S(2)}, u32[]{:S(2)}) collective-permute-start(bf16[336,512]{1,0:T(8,128)(2,1)S(1)} %scale_rows.1.refs_0_.after_ref), channel_id=1, source_target_pairs={{0,16},{16,0},{1,17},{17,1},{2,18},{18,2},{3,19},{19,3},{4,20},{20... | collective-permute-start | bytes 1032200 | tf_op jit(solution)/shard_map/ppermute | solution.py:477
  13.1 2.2 %copy-start = (bf16[256,8192]{1,0:T(8,128)(2,1)S(1)}, bf16[256,8192]{1,0:T(8,128)(2,1)}, u32[]{:S(2)}) copy-start(bf16[256,8192]{1,0:T(8,128)(2,1)} %weight_ref.5) | copy-start | bytes 12582916
  16.8 16.6 %collective-permute-start.3 = (bf16[256,1024]{1,0:T(8,128)(2,1)}, bf16[256,1024]{1,0:T(8,128)(2,1)S(1)}, u32[]{:S(2)}, u32[]{:S(2)}) collective-permute-start(bf16[256,1024]{1,0:T(8,128)(2,1)} %get-tuple-element.11), channel_id=1, source_target_pairs={{0,1},{1,0},{2,3},{3,2},{4,5},{5,4},{6,7},{7,6},{8,9},{9,8},{10,11... | collective-permute-start | bytes 1572872 | tf_op jit(solution)/shard_map/ppermute | solution.py:479
  23.7 9.7 %collective-permute-start.2 = (bf16[336,512]{1,0:T(8,128)(2,1)}, bf16[336,512]{1,0:T(8,128)(2,1)S(1)}, u32[]{:S(2)}, u32[]{:S(2)}) collective-permute-start(bf16[336,512]{1,0:T(8,128)(2,1)} %collective-permute-done.refs_1_), channel_id=1, source_target_pairs={{0,16},{16,0},{1,17},{17,1},{2,18},{18,2},{3,19},{19,3},{4,20},{20... | collective-permute-start | bytes 1032200 | tf_op jit(solution)/shard_map/ppermute | solution.py:477
  40.4 14.2 %collective-permute-start.4 = (bf16[8,64,512]{2,1,0:T(8,128)(2,1)}, bf16[8,64,512]{2,1,0:T(8,128)(2,1)}, u32[]{:S(2)}, u32[]{:S(2)}) collective-permute-start(bf16[8,64,512]{2,1,0:T(8,128)(2,1)} %split.1.own_ref), channel_id=1, source_target_pairs={{0,1},{1,0},{2,3},{3,2},{4,5},{5,4},{6,7},{7,6},{8,9},{9,8},{10,11... | collective-permute-start | bytes 1572872 | tf_op jit(solution)/shard_map/ppermute | solution.py:481
  43.5 17.5 %all-to-all-start.1 = ((bf16[8,176,128]{2,1,0:T(8,128)(2,1)}), bf16[8,176,128]{2,1,0:T(8,128)(2,1)S(1)}, u32[]{:S(2)}, u32[]{:S(2)}) async-start(bf16[8,176,128]{2,1,0:T(8,128)(2,1)} %partial_products.1), calls=%async_computation.1 | async-start | bytes 720896 | tf_op jit(solution)/shard_map/all_to_all | solution.py:434
  54.6 2.2 %copy-start.4 = (bf16[8192,256]{1,0:T(8,128)(2,1)S(1)}, bf16[8192,256]{1,0:T(8,128)(2,1)}, u32[]{:S(2)}) copy-start(bf16[8192,256]{1,0:T(8,128)(2,1)} %weight_ref.4) | copy-start | bytes 12582916
  62.2 15.6 %all-to-all-start.2 = ((bf16[16,144,128]{2,1,0:T(8,128)(2,1)}), bf16[16,144,128]{2,1,0:T(8,128)(2,1)S(1)}, u32[]{:S(2)}, u32[]{:S(2)}) async-start(bf16[16,144,128]{2,1,0:T(8,128)(2,1)} %finish_keys.1), calls=%async_computation.2 | async-start | bytes 1179648 | tf_op jit(solution)/shard_map/all_to_all | solution.py:434
  67.7 19.2 %collective-permute-start.12 = (bf16[256,1024]{1,0:T(8,128)(2,1)S(1)}, bf16[256,1024]{1,0:T(8,128)(2,1)S(1)}, u32[]{:S(2)}, u32[]{:S(2)}) collective-permute-start(bf16[256,1024]{1,0:T(8,128)(2,1)S(1)} %get-tuple-element.12.refs_3_), channel_id=1, source_target_pairs={{0,1},{1,0},{2,3},{3,2},{4,5},{5,4},{6,7},{7,6},{8,9},{9,8},{10,11... | collective-permute-start | bytes 1572872 | tf_op jit(solution)/shard_map/ppermute | solution.py:479
  67.9 5.8 %collective-permute-start.5 = (bf16[64,256]{1,0:T(8,128)(2,1)S(1)}, bf16[64,256]{1,0:T(8,128)(2,1)S(1)}, u32[]{:S(2)}, u32[]{:S(2)}) collective-permute-start(bf16[64,256]{1,0:T(8,128)(2,1)S(1)} %queries.1.refs_0_), channel_id=1, source_target_pairs={{0,32},{32,64},{64,96},{96,0},{1,33},{33,65},{65,97},{97,1},{2,34}... | collective-permute-start | bytes 98312 | tf_op jit(solution)/shard_map/ppermute | solution.py:490
  69.5 5.4 %collective-permute-start.6 = (bf16[64,256]{1,0:T(8,128)(2,1)S(1)}, bf16[64,256]{1,0:T(8,128)(2,1)S(1)}, u32[]{:S(2)}, u32[]{:S(2)}) collective-permute-start(bf16[64,256]{1,0:T(8,128)(2,1)S(1)} %queries.1.refs_0_), channel_id=1, source_target_pairs={{0,64},{32,96},{64,0},{96,32},{1,65},{33,97},{65,1},{97,33},{2,66}... | collective-permute-start | bytes 98312 | tf_op jit(solution)/shard_map/ppermute | solution.py:490
  72.4 3.9 %collective-permute-start.7 = (bf16[64,256]{1,0:T(8,128)(2,1)S(1)}, bf16[64,256]{1,0:T(8,128)(2,1)S(1)}, u32[]{:S(2)}, u32[]{:S(2)}) collective-permute-start(bf16[64,256]{1,0:T(8,128)(2,1)S(1)} %queries.1.refs_0_), channel_id=1, source_target_pairs={{0,96},{32,0},{64,32},{96,64},{1,97},{33,1},{65,33},{97,65},{2,98}... | collective-permute-start | bytes 98312 | tf_op jit(solution)/shard_map/ppermute | solution.py:490
  80.6 6.3 %collective-permute-start.8 = (bf16[64,384]{1,0:T(8,128)(2,1)S(1)}, bf16[64,384]{1,0:T(8,128)(2,1)S(1)}, u32[]{:S(2)}, u32[]{:S(2)}) collective-permute-start(bf16[64,384]{1,0:T(8,128)(2,1)S(1)} %get-tuple-element.14), channel_id=1, source_target_pairs={{0,96},{32,0},{64,32},{96,64},{1,97},{33,1},{65,33},{97,65},{2,98}... | collective-permute-start | bytes 147464 | tf_op jit(solution)/shard_map/ppermute | solution.py:490
  83.7 5.6 %collective-permute-start.9 = (bf16[64,384]{1,0:T(8,128)(2,1)S(1)}, bf16[64,384]{1,0:T(8,128)(2,1)S(1)}, u32[]{:S(2)}, u32[]{:S(2)}) collective-permute-start(bf16[64,384]{1,0:T(8,128)(2,1)S(1)} %get-tuple-element.15), channel_id=1, source_target_pairs={{0,64},{32,96},{64,0},{96,32},{1,65},{33,97},{65,1},{97,33},{2,66}... | collective-permute-start | bytes 147464 | tf_op jit(solution)/shard_map/ppermute | solution.py:490
  84.3 5.5 %collective-permute-start.10 = (bf16[64,384]{1,0:T(8,128)(2,1)S(1)}, bf16[64,384]{1,0:T(8,128)(2,1)S(1)}, u32[]{:S(2)}, u32[]{:S(2)}) collective-permute-start(bf16[64,384]{1,0:T(8,128)(2,1)S(1)} %get-tuple-element.16), channel_id=1, source_target_pairs={{0,32},{32,64},{64,96},{96,0},{1,33},{33,65},{65,97},{97,1},{2,34}... | collective-permute-start | bytes 147464 | tf_op jit(solution)/shard_map/ppermute | solution.py:490
  85.3 9.6 %collective-permute-start.13 = (bf16[256,1024]{1,0:T(8,128)(2,1)S(1)}, bf16[256,1024]{1,0:T(8,128)(2,1)S(1)}, u32[]{:S(2)}, u32[]{:S(2)}) collective-permute-start(bf16[256,1024]{1,0:T(8,128)(2,1)S(1)} %collective-permute-done.3.refs_2_.refs_0_), channel_id=1, source_target_pairs={{0,16},{16,0},{1,17},{17,1},{2,18},{18,2},{3,19},{19,3},{4,20},{20... | collective-permute-start | bytes 1572872 | tf_op jit(solution)/shard_map/ppermute | solution.py:485
  86.9 8.0 %collective-permute-start.14 = (bf16[256,1024]{1,0:T(8,128)(2,1)S(1)}, bf16[256,1024]{1,0:T(8,128)(2,1)S(1)}, u32[]{:S(2)}, u32[]{:S(2)}) collective-permute-start(bf16[256,1024]{1,0:T(8,128)(2,1)S(1)} %collective-permute-done.12.refs_1_), channel_id=1, source_target_pairs={{0,16},{16,0},{1,17},{17,1},{2,18},{18,2},{3,19},{19,3},{4,20},{20... | collective-permute-start | bytes 1572872 | tf_op jit(solution)/shard_map/ppermute | solution.py:485
  90.1 4.8 %collective-permute-start.11 = (bf16[64,256]{1,0:T(8,128)(2,1)S(1)}, bf16[64,256]{1,0:T(8,128)(2,1)S(1)}, u32[]{:S(2)}, u32[]{:S(2)}) collective-permute-start(bf16[64,256]{1,0:T(8,128)(2,1)S(1)} %merge.1.own_ref), channel_id=1, source_target_pairs={{0,1},{1,0},{2,3},{3,2},{4,5},{5,4},{6,7},{7,6},{8,9},{9,8},{10,11... | collective-permute-start | bytes 98312 | tf_op jit(solution)/shard_map/ppermute | solution.py:495
  91.6 2.2 %copy-start.1 = (bf16[256,8192]{1,0:T(8,128)(2,1)S(1)}, bf16[256,8192]{1,0:T(8,128)(2,1)}, u32[]{:S(2)}) copy-start(bf16[256,8192]{1,0:T(8,128)(2,1)} %weight_ref.5) | copy-start | bytes 12582916
  96.7 18.9 %all-to-all-start.3 = ((bf16[8,64,512]{2,1,0:T(8,128)(2,1)}), bf16[8,64,512]{2,1,0:T(8,128)(2,1)S(1)}, u32[]{:S(2)}, u32[]{:S(2)}) async-start(bf16[8,64,512]{2,1,0:T(8,128)(2,1)} %project.1), calls=%async_computation.3 | async-start | bytes 1048576 | tf_op jit(solution)/shard_map/all_to_all | solution.py:434

commit v5 on v4

--- a/solution.py
+++ b/solution.py
@@ -54,30 +54,26 @@
 
 
 def pack_kernel(core_ref, key_ref, value_ref, hidden_ref, out_ref):
-    row, col = iota((32, 64), 0), iota((32, 64), 1)
-    source = ((row >> 2) & 1) * 32 + (4 * core_ref[0] + (row & 3)) * 4 + (row >> 3)
-    pick = jnp.where(col == source, 1.0, 0.0).astype(BF16)
-    both = jnp.concatenate([key_ref[...], value_ref[...]], axis=0)
     for i in range(out_ref.shape[0]):
         for x in range(2):
             at = (2 * i + x) * BLOCK
-            out_ref[i, 32 * x : 32 * x + 32] = dot(pick, both[:, at : at + BLOCK]).astype(BF16)
+            out_ref[i, 32 * x : 32 * x + 16] = key_ref[:, at : at + BLOCK]
+            out_ref[i, 32 * x + 16 : 32 * x + 32] = value_ref[:, at : at + BLOCK]
         out_ref[i, 64:] = hidden_ref[...]
 
 
 def pack(core, key_rows, value_rows, hidden):
     steps = 2
     each = 8 // steps
+    rows = pl.BlockSpec((16, 2 * each * BLOCK), lambda i, core: (core[0], i))
     return pl.pallas_call(
         pack_kernel,
-        grid=(steps,),
-        in_specs=[
-            pl.BlockSpec(memory_space=pltpu.SMEM),
-            pl.BlockSpec((32, 2 * each * BLOCK), lambda i: (0, i)),
-            pl.BlockSpec((32, 2 * each * BLOCK), lambda i: (0, i)),
-            pl.BlockSpec((RESP, BLOCK), lambda i: (0, 0)),
-        ],
-        out_specs=pl.BlockSpec((each, PACKED, BLOCK), lambda i: (i, 0, 0)),
+        grid_spec=pltpu.PrefetchScalarGridSpec(
+            num_scalar_prefetch=1,
+            grid=(steps,),
+            in_specs=[rows, rows, pl.BlockSpec((RESP, BLOCK), lambda i, core: (0, 0))],
+            out_specs=pl.BlockSpec((each, PACKED, BLOCK), lambda i, core: (i, 0, 0)),
+        ),
         out_shape=jax.ShapeDtypeStruct((8, PACKED, BLOCK), BF16),
         compiler_params=params(),
         name="pack",
@@ -142,7 +138,7 @@
     xl, core = info_ref[XL_AT], info_ref[CORE_AT]
     weights = [got_ref[:, pl.ds(pl.multiple_of(32 * x, 32), 32)].reshape(256, BLOCK) for x in (xl, 1 - xl)]
     row, col = iota((256, 512), 0), iota((256, 512), 1)
-    target = ((row >> 3) & 3) * 128 + (row >> 5) * 8 + (row & 7)
+    target = (row & 3) * 128 + (row >> 5) * 8 + ((row >> 2) & 7)
     total = jnp.zeros((2 * ROWS, 512), F32)
     sums = []
     for n, at in enumerate((core, 1 - core)):
@@ -260,25 +256,25 @@
     queries, outs = refs[:4], refs[4:]
     own_y = info_ref[Y_AT]
 
-    row, col = iota((512, 512), 0), iota((512, 512), 1)
-    target = ((row >> 5) & 3) * 128 + ((row >> 7) & 1) * 64 + (row >> 8) * 32 + (row & 31)
-    pick = jnp.where(col == target, 1.0, 0.0).astype(BF16)
-
     def joined(xh, zl, at, count):
-        pieces = [rows_ref[xh * 8 + core * 4 + zl * 2 + x, at : at + count] for core in range(2) for x in range(2)]
-        return dot(jnp.concatenate(pieces, axis=1), pick).astype(BF16)
+        group = iota((count, 128), 1) >> 5
+        pieces = [
+            rows_ref[xh * 8 + core * 4 + zl * 2 + x, at : at + count].astype(F32) for x in range(2) for core in range(2)
+        ]
+        result = []
+        for g in range(4):
+            rows = pltpu.roll(pieces[0], (-32 * g) % 128, 1) if g else pieces[0]
+            for p in range(1, 4):
+                shift = (32 * (p - g)) % 128
+                rows = jnp.where(group == p, pltpu.roll(pieces[p], shift, 1) if shift else pieces[p], rows)
+            result.append(rows.astype(BF16))
+        return result
 
     prompt = [[joined(xh, zl, 0, 128) for zl in range(2)] for xh in range(2)]
 
     def prompt_rows(kv):
         return jnp.concatenate(
-            [
-                prompt[xh][zl][:, (2 * core + kv) * 128 : (2 * core + kv) * 128 + 128]
-                for xh in range(2)
-                for core in range(2)
-                for zl in range(2)
-            ],
-            axis=0,
+            [prompt[xh][zl][2 * core + kv] for xh in range(2) for core in range(2) for zl in range(2)], axis=0
         )
 
     prompt_keys, prompt_values = prompt_rows(0), prompt_rows(1)
@@ -286,9 +282,7 @@
     own = [joined(own_xh, zl, 128, 16) for zl in range(2)]
 
     def own_rows(kv):
-        return jnp.concatenate(
-            [o[:, (2 * n + kv) * 128 : (2 * n + kv) * 128 + 128] for o in own for n in range(2)], axis=0
-        )
+        return jnp.concatenate([o[2 * n + kv] for o in own for n in range(2)], axis=0)
 
     own_keys, own_values = own_rows(0), own_rows(1)
     scale = HEAD_DIM ** (-0.5)
@@ -300,35 +294,34 @@
     causal = iota((2 * RESP, RESP), 1) <= (iota((2 * RESP, RESP), 0) & (RESP - 1))
     lane = iota((RESP, 128), 1)
 
+    query = jnp.concatenate([q[:, h * HEAD_DIM : (h + 1) * HEAD_DIM] for q in queries for h in range(2)], axis=0)
+    mine = 2 * RESP
+    far = jnp.where(live, dot_t(query, prompt_keys), NEG_BIG)
+    near = jnp.where(causal, dot_t(query[:mine], own_keys), NEG_BIG)
+    top = jnp.max(far, axis=1, keepdims=True)
+    top_mine = jnp.maximum(top[:mine], jnp.max(near, axis=1, keepdims=True))
+    top = jnp.maximum(jnp.concatenate([top_mine, top[mine:]], axis=0), 0.5 * NEG_BIG)
+    far = jnp.exp2((far - top) * power)
+    near = jnp.exp2((near - top[:mine]) * power)
+    total = jnp.sum(far, axis=1, keepdims=True)
+    total = jnp.concatenate([total[:mine] + jnp.sum(near, axis=1, keepdims=True), total[mine:]], axis=0)
+    summed = dot(far.astype(BF16), prompt_values)
+    summed = jnp.concatenate([summed[:mine] + dot(near.astype(BF16), own_values), summed[mine:]], axis=0)
+    some = total > 0.0
+    safe = jnp.where(some, total, 1.0)
+    result = (summed / safe).astype(BF16)
+    level = jnp.where(some, top * scale + jnp.log(safe), NEG_BIG)
+    first = level.astype(BF16).astype(F32)
+    rest = level - first
+    second = rest.astype(BF16).astype(F32)
+    third = rest - second
     for i in range(4):
-        query = jnp.concatenate([queries[i][:, :HEAD_DIM], queries[i][:, HEAD_DIM:]], axis=0)
-        far = jnp.where(live, dot_t(query, prompt_keys), NEG_BIG)
-        top = jnp.max(far, axis=1, keepdims=True)
-        if i == 0:
-            near = jnp.where(causal, dot_t(query, own_keys), NEG_BIG)
-            top = jnp.maximum(top, jnp.max(near, axis=1, keepdims=True))
-        top = jnp.maximum(top, 0.5 * NEG_BIG)
-        far = jnp.exp2((far - top) * power)
-        total = jnp.sum(far, axis=1, keepdims=True)
-        summed = dot(far.astype(BF16), prompt_values)
-        if i == 0:
-            near = jnp.exp2((near - top) * power)
-            total += jnp.sum(near, axis=1, keepdims=True)
-            summed += dot(near.astype(BF16), own_values)
-        some = total > 0.0
-        safe = jnp.where(some, total, 1.0)
-        result = (summed / safe).astype(BF16)
-        level = jnp.where(some, top * scale + jnp.log(safe), NEG_BIG)
-        first = level.astype(BF16).astype(F32)
-        rest = level - first
-        second = rest.astype(BF16).astype(F32)
-        third = rest - second
         extra = jnp.zeros((RESP, 128), F32)
         for h in range(2):
-            mine = slice(h * RESP, (h + 1) * RESP)
-            outs[i][:, h * HEAD_DIM : (h + 1) * HEAD_DIM] = result[mine]
+            at = slice((2 * i + h) * RESP, (2 * i + h + 1) * RESP)
+            outs[i][:, h * HEAD_DIM : (h + 1) * HEAD_DIM] = result[at]
             for n, piece in enumerate((first, second, third)):
-                extra = jnp.where(lane == 3 * h + n, piece[mine], extra)
+                extra = jnp.where(lane == 3 * h + n, piece[at], extra)
         outs[i][:, 256:] = extra.astype(BF16)
 
 

time: 117 us -> 117 us (level)
  no operation moved by 1% of the time
where the time goes in v5:
time: 117 us; the launch traced here: 116 us
  waiting for transfers between devices  53.7 us (46%)
  starting transfers between devices  35.8 us (31%)
  Pallas kernels  17.1 us (15%)
  local copies, waits for them, and re-layouts  6.66 us (6%)
  other arithmetic  1.47 us (1%)
  between operations  1.46 us (1%)
    all_to_all x4, waiting for transfers between devices, swap(): return lax.all_to_all(values, axis, 0, 0, tiled=False)  24.5 us
    all_to_all x4, starting transfers between devices, swap(): return lax.all_to_all(values, axis, 0, 0, tiled=False)  20.9 us
    ppermute x2, waiting for transfers between devices, body(): early, late = (lax.ppermute(piece, 'xl', flip) for piece in sent)  10.8 us
    ppermute x6, starting transfers between devices, along(): return lax.ppermute(values, 'y', [(i, (i + step) % 4) for i in range(4)])  10.5 us
    ppermute x1, waiting for transfers between devices, body(): other_hidden = lax.ppermute(own_hidden, 'xl', flip)  7.66 us
    unnamed x12, local copies, waits for them, and re-layouts  6.57 us
    ppermute x1, waiting for transfers between devices, body(): beside = lax.ppermute(scaled, 'xl', flip)  5.39 us
    ppermute x6, waiting for transfers between devices, along(): return lax.ppermute(values, 'y', [(i, (i + step) % 4) for i in range(4)])  5.23 us
  transfers between devices with their start and end apart: 19, of which 12 were waited for; matrix products, arithmetic and copies ran while one was open for 1% of the time, Pallas kernels for 10%

profile of v5, /device:TPU:2, one launch (start us, length us, event | category | flops | bytes accessed | tf_op | source)
XLA Modules:
  0.0 116.1 jit_solution(9421824920718412059)
XLA Ops:
  0.0 0.0 copy-start.2
  0.0 0.0 copy-start.5
  0.0 0.0 copy-start.3
  0.0 2.1 %pack.1 = bf16[8,128,512]{2,1,0:T(8,128)(2,1)} custom-call(s32[1]{0:T(128)} %bitcast.1.core_ref, bf16[32,8192]{1,0:T(8,128)(2,1)} %bitcast.15, bf16[32,8192]{1,0:T(8,128)(2,1)} %bitcast.16, bf16[64,512]{1,0:T(8,128)(2,1)} %resp_ref.1), custom_call_target="tpu_custom_call" | custom-call | tf_op jit(solution)/shard_map/pack/pallas_call | solution.py:69
  2.1 8.5 %all-to-all-start = ((bf16[8,128,512]{2,1,0:T(8,128)(2,1)}), bf16[8,128,512]{2,1,0:T(8,128)(2,1)S(1)}, u32[]{:S(2)}, u32[]{:S(2)}) async-start(bf16[8,128,512]{2,1,0:T(8,128)(2,1)} %pack.1), calls=%async_computation | async-start | bytes 2097152 | tf_op jit(solution)/shard_map/all_to_all | solution.py:427
  11.2 0.0 copy-done.5
  11.2 0.1 stack.28.info_ref
  11.3 0.0 copy-done.2
  11.3 0.0 copy-done.3
  11.3 1.0 scale_rows.1.refs_0_.after_ref
  12.3 0.6 collective-permute-start
  12.8 0.0 collective-permute-start.1
  12.8 0.0 copy-start
  12.8 2.2 %copy-done = bf16[256,8192]{1,0:T(8,128)(2,1)S(1)} copy-done((bf16[256,8192]{1,0:T(8,128)(2,1)S(1)}, bf16[256,8192]{1,0:T(8,128)(2,1)}, u32[]{:S(2)}) %copy-start) | copy-done | bytes 4194328
  15.0 1.4 %pick_columns.1 = (bf16[256,1024]{1,0:T(8,128)(2,1)}, bf16[256,1024]{1,0:T(8,128)(2,1)S(1)}) custom-call(s32[6]{0:T(128)S(1)} %stack.28.info_ref, bf16[256,8192]{1,0:T(8,128)(2,1)S(1)} %copy-done, bf16[336,512]{1,0:T(8,128)(2,1)S(1)} %scale_rows.1.refs_0_.after_ref), custom_call_target="tpu_custom_call" | custom-call | tf_op jit(solution)/shard_map/pick_columns/pallas_call | solution.py:417
  16.5 1.5 %collective-permute-start.3 = (bf16[256,1024]{1,0:T(8,128)(2,1)}, bf16[256,1024]{1,0:T(8,128)(2,1)S(1)}, u32[]{:S(2)}, u32[]{:S(2)}) collective-permute-start(bf16[256,1024]{1,0:T(8,128)(2,1)} %get-tuple-element.11), channel_id=1, source_target_pairs={{0,1},{1,0},{2,3},{3,2},{4,5},{5,4},{6,7},{7,6},{8,9},{9,8},{10,11... | collective-permute-start | bytes 1572872 | tf_op jit(solution)/shard_map/ppermute | solution.py:472
  18.0 5.4 %collective-permute-done.refs_1_ = bf16[336,512]{1,0:T(8,128)(2,1)} collective-permute-done((bf16[336,512]{1,0:T(8,128)(2,1)S(1)}, bf16[336,512]{1,0:T(8,128)(2,1)}, u32[]{:S(2)}, u32[]{:S(2)}) %collective-permute-start) | collective-permute-done | bytes 344096 | tf_op jit(solution)/shard_map/ppermute | solution.py:469
  23.4 0.0 collective-permute-start.2
  23.4 0.6 fusion.11
  24.0 0.0 collective-permute-done.1.refs_2_.refs_0_
  24.1 9.0 %collective-permute-done.3.refs_2_.refs_0_ = bf16[256,1024]{1,0:T(8,128)(2,1)S(1)} collective-permute-done((bf16[256,1024]{1,0:T(8,128)(2,1)}, bf16[256,1024]{1,0:T(8,128)(2,1)S(1)}, u32[]{:S(2)}, u32[]{:S(2)}) %collective-permute-start.3) | collective-permute-done | bytes 524320 | tf_op jit(solution)/shard_map/ppermute | solution.py:472
  33.1 0.0 collective-permute-done.2.refs_3_.refs_1_
  33.1 6.2 %all-to-all-done.got_ref = bf16[8,128,512]{2,1,0:T(8,128)(2,1)S(1)} async-done(((bf16[8,128,512]{2,1,0:T(8,128)(2,1)}), bf16[8,128,512]{2,1,0:T(8,128)(2,1)S(1)}, u32[]{:S(2)}, u32[]{:S(2)}) %all-to-all-start) | async-done | bytes 1048608 | tf_op jit(solution)/shard_map/all_to_all | solution.py:427
  39.3 0.8 split.1.own_ref
  40.1 0.5 collective-permute-start.4
  40.6 2.5 %partial_products.1 = bf16[8,176,128]{2,1,0:T(8,128)(2,1)} custom-call(s32[6]{0:T(128)S(1)} %stack.28.info_ref, bf16[8,128,512]{2,1,0:T(8,128)(2,1)S(1)} %all-to-all-done.got_ref, bf16[336,512]{1,0:T(8,128)(2,1)S(1)} %scale_rows.1.refs_0_.after_ref, bf16[336,512]{1,0:T(8,128)(2,1)} %collective-permute-done.refs_1_, ...), custom_call_target="tpu_custom_call" | custom-call | tf_op jit(solution)/shard_map/partial_products/pallas_call | solution.py:162
  43.2 3.4 %all-to-all-start.1 = ((bf16[8,176,128]{2,1,0:T(8,128)(2,1)}), bf16[8,176,128]{2,1,0:T(8,128)(2,1)S(1)}, u32[]{:S(2)}, u32[]{:S(2)}) async-start(bf16[8,176,128]{2,1,0:T(8,128)(2,1)} %partial_products.1), calls=%async_computation.1 | async-start | bytes 720896 | tf_op jit(solution)/shard_map/all_to_all | solution.py:427
  46.6 7.7 %collective-permute-done.4.other_ref = bf16[8,64,512]{2,1,0:T(8,128)(2,1)} collective-permute-done((bf16[8,64,512]{2,1,0:T(8,128)(2,1)}, bf16[8,64,512]{2,1,0:T(8,128)(2,1)}, u32[]{:S(2)}, u32[]{:S(2)}) %collective-permute-start.4) | collective-permute-done | bytes 524320 | tf_op jit(solution)/shard_map/ppermute | solution.py:474
  54.3 0.0 copy-start.4
  54.3 2.2 %copy-done.4 = bf16[8192,256]{1,0:T(8,128)(2,1)S(1)} copy-done((bf16[8192,256]{1,0:T(8,128)(2,1)S(1)}, bf16[8192,256]{1,0:T(8,128)(2,1)}, u32[]{:S(2)}) %copy-start.4) | copy-done | bytes 4194328
  56.5 2.3 %queries.1.refs_0_ = bf16[64,256]{1,0:T(8,128)(2,1)S(1)} custom-call(s32[6]{0:T(128)S(1)} %stack.28.info_ref, f32[16,1,512]{2,1,0:T(1,128)S(1)} %bitcast.14, f32[2,224,128]{2,1,0:T(8,128)S(1)} %pad_maximum_fusion.refs_4_.trig_ref, bf16[8192,256]{1,0:T(8,128)(2,1)S(1)} %copy-done.4, bf16[8,64,512]{2,1,0:T(8,128)(2,1)} %split.1.own_ref, ...), custom_call_target="tpu_custom_call" | custom-call | flops 30000001024 | bytes 1000000 | tf_op jit(solution)/shard_map/queries/pallas_call | solution.py:245
  58.8 1.9 %all-to-all-done.1.parts_ref = bf16[8,176,128]{2,1,0:T(8,128)(2,1)S(1)} async-done(((bf16[8,176,128]{2,1,0:T(8,128)(2,1)}), bf16[8,176,128]{2,1,0:T(8,128)(2,1)S(1)}, u32[]{:S(2)}, u32[]{:S(2)}) %all-to-all-start.1) | async-done | bytes 360480 | tf_op jit(solution)/shard_map/all_to_all | solution.py:427
  60.7 1.2 %finish_keys.1 = bf16[16,144,128]{2,1,0:T(8,128)(2,1)} custom-call(bf16[8,176,128]{2,1,0:T(8,128)(2,1)S(1)} %all-to-all-done.1.parts_ref, f32[2,224,128]{2,1,0:T(8,128)S(1)} %pad_maximum_fusion.refs_4_.trig_ref, bf16[64,256]{1,0:T(8,128)(2,1)S(1)} %queries.1.refs_0_), custom_call_target="tpu_custom_call" | custom-call | flops 30000001024 | bytes 1000000 | tf_op jit(solution)/shard_map/finish_keys/pallas_call | solution.py:209
  61.9 5.5 %all-to-all-start.2 = ((bf16[16,144,128]{2,1,0:T(8,128)(2,1)}), bf16[16,144,128]{2,1,0:T(8,128)(2,1)S(1)}, u32[]{:S(2)}, u32[]{:S(2)}) async-start(bf16[16,144,128]{2,1,0:T(8,128)(2,1)} %finish_keys.1), calls=%async_computation.2 | async-start | bytes 1179648 | tf_op jit(solution)/shard_map/all_to_all | solution.py:427
  67.4 0.2 collective-permute-start.12
  67.6 1.6 %collective-permute-start.5 = (bf16[64,256]{1,0:T(8,128)(2,1)S(1)}, bf16[64,256]{1,0:T(8,128)(2,1)S(1)}, u32[]{:S(2)}, u32[]{:S(2)}) collective-permute-start(bf16[64,256]{1,0:T(8,128)(2,1)S(1)} %queries.1.refs_0_), channel_id=1, source_target_pairs={{0,32},{32,64},{64,96},{96,0},{1,33},{33,65},{65,97},{97,1},{2,34}... | collective-permute-start | bytes 98312 | tf_op jit(solution)/shard_map/ppermute | solution.py:483
  69.2 2.9 %collective-permute-start.6 = (bf16[64,256]{1,0:T(8,128)(2,1)S(1)}, bf16[64,256]{1,0:T(8,128)(2,1)S(1)}, u32[]{:S(2)}, u32[]{:S(2)}) collective-permute-start(bf16[64,256]{1,0:T(8,128)(2,1)S(1)} %queries.1.refs_0_), channel_id=1, source_target_pairs={{0,64},{32,96},{64,0},{96,32},{1,65},{33,97},{65,1},{97,33},{2,66}... | collective-permute-start | bytes 98312 | tf_op jit(solution)/shard_map/ppermute | solution.py:483
  72.1 1.3 %collective-permute-start.7 = (bf16[64,256]{1,0:T(8,128)(2,1)S(1)}, bf16[64,256]{1,0:T(8,128)(2,1)S(1)}, u32[]{:S(2)}, u32[]{:S(2)}) collective-permute-start(bf16[64,256]{1,0:T(8,128)(2,1)S(1)} %queries.1.refs_0_), channel_id=1, source_target_pairs={{0,96},{32,0},{64,32},{96,64},{1,97},{33,1},{65,33},{97,65},{2,98}... | collective-permute-start | bytes 98312 | tf_op jit(solution)/shard_map/ppermute | solution.py:483
  73.5 0.0 collective-permute-done.5.refs_1_
  73.5 1.2 %collective-permute-done.6.refs_2_ = bf16[64,256]{1,0:T(8,128)(2,1)S(1)} collective-permute-done((bf16[64,256]{1,0:T(8,128)(2,1)S(1)}, bf16[64,256]{1,0:T(8,128)(2,1)S(1)}, u32[]{:S(2)}, u32[]{:S(2)}) %collective-permute-start.6) | collective-permute-done | bytes 32800 | tf_op jit(solution)/shard_map/ppermute | solution.py:483
  74.6 1.4 %collective-permute-done.7.refs_3_ = bf16[64,256]{1,0:T(8,128)(2,1)S(1)} collective-permute-done((bf16[64,256]{1,0:T(8,128)(2,1)S(1)}, bf16[64,256]{1,0:T(8,128)(2,1)S(1)}, u32[]{:S(2)}, u32[]{:S(2)}) %collective-permute-start.7) | collective-permute-done | bytes 32800 | tf_op jit(solution)/shard_map/ppermute | solution.py:483
  76.0 1.5 %all-to-all-done.2.rows_ref = bf16[16,144,128]{2,1,0:T(8,128)(2,1)S(1)} async-done(((bf16[16,144,128]{2,1,0:T(8,128)(2,1)}), bf16[16,144,128]{2,1,0:T(8,128)(2,1)S(1)}, u32[]{:S(2)}, u32[]{:S(2)}) %all-to-all-start.2) | async-done | bytes 589856 | tf_op jit(solution)/shard_map/all_to_all | solution.py:427
  77.5 2.5 %attend.1 = (bf16[64,384]{1,0:T(8,128)(2,1)S(1)}, bf16[64,384]{1,0:T(8,128)(2,1)S(1)}, bf16[64,384]{1,0:T(8,128)(2,1)S(1)}, bf16[64,384]{1,0:T(8,128)(2,1)S(1)}) custom-call(s32[6]{0:T(128)S(1)} %stack.28.info_ref, bf16[16,144,128]{2,1,0:T(8,128)(2,1)S(1)} %all-to-all-done.2.rows_ref, bf16[64,256]{1,0:T(8,128)(2,1)S(1)} %queries.1.refs_0_, ...), custom_call_target="tpu_custom_call" | custom-call | tf_op jit(solution)/shard_map/attend/pallas_call | solution.py:330
  80.1 3.1 %collective-permute-start.8 = (bf16[64,384]{1,0:T(8,128)(2,1)S(1)}, bf16[64,384]{1,0:T(8,128)(2,1)S(1)}, u32[]{:S(2)}, u32[]{:S(2)}) collective-permute-start(bf16[64,384]{1,0:T(8,128)(2,1)S(1)} %get-tuple-element.14), channel_id=1, source_target_pairs={{0,96},{32,0},{64,32},{96,64},{1,97},{33,1},{65,33},{97,65},{2,98}... | collective-permute-start | bytes 147464 | tf_op jit(solution)/shard_map/ppermute | solution.py:483
  83.2 0.6 collective-permute-start.9
  83.8 1.0 collective-permute-start.10
  84.8 0.0 collective-permute-start.13
  84.8 1.8 %collective-permute-done.12.refs_1_ = bf16[256,1024]{1,0:T(8,128)(2,1)S(1)} collective-permute-done((bf16[256,1024]{1,0:T(8,128)(2,1)S(1)}, bf16[256,1024]{1,0:T(8,128)(2,1)S(1)}, u32[]{:S(2)}, u32[]{:S(2)}) %collective-permute-start.12) | collective-permute-done | bytes 524320 | tf_op jit(solution)/shard_map/ppermute | solution.py:472
  86.6 0.0 collective-permute-start.14
  86.6 0.0 collective-permute-done.8.refs_1_
  86.6 2.2 %collective-permute-done.9.refs_2_ = bf16[64,384]{1,0:T(8,128)(2,1)S(1)} collective-permute-done((bf16[64,384]{1,0:T(8,128)(2,1)S(1)}, bf16[64,384]{1,0:T(8,128)(2,1)S(1)}, u32[]{:S(2)}, u32[]{:S(2)}) %collective-permute-start.9) | collective-permute-done | bytes 49184 | tf_op jit(solution)/shard_map/ppermute | solution.py:483
  88.8 0.5 collective-permute-done.10.refs_3_
  89.3 0.3 merge.1.own_ref
  89.6 1.5 %collective-permute-start.11 = (bf16[64,256]{1,0:T(8,128)(2,1)S(1)}, bf16[64,256]{1,0:T(8,128)(2,1)S(1)}, u32[]{:S(2)}, u32[]{:S(2)}) collective-permute-start(bf16[64,256]{1,0:T(8,128)(2,1)S(1)} %merge.1.own_ref), channel_id=1, source_target_pairs={{0,1},{1,0},{2,3},{3,2},{4,5},{5,4},{6,7},{7,6},{8,9},{9,8},{10,11... | collective-permute-start | bytes 98312 | tf_op jit(solution)/shard_map/ppermute | solution.py:488
  91.1 2.2 %copy-done.1 = bf16[256,8192]{1,0:T(8,128)(2,1)S(1)} copy-done((bf16[256,8192]{1,0:T(8,128)(2,1)S(1)}, bf16[256,8192]{1,0:T(8,128)(2,1)}, u32[]{:S(2)}) %copy-start.1) | copy-done | bytes 4194328
  93.3 1.0 project_own.1.started_ref
  94.3 0.0 collective-permute-done.13.refs_2_
  94.3 0.0 collective-permute-done.14.refs_3_
  94.3 0.0 collective-permute-done.11.other_ref
  94.4 1.8 %project.1 = bf16[8,64,512]{2,1,0:T(8,128)(2,1)} custom-call(s32[6]{0:T(128)S(1)} %stack.28.info_ref, f32[8,64,512]{2,1,0:T(8,128)S(1)} %project_own.1.started_ref, bf16[64,256]{1,0:T(8,128)(2,1)S(1)} %collective-permute-done.11.other_ref, bf16[256,1024]{1,0:T(8,128)(2,1)S(1)} %collective-permute-done.3.refs_2_.refs_0_, ...), custom_call_target="tpu_custom_call" | custom-call | tf_op jit(solution)/shard_map/project/pallas_call | solution.py:399
  96.2 3.5 %all-to-all-start.3 = ((bf16[8,64,512]{2,1,0:T(8,128)(2,1)}), bf16[8,64,512]{2,1,0:T(8,128)(2,1)S(1)}, u32[]{:S(2)}, u32[]{:S(2)}) async-start(bf16[8,64,512]{2,1,0:T(8,128)(2,1)} %project.1), calls=%async_computation.3 | async-start | bytes 1048576 | tf_op jit(solution)/shard_map/all_to_all | solution.py:427
  100.4 15.0 %all-to-all-done.3 = bf16[8,64,512]{2,1,0:T(8,128)(2,1)S(1)} async-done(((bf16[8,64,512]{2,1,0:T(8,128)(2,1)}), bf16[8,64,512]{2,1,0:T(8,128)(2,1)S(1)}, u32[]{:S(2)}, u32[]{:S(2)}) %all-to-all-start.3) | async-done | bytes 524320 | tf_op jit(solution)/shard_map/all_to_all | solution.py:427
  115.3 0.1 convert_reduce_fusion
  115.4 0.7 select_convert_fusion
  (8 shorter events, 0.1 us)
Async XLA Ops:
  0.0 11.3 %copy-start.2 = (bf16[64,512]{1,0:T(8,128)(2,1)S(1)}, bf16[64,512]{1,0:T(8,128)(2,1)}, u32[]{:S(2)}) copy-start(bf16[64,512]{1,0:T(8,128)(2,1)} %resp_ref.1) | copy-start | bytes 196612
  0.0 11.2 %copy-start.5 = (bf16[8192]{0:T(1024)(128)(2,1)S(1)}, bf16[8192]{0:T(1024)(128)(2,1)}, u32[]{:S(2)}) copy-start(bf16[8192]{0:T(1024)(128)(2,1)} %param.11) | copy-start | bytes 49156
  0.0 11.3 %copy-start.3 = (bf16[256,512]{1,0:T(8,128)(2,1)S(1)}, bf16[256,512]{1,0:T(8,128)(2,1)}, u32[]{:S(2)}) copy-start(bf16[256,512]{1,0:T(8,128)(2,1)} %prompt_ref.1) | copy-start | bytes 786436
  2.1 37.2 %all-to-all-start = ((bf16[8,128,512]{2,1,0:T(8,128)(2,1)}), bf16[8,128,512]{2,1,0:T(8,128)(2,1)S(1)}, u32[]{:S(2)}, u32[]{:S(2)}) async-start(bf16[8,128,512]{2,1,0:T(8,128)(2,1)} %pack.1), calls=%async_computation | async-start | bytes 2097152 | tf_op jit(solution)/shard_map/all_to_all | solution.py:427
  12.3 11.1 %collective-permute-start = (bf16[336,512]{1,0:T(8,128)(2,1)S(1)}, bf16[336,512]{1,0:T(8,128)(2,1)}, u32[]{:S(2)}, u32[]{:S(2)}) collective-permute-start(bf16[336,512]{1,0:T(8,128)(2,1)S(1)} %scale_rows.1.refs_0_.after_ref), channel_id=1, source_target_pairs={{0,1},{1,0},{2,3},{3,2},{4,5},{5,4},{6,7},{7,6},{8,9},{9,8},{10,11... | collective-permute-start | bytes 1032200 | tf_op jit(solution)/shard_map/ppermute | solution.py:469
  12.8 11.2 %collective-permute-start.1 = (bf16[336,512]{1,0:T(8,128)(2,1)S(1)}, bf16[336,512]{1,0:T(8,128)(2,1)S(1)}, u32[]{:S(2)}, u32[]{:S(2)}) collective-permute-start(bf16[336,512]{1,0:T(8,128)(2,1)S(1)} %scale_rows.1.refs_0_.after_ref), channel_id=1, source_target_pairs={{0,16},{16,0},{1,17},{17,1},{2,18},{18,2},{3,19},{19,3},{4,20},{20... | collective-permute-start | bytes 1032200 | tf_op jit(solution)/shard_map/ppermute | solution.py:470
  12.8 2.2 %copy-start = (bf16[256,8192]{1,0:T(8,128)(2,1)S(1)}, bf16[256,8192]{1,0:T(8,128)(2,1)}, u32[]{:S(2)}) copy-start(bf16[256,8192]{1,0:T(8,128)(2,1)} %weight_ref.5) | copy-start | bytes 12582916
  16.5 16.6 %collective-permute-start.3 = (bf16[256,1024]{1,0:T(8,128)(2,1)}, bf16[256,1024]{1,0:T(8,128)(2,1)S(1)}, u32[]{:S(2)}, u32[]{:S(2)}) collective-permute-start(bf16[256,1024]{1,0:T(8,128)(2,1)} %get-tuple-element.11), channel_id=1, source_target_pairs={{0,1},{1,0},{2,3},{3,2},{4,5},{5,4},{6,7},{7,6},{8,9},{9,8},{10,11... | collective-permute-start | bytes 1572872 | tf_op jit(solution)/shard_map/ppermute | solution.py:472
  23.4 9.7 %collective-permute-start.2 = (bf16[336,512]{1,0:T(8,128)(2,1)}, bf16[336,512]{1,0:T(8,128)(2,1)S(1)}, u32[]{:S(2)}, u32[]{:S(2)}) collective-permute-start(bf16[336,512]{1,0:T(8,128)(2,1)} %collective-permute-done.refs_1_), channel_id=1, source_target_pairs={{0,16},{16,0},{1,17},{17,1},{2,18},{18,2},{3,19},{19,3},{4,20},{20... | collective-permute-start | bytes 1032200 | tf_op jit(solution)/shard_map/ppermute | solution.py:470
  40.1 14.2 %collective-permute-start.4 = (bf16[8,64,512]{2,1,0:T(8,128)(2,1)}, bf16[8,64,512]{2,1,0:T(8,128)(2,1)}, u32[]{:S(2)}, u32[]{:S(2)}) collective-permute-start(bf16[8,64,512]{2,1,0:T(8,128)(2,1)} %split.1.own_ref), channel_id=1, source_target_pairs={{0,1},{1,0},{2,3},{3,2},{4,5},{5,4},{6,7},{7,6},{8,9},{9,8},{10,11... | collective-permute-start | bytes 1572872 | tf_op jit(solution)/shard_map/ppermute | solution.py:474
  43.2 17.5 %all-to-all-start.1 = ((bf16[8,176,128]{2,1,0:T(8,128)(2,1)}), bf16[8,176,128]{2,1,0:T(8,128)(2,1)S(1)}, u32[]{:S(2)}, u32[]{:S(2)}) async-start(bf16[8,176,128]{2,1,0:T(8,128)(2,1)} %partial_products.1), calls=%async_computation.1 | async-start | bytes 720896 | tf_op jit(solution)/shard_map/all_to_all | solution.py:427
  54.3 2.2 %copy-start.4 = (bf16[8192,256]{1,0:T(8,128)(2,1)S(1)}, bf16[8192,256]{1,0:T(8,128)(2,1)}, u32[]{:S(2)}) copy-start(bf16[8192,256]{1,0:T(8,128)(2,1)} %weight_ref.4) | copy-start | bytes 12582916
  61.9 15.6 %all-to-all-start.2 = ((bf16[16,144,128]{2,1,0:T(8,128)(2,1)}), bf16[16,144,128]{2,1,0:T(8,128)(2,1)S(1)}, u32[]{:S(2)}, u32[]{:S(2)}) async-start(bf16[16,144,128]{2,1,0:T(8,128)(2,1)} %finish_keys.1), calls=%async_computation.2 | async-start | bytes 1179648 | tf_op jit(solution)/shard_map/all_to_all | solution.py:427
  67.4 19.2 %collective-permute-start.12 = (bf16[256,1024]{1,0:T(8,128)(2,1)S(1)}, bf16[256,1024]{1,0:T(8,128)(2,1)S(1)}, u32[]{:S(2)}, u32[]{:S(2)}) collective-permute-start(bf16[256,1024]{1,0:T(8,128)(2,1)S(1)} %get-tuple-element.12.refs_3_), channel_id=1, source_target_pairs={{0,1},{1,0},{2,3},{3,2},{4,5},{5,4},{6,7},{7,6},{8,9},{9,8},{10,11... | collective-permute-start | bytes 1572872 | tf_op jit(solution)/shard_map/ppermute | solution.py:472
  67.6 5.8 %collective-permute-start.5 = (bf16[64,256]{1,0:T(8,128)(2,1)S(1)}, bf16[64,256]{1,0:T(8,128)(2,1)S(1)}, u32[]{:S(2)}, u32[]{:S(2)}) collective-permute-start(bf16[64,256]{1,0:T(8,128)(2,1)S(1)} %queries.1.refs_0_), channel_id=1, source_target_pairs={{0,32},{32,64},{64,96},{96,0},{1,33},{33,65},{65,97},{97,1},{2,34}... | collective-permute-start | bytes 98312 | tf_op jit(solution)/shard_map/ppermute | solution.py:483
  69.2 5.4 %collective-permute-start.6 = (bf16[64,256]{1,0:T(8,128)(2,1)S(1)}, bf16[64,256]{1,0:T(8,128)(2,1)S(1)}, u32[]{:S(2)}, u32[]{:S(2)}) collective-permute-start(bf16[64,256]{1,0:T(8,128)(2,1)S(1)} %queries.1.refs_0_), channel_id=1, source_target_pairs={{0,64},{32,96},{64,0},{96,32},{1,65},{33,97},{65,1},{97,33},{2,66}... | collective-permute-start | bytes 98312 | tf_op jit(solution)/shard_map/ppermute | solution.py:483
  72.1 3.9 %collective-permute-start.7 = (bf16[64,256]{1,0:T(8,128)(2,1)S(1)}, bf16[64,256]{1,0:T(8,128)(2,1)S(1)}, u32[]{:S(2)}, u32[]{:S(2)}) collective-permute-start(bf16[64,256]{1,0:T(8,128)(2,1)S(1)} %queries.1.refs_0_), channel_id=1, source_target_pairs={{0,96},{32,0},{64,32},{96,64},{1,97},{33,1},{65,33},{97,65},{2,98}... | collective-permute-start | bytes 98312 | tf_op jit(solution)/shard_map/ppermute | solution.py:483
  80.1 6.6 %collective-permute-start.8 = (bf16[64,384]{1,0:T(8,128)(2,1)S(1)}, bf16[64,384]{1,0:T(8,128)(2,1)S(1)}, u32[]{:S(2)}, u32[]{:S(2)}) collective-permute-start(bf16[64,384]{1,0:T(8,128)(2,1)S(1)} %get-tuple-element.14), channel_id=1, source_target_pairs={{0,96},{32,0},{64,32},{96,64},{1,97},{33,1},{65,33},{97,65},{2,98}... | collective-permute-start | bytes 147464 | tf_op jit(solution)/shard_map/ppermute | solution.py:483
  83.2 5.6 %collective-permute-start.9 = (bf16[64,384]{1,0:T(8,128)(2,1)S(1)}, bf16[64,384]{1,0:T(8,128)(2,1)S(1)}, u32[]{:S(2)}, u32[]{:S(2)}) collective-permute-start(bf16[64,384]{1,0:T(8,128)(2,1)S(1)} %get-tuple-element.15), channel_id=1, source_target_pairs={{0,64},{32,96},{64,0},{96,32},{1,65},{33,97},{65,1},{97,33},{2,66}... | collective-permute-start | bytes 147464 | tf_op jit(solution)/shard_map/ppermute | solution.py:483
  83.8 5.5 %collective-permute-start.10 = (bf16[64,384]{1,0:T(8,128)(2,1)S(1)}, bf16[64,384]{1,0:T(8,128)(2,1)S(1)}, u32[]{:S(2)}, u32[]{:S(2)}) collective-permute-start(bf16[64,384]{1,0:T(8,128)(2,1)S(1)} %get-tuple-element.16), channel_id=1, source_target_pairs={{0,32},{32,64},{64,96},{96,0},{1,33},{33,65},{65,97},{97,1},{2,34}... | collective-permute-start | bytes 147464 | tf_op jit(solution)/shard_map/ppermute | solution.py:483
  84.8 9.6 %collective-permute-start.13 = (bf16[256,1024]{1,0:T(8,128)(2,1)S(1)}, bf16[256,1024]{1,0:T(8,128)(2,1)S(1)}, u32[]{:S(2)}, u32[]{:S(2)}) collective-permute-start(bf16[256,1024]{1,0:T(8,128)(2,1)S(1)} %collective-permute-done.3.refs_2_.refs_0_), channel_id=1, source_target_pairs={{0,16},{16,0},{1,17},{17,1},{2,18},{18,2},{3,19},{19,3},{4,20},{20... | collective-permute-start | bytes 1572872 | tf_op jit(solution)/shard_map/ppermute | solution.py:478
  86.6 7.7 %collective-permute-start.14 = (bf16[256,1024]{1,0:T(8,128)(2,1)S(1)}, bf16[256,1024]{1,0:T(8,128)(2,1)S(1)}, u32[]{:S(2)}, u32[]{:S(2)}) collective-permute-start(bf16[256,1024]{1,0:T(8,128)(2,1)S(1)} %collective-permute-done.12.refs_1_), channel_id=1, source_target_pairs={{0,16},{16,0},{1,17},{17,1},{2,18},{18,2},{3,19},{19,3},{4,20},{20... | collective-permute-start | bytes 1572872 | tf_op jit(solution)/shard_map/ppermute | solution.py:478
  89.6 4.8 %collective-permute-start.11 = (bf16[64,256]{1,0:T(8,128)(2,1)S(1)}, bf16[64,256]{1,0:T(8,128)(2,1)S(1)}, u32[]{:S(2)}, u32[]{:S(2)}) collective-permute-start(bf16[64,256]{1,0:T(8,128)(2,1)S(1)} %merge.1.own_ref), channel_id=1, source_target_pairs={{0,1},{1,0},{2,3},{3,2},{4,5},{5,4},{6,7},{7,6},{8,9},{9,8},{10,11... | collective-permute-start | bytes 98312 | tf_op jit(solution)/shard_map/ppermute | solution.py:488
  91.1 2.2 %copy-start.1 = (bf16[256,8192]{1,0:T(8,128)(2,1)S(1)}, bf16[256,8192]{1,0:T(8,128)(2,1)}, u32[]{:S(2)}) copy-start(bf16[256,8192]{1,0:T(8,128)(2,1)} %weight_ref.5) | copy-start | bytes 12582916
  96.2 19.1 %all-to-all-start.3 = ((bf16[8,64,512]{2,1,0:T(8,128)(2,1)}), bf16[8,64,512]{2,1,0:T(8,128)(2,1)S(1)}, u32[]{:S(2)}, u32[]{:S(2)}) async-start(bf16[8,64,512]{2,1,0:T(8,128)(2,1)} %project.1), calls=%async_computation.3 | async-start | bytes 1048576 | tf_op jit(solution)/shard_map/all_to_all | solution.py:427

commit v6 on v5

--- a/solution.py
+++ b/solution.py
@@ -173,7 +173,7 @@
 
 
 def finish_kernel(parts_ref, trig_ref, *refs):
-    out_ref = refs[-1]
+    out_ref, shared, sems = refs[-3:]
     total = jnp.sum(parts_ref[...].astype(F32), axis=0)
     sums = total[ROWS:]
     factors = []
@@ -200,16 +200,23 @@
         jnp.where(left, first, pltpu.roll(second, 64, 1)).astype(BF16),
         jnp.where(left, pltpu.roll(first, 64, 1), second).astype(BF16),
     )
-    for i in range(out_ref.shape[0]):
-        out_ref[i, :128] = prompt
-        out_ref[i, 128:] = resp[(i >> 2) & 1]
+    for core in range(2):
+        shared[core, :128] = prompt
+        shared[core, 128:] = resp[core]
+    copies = [pltpu.make_async_copy(shared.at[(i >> 2) & 1], out_ref.at[i], sems.at[i]) for i in range(16)]
+    for copy in copies:
+        copy.start()
+    for copy in copies:
+        copy.wait()
 
 
 def finish_keys(parts, trig, *after):
     return pl.pallas_call(
         finish_kernel,
         in_specs=[pl.BlockSpec(memory_space=pltpu.VMEM)] * (2 + len(after)),
+        out_specs=pl.BlockSpec(memory_space=pl.ANY),
         out_shape=jax.ShapeDtypeStruct((16, SHARED_ROWS, 128), BF16),
+        scratch_shapes=[pltpu.VMEM((2, SHARED_ROWS, 128), BF16), pltpu.SemaphoreType.DMA((16,))],
         compiler_params=params(SMALL),
         cost_estimate=LONG,
         name="finish_keys",
@@ -482,9 +489,10 @@
     def along(values, step):
         return lax.ppermute(values, "y", [(i, (i + step) % 4) for i in range(4)])
 
-    pooled = [queries] + [along(queries, step) for step in (1, 2, 3)]
+    around = {step: along(queries, step) for step in (2, 1, 3)}
+    pooled = [queries] + [around[step] for step in (1, 2, 3)]
     parts = attend(info, rows, pooled)
-    attention = merge([parts[0]] + [along(parts[step], -step) for step in (1, 2, 3)])
+    attention = merge([along(parts[step], -step) for step in (2, 1, 3)] + [parts[0]])
     partner = lax.ppermute(attention, "xl", flip)
     partial = project(info, project_own(info, attention, output_weight), partner, cross)
     summed = jnp.sum(swap(partial, ZRING).astype(F32), axis=0)

time: 117 us -> 117 us (level)
  no operation moved by 1% of the time
where the time goes in v6:
time: 117 us; the launch traced here: 116 us
  waiting for transfers between devices  53.1 us (45%)
  starting transfers between devices  36.4 us (31%)
  Pallas kernels  17.2 us (15%)
  local copies, waits for them, and re-layouts  6.66 us (6%)
  other arithmetic  1.47 us (1%)
  between operations  1.47 us (1%)
    all_to_all x4, waiting for transfers between devices, swap(): return lax.all_to_all(values, axis, 0, 0, tiled=False)  24.1 us
    all_to_all x4, starting transfers between devices, swap(): return lax.all_to_all(values, axis, 0, 0, tiled=False)  20.9 us
    ppermute x6, starting transfers between devices, along(): return lax.ppermute(values, 'y', [(i, (i + step) % 4) for i in range(4)])  11.1 us
    ppermute x2, waiting for transfers between devices, body(): early, late = (lax.ppermute(piece, 'xl', flip) for piece in sent)  10.2 us
    ppermute x1, waiting for transfers between devices, body(): other_hidden = lax.ppermute(own_hidden, 'xl', flip)  7.66 us
    unnamed x12, local copies, waits for them, and re-layouts  6.57 us
    ppermute x6, waiting for transfers between devices, along(): return lax.ppermute(values, 'y', [(i, (i + step) % 4) for i in range(4)])  5.67 us
    ppermute x1, waiting for transfers between devices, body(): beside = lax.ppermute(scaled, 'xl', flip)  5.39 us
  transfers between devices with their start and end apart: 19, of which 12 were waited for; matrix products, arithmetic and copies ran while one was open for 1% of the time, Pallas kernels for 10%

profile of v6, /device:TPU:2, one launch (start us, length us, event | category | flops | bytes accessed | tf_op | source)
XLA Modules:
  0.0 116.3 jit_solution(14964178906867353404)
XLA Ops:
  0.0 0.0 copy-start.2
  0.0 0.0 copy-start.5
  0.0 0.0 copy-start.3
  0.0 2.1 %pack.1 = bf16[8,128,512]{2,1,0:T(8,128)(2,1)} custom-call(s32[1]{0:T(128)} %bitcast.1.core_ref, bf16[32,8192]{1,0:T(8,128)(2,1)} %bitcast.15, bf16[32,8192]{1,0:T(8,128)(2,1)} %bitcast.16, bf16[64,512]{1,0:T(8,128)(2,1)} %resp_ref.1), custom_call_target="tpu_custom_call" | custom-call | tf_op jit(solution)/shard_map/pack/pallas_call | solution.py:69
  2.1 8.5 %all-to-all-start = ((bf16[8,128,512]{2,1,0:T(8,128)(2,1)}), bf16[8,128,512]{2,1,0:T(8,128)(2,1)S(1)}, u32[]{:S(2)}, u32[]{:S(2)}) async-start(bf16[8,128,512]{2,1,0:T(8,128)(2,1)} %pack.1), calls=%async_computation | async-start | bytes 2097152 | tf_op jit(solution)/shard_map/all_to_all | solution.py:434
  11.2 0.0 copy-done.5
  11.2 0.1 stack.28.info_ref
  11.3 0.0 copy-done.2
  11.3 0.0 copy-done.3
  11.3 1.0 scale_rows.1.refs_0_.after_ref
  12.3 0.6 collective-permute-start
  12.8 0.0 collective-permute-start.1
  12.8 0.0 copy-start
  12.8 2.2 %copy-done = bf16[256,8192]{1,0:T(8,128)(2,1)S(1)} copy-done((bf16[256,8192]{1,0:T(8,128)(2,1)S(1)}, bf16[256,8192]{1,0:T(8,128)(2,1)}, u32[]{:S(2)}) %copy-start) | copy-done | bytes 4194328
  15.0 1.4 %pick_columns.1 = (bf16[256,1024]{1,0:T(8,128)(2,1)}, bf16[256,1024]{1,0:T(8,128)(2,1)S(1)}) custom-call(s32[6]{0:T(128)S(1)} %stack.28.info_ref, bf16[256,8192]{1,0:T(8,128)(2,1)S(1)} %copy-done, bf16[336,512]{1,0:T(8,128)(2,1)S(1)} %scale_rows.1.refs_0_.after_ref), custom_call_target="tpu_custom_call" | custom-call | tf_op jit(solution)/shard_map/pick_columns/pallas_call | solution.py:424
  16.5 1.5 %collective-permute-start.3 = (bf16[256,1024]{1,0:T(8,128)(2,1)}, bf16[256,1024]{1,0:T(8,128)(2,1)S(1)}, u32[]{:S(2)}, u32[]{:S(2)}) collective-permute-start(bf16[256,1024]{1,0:T(8,128)(2,1)} %get-tuple-element.11), channel_id=1, source_target_pairs={{0,1},{1,0},{2,3},{3,2},{4,5},{5,4},{6,7},{7,6},{8,9},{9,8},{10,11... | collective-permute-start | bytes 1572872 | tf_op jit(solution)/shard_map/ppermute | solution.py:479
  18.0 5.4 %collective-permute-done.refs_1_ = bf16[336,512]{1,0:T(8,128)(2,1)} collective-permute-done((bf16[336,512]{1,0:T(8,128)(2,1)S(1)}, bf16[336,512]{1,0:T(8,128)(2,1)}, u32[]{:S(2)}, u32[]{:S(2)}) %collective-permute-start) | collective-permute-done | bytes 344096 | tf_op jit(solution)/shard_map/ppermute | solution.py:476
  23.4 0.0 collective-permute-start.2
  23.4 0.6 fusion.11
  24.0 0.0 collective-permute-done.1.refs_2_.refs_0_
  24.1 9.0 %collective-permute-done.3.refs_2_.refs_0_ = bf16[256,1024]{1,0:T(8,128)(2,1)S(1)} collective-permute-done((bf16[256,1024]{1,0:T(8,128)(2,1)}, bf16[256,1024]{1,0:T(8,128)(2,1)S(1)}, u32[]{:S(2)}, u32[]{:S(2)}) %collective-permute-start.3) | collective-permute-done | bytes 524320 | tf_op jit(solution)/shard_map/ppermute | solution.py:479
  33.1 0.0 collective-permute-done.2.refs_3_.refs_1_
  33.1 6.2 %all-to-all-done.got_ref = bf16[8,128,512]{2,1,0:T(8,128)(2,1)S(1)} async-done(((bf16[8,128,512]{2,1,0:T(8,128)(2,1)}), bf16[8,128,512]{2,1,0:T(8,128)(2,1)S(1)}, u32[]{:S(2)}, u32[]{:S(2)}) %all-to-all-start) | async-done | bytes 1048608 | tf_op jit(solution)/shard_map/all_to_all | solution.py:434
  39.3 0.8 split.1.own_ref
  40.1 0.5 collective-permute-start.4
  40.6 2.5 %partial_products.1 = bf16[8,176,128]{2,1,0:T(8,128)(2,1)} custom-call(s32[6]{0:T(128)S(1)} %stack.28.info_ref, bf16[8,128,512]{2,1,0:T(8,128)(2,1)S(1)} %all-to-all-done.got_ref, bf16[336,512]{1,0:T(8,128)(2,1)S(1)} %scale_rows.1.refs_0_.after_ref, bf16[336,512]{1,0:T(8,128)(2,1)} %collective-permute-done.refs_1_, ...), custom_call_target="tpu_custom_call" | custom-call | tf_op jit(solution)/shard_map/partial_products/pallas_call | solution.py:162
  43.2 3.4 %all-to-all-start.1 = ((bf16[8,176,128]{2,1,0:T(8,128)(2,1)}), bf16[8,176,128]{2,1,0:T(8,128)(2,1)S(1)}, u32[]{:S(2)}, u32[]{:S(2)}) async-start(bf16[8,176,128]{2,1,0:T(8,128)(2,1)} %partial_products.1), calls=%async_computation.1 | async-start | bytes 720896 | tf_op jit(solution)/shard_map/all_to_all | solution.py:434
  46.6 7.7 %collective-permute-done.4.other_ref = bf16[8,64,512]{2,1,0:T(8,128)(2,1)} collective-permute-done((bf16[8,64,512]{2,1,0:T(8,128)(2,1)}, bf16[8,64,512]{2,1,0:T(8,128)(2,1)}, u32[]{:S(2)}, u32[]{:S(2)}) %collective-permute-start.4) | collective-permute-done | bytes 524320 | tf_op jit(solution)/shard_map/ppermute | solution.py:481
  54.3 0.0 copy-start.4
  54.3 2.2 %copy-done.4 = bf16[8192,256]{1,0:T(8,128)(2,1)S(1)} copy-done((bf16[8192,256]{1,0:T(8,128)(2,1)S(1)}, bf16[8192,256]{1,0:T(8,128)(2,1)}, u32[]{:S(2)}) %copy-start.4) | copy-done | bytes 4194328
  56.5 2.3 %queries.1.refs_0_ = bf16[64,256]{1,0:T(8,128)(2,1)S(1)} custom-call(s32[6]{0:T(128)S(1)} %stack.28.info_ref, f32[16,1,512]{2,1,0:T(1,128)S(1)} %bitcast.14, f32[2,224,128]{2,1,0:T(8,128)S(1)} %pad_maximum_fusion.refs_4_.trig_ref, bf16[8192,256]{1,0:T(8,128)(2,1)S(1)} %copy-done.4, bf16[8,64,512]{2,1,0:T(8,128)(2,1)} %split.1.own_ref, ...), custom_call_target="tpu_custom_call" | custom-call | flops 30000001024 | bytes 1000000 | tf_op jit(solution)/shard_map/queries/pallas_call | solution.py:252
  58.8 1.9 %all-to-all-done.1.parts_ref = bf16[8,176,128]{2,1,0:T(8,128)(2,1)S(1)} async-done(((bf16[8,176,128]{2,1,0:T(8,128)(2,1)}), bf16[8,176,128]{2,1,0:T(8,128)(2,1)S(1)}, u32[]{:S(2)}, u32[]{:S(2)}) %all-to-all-start.1) | async-done | bytes 360480 | tf_op jit(solution)/shard_map/all_to_all | solution.py:434
  60.7 1.4 %finish_keys.1 = bf16[16,144,128]{2,1,0:T(8,128)(2,1)} custom-call(bf16[8,176,128]{2,1,0:T(8,128)(2,1)S(1)} %all-to-all-done.1.parts_ref, f32[2,224,128]{2,1,0:T(8,128)S(1)} %pad_maximum_fusion.refs_4_.trig_ref, bf16[64,256]{1,0:T(8,128)(2,1)S(1)} %queries.1.refs_0_), custom_call_target="tpu_custom_call" | custom-call | flops 30000001024 | bytes 1000000 | tf_op jit(solution)/shard_map/finish_keys/pallas_call | solution.py:214
  62.1 5.5 %all-to-all-start.2 = ((bf16[16,144,128]{2,1,0:T(8,128)(2,1)}), bf16[16,144,128]{2,1,0:T(8,128)(2,1)S(1)}, u32[]{:S(2)}, u32[]{:S(2)}) async-start(bf16[16,144,128]{2,1,0:T(8,128)(2,1)} %finish_keys.1), calls=%async_computation.2 | async-start | bytes 1179648 | tf_op jit(solution)/shard_map/all_to_all | solution.py:434
  67.6 0.2 collective-permute-start.12
  67.8 1.6 %collective-permute-start.5 = (bf16[64,256]{1,0:T(8,128)(2,1)S(1)}, bf16[64,256]{1,0:T(8,128)(2,1)S(1)}, u32[]{:S(2)}, u32[]{:S(2)}) collective-permute-start(bf16[64,256]{1,0:T(8,128)(2,1)S(1)} %queries.1.refs_0_), channel_id=1, source_target_pairs={{0,32},{32,64},{64,96},{96,0},{1,33},{33,65},{65,97},{97,1},{2,34}... | collective-permute-start | bytes 98312 | tf_op jit(solution)/shard_map/ppermute | solution.py:490
  69.4 2.9 %collective-permute-start.6 = (bf16[64,256]{1,0:T(8,128)(2,1)S(1)}, bf16[64,256]{1,0:T(8,128)(2,1)S(1)}, u32[]{:S(2)}, u32[]{:S(2)}) collective-permute-start(bf16[64,256]{1,0:T(8,128)(2,1)S(1)} %queries.1.refs_0_), channel_id=1, source_target_pairs={{0,64},{32,96},{64,0},{96,32},{1,65},{33,97},{65,1},{97,33},{2,66}... | collective-permute-start | bytes 98312 | tf_op jit(solution)/shard_map/ppermute | solution.py:490
  72.3 1.3 %collective-permute-start.7 = (bf16[64,256]{1,0:T(8,128)(2,1)S(1)}, bf16[64,256]{1,0:T(8,128)(2,1)S(1)}, u32[]{:S(2)}, u32[]{:S(2)}) collective-permute-start(bf16[64,256]{1,0:T(8,128)(2,1)S(1)} %queries.1.refs_0_), channel_id=1, source_target_pairs={{0,96},{32,0},{64,32},{96,64},{1,97},{33,1},{65,33},{97,65},{2,98}... | collective-permute-start | bytes 98312 | tf_op jit(solution)/shard_map/ppermute | solution.py:490
  73.6 0.0 collective-permute-done.5.refs_1_
  73.6 1.2 %collective-permute-done.6.refs_2_ = bf16[64,256]{1,0:T(8,128)(2,1)S(1)} collective-permute-done((bf16[64,256]{1,0:T(8,128)(2,1)S(1)}, bf16[64,256]{1,0:T(8,128)(2,1)S(1)}, u32[]{:S(2)}, u32[]{:S(2)}) %collective-permute-start.6) | collective-permute-done | bytes 32800 | tf_op jit(solution)/shard_map/ppermute | solution.py:490
  74.8 1.4 %collective-permute-done.7.refs_3_ = bf16[64,256]{1,0:T(8,128)(2,1)S(1)} collective-permute-done((bf16[64,256]{1,0:T(8,128)(2,1)S(1)}, bf16[64,256]{1,0:T(8,128)(2,1)S(1)}, u32[]{:S(2)}, u32[]{:S(2)}) %collective-permute-start.7) | collective-permute-done | bytes 32800 | tf_op jit(solution)/shard_map/ppermute | solution.py:490
  76.2 1.5 %all-to-all-done.2.rows_ref = bf16[16,144,128]{2,1,0:T(8,128)(2,1)S(1)} async-done(((bf16[16,144,128]{2,1,0:T(8,128)(2,1)}), bf16[16,144,128]{2,1,0:T(8,128)(2,1)S(1)}, u32[]{:S(2)}, u32[]{:S(2)}) %all-to-all-start.2) | async-done | bytes 589856 | tf_op jit(solution)/shard_map/all_to_all | solution.py:434
  77.7 2.6 %attend.1 = (bf16[64,384]{1,0:T(8,128)(2,1)S(1)}, bf16[64,384]{1,0:T(8,128)(2,1)S(1)}, bf16[64,384]{1,0:T(8,128)(2,1)S(1)}, bf16[64,384]{1,0:T(8,128)(2,1)S(1)}) custom-call(s32[6]{0:T(128)S(1)} %stack.28.info_ref, bf16[16,144,128]{2,1,0:T(8,128)(2,1)S(1)} %all-to-all-done.2.rows_ref, bf16[64,256]{1,0:T(8,128)(2,1)S(1)} %queries.1.refs_0_, ...), custom_call_target="tpu_custom_call" | custom-call | tf_op jit(solution)/shard_map/attend/pallas_call | solution.py:337
  80.2 3.3 %collective-permute-start.8 = (bf16[64,384]{1,0:T(8,128)(2,1)S(1)}, bf16[64,384]{1,0:T(8,128)(2,1)S(1)}, u32[]{:S(2)}, u32[]{:S(2)}) collective-permute-start(bf16[64,384]{1,0:T(8,128)(2,1)S(1)} %get-tuple-element.13), channel_id=1, source_target_pairs={{0,64},{32,96},{64,0},{96,32},{1,65},{33,97},{65,1},{97,33},{2,66}... | collective-permute-start | bytes 147464 | tf_op jit(solution)/shard_map/ppermute | solution.py:490
  83.5 1.1 collective-permute-start.9
  84.6 1.0 collective-permute-start.10
  85.5 0.0 collective-permute-start.13
  85.5 1.2 %collective-permute-done.12.refs_1_ = bf16[256,1024]{1,0:T(8,128)(2,1)S(1)} collective-permute-done((bf16[256,1024]{1,0:T(8,128)(2,1)S(1)}, bf16[256,1024]{1,0:T(8,128)(2,1)S(1)}, u32[]{:S(2)}, u32[]{:S(2)}) %collective-permute-start.12) | collective-permute-done | bytes 524320 | tf_op jit(solution)/shard_map/ppermute | solution.py:479
  86.8 0.0 collective-permute-start.14
  86.8 0.0 collective-permute-done.8.refs_0_
  86.8 0.8 collective-permute-done.9.refs_1_
  87.6 2.3 %collective-permute-done.10.refs_2_ = bf16[64,384]{1,0:T(8,128)(2,1)S(1)} collective-permute-done((bf16[64,384]{1,0:T(8,128)(2,1)S(1)}, bf16[64,384]{1,0:T(8,128)(2,1)S(1)}, u32[]{:S(2)}, u32[]{:S(2)}) %collective-permute-start.10) | collective-permute-done | bytes 49184 | tf_op jit(solution)/shard_map/ppermute | solution.py:490
  89.9 0.3 merge.1.own_ref
  90.2 1.5 %collective-permute-start.11 = (bf16[64,256]{1,0:T(8,128)(2,1)S(1)}, bf16[64,256]{1,0:T(8,128)(2,1)S(1)}, u32[]{:S(2)}, u32[]{:S(2)}) collective-permute-start(bf16[64,256]{1,0:T(8,128)(2,1)S(1)} %merge.1.own_ref), channel_id=1, source_target_pairs={{0,1},{1,0},{2,3},{3,2},{4,5},{5,4},{6,7},{7,6},{8,9},{9,8},{10,11... | collective-permute-start | bytes 98312 | tf_op jit(solution)/shard_map/ppermute | solution.py:496
  91.7 2.2 %copy-done.1 = bf16[256,8192]{1,0:T(8,128)(2,1)S(1)} copy-done((bf16[256,8192]{1,0:T(8,128)(2,1)S(1)}, bf16[256,8192]{1,0:T(8,128)(2,1)}, u32[]{:S(2)}) %copy-start.1) | copy-done | bytes 4194328
  93.9 1.0 project_own.1.started_ref
  94.9 0.0 collective-permute-done.13.refs_2_
  94.9 0.0 collective-permute-done.14.refs_3_
  94.9 0.0 collective-permute-done.11.other_ref
  94.9 1.8 %project.1 = bf16[8,64,512]{2,1,0:T(8,128)(2,1)} custom-call(s32[6]{0:T(128)S(1)} %stack.28.info_ref, f32[8,64,512]{2,1,0:T(8,128)S(1)} %project_own.1.started_ref, bf16[64,256]{1,0:T(8,128)(2,1)S(1)} %collective-permute-done.11.other_ref, bf16[256,1024]{1,0:T(8,128)(2,1)S(1)} %collective-permute-done.3.refs_2_.refs_0_, ...), custom_call_target="tpu_custom_call" | custom-call | tf_op jit(solution)/shard_map/project/pallas_call | solution.py:406
  96.8 3.5 %all-to-all-start.3 = ((bf16[8,64,512]{2,1,0:T(8,128)(2,1)}), bf16[8,64,512]{2,1,0:T(8,128)(2,1)S(1)}, u32[]{:S(2)}, u32[]{:S(2)}) async-start(bf16[8,64,512]{2,1,0:T(8,128)(2,1)} %project.1), calls=%async_computation.3 | async-start | bytes 1048576 | tf_op jit(solution)/shard_map/all_to_all | solution.py:434
  100.9 14.6 %all-to-all-done.3 = bf16[8,64,512]{2,1,0:T(8,128)(2,1)S(1)} async-done(((bf16[8,64,512]{2,1,0:T(8,128)(2,1)}), bf16[8,64,512]{2,1,0:T(8,128)(2,1)S(1)}, u32[]{:S(2)}, u32[]{:S(2)}) %all-to-all-start.3) | async-done | bytes 524320 | tf_op jit(solution)/shard_map/all_to_all | solution.py:434
  115.5 0.1 convert_reduce_fusion
  115.5 0.7 select_convert_fusion
  (8 shorter events, 0.1 us)
Async XLA Ops:
  0.0 11.3 %copy-start.2 = (bf16[64,512]{1,0:T(8,128)(2,1)S(1)}, bf16[64,512]{1,0:T(8,128)(2,1)}, u32[]{:S(2)}) copy-start(bf16[64,512]{1,0:T(8,128)(2,1)} %resp_ref.1) | copy-start | bytes 196612
  0.0 11.2 %copy-start.5 = (bf16[8192]{0:T(1024)(128)(2,1)S(1)}, bf16[8192]{0:T(1024)(128)(2,1)}, u32[]{:S(2)}) copy-start(bf16[8192]{0:T(1024)(128)(2,1)} %param.11) | copy-start | bytes 49156
  0.0 11.3 %copy-start.3 = (bf16[256,512]{1,0:T(8,128)(2,1)S(1)}, bf16[256,512]{1,0:T(8,128)(2,1)}, u32[]{:S(2)}) copy-start(bf16[256,512]{1,0:T(8,128)(2,1)} %prompt_ref.1) | copy-start | bytes 786436
  2.1 37.2 %all-to-all-start = ((bf16[8,128,512]{2,1,0:T(8,128)(2,1)}), bf16[8,128,512]{2,1,0:T(8,128)(2,1)S(1)}, u32[]{:S(2)}, u32[]{:S(2)}) async-start(bf16[8,128,512]{2,1,0:T(8,128)(2,1)} %pack.1), calls=%async_computation | async-start | bytes 2097152 | tf_op jit(solution)/shard_map/all_to_all | solution.py:434
  12.3 11.1 %collective-permute-start = (bf16[336,512]{1,0:T(8,128)(2,1)S(1)}, bf16[336,512]{1,0:T(8,128)(2,1)}, u32[]{:S(2)}, u32[]{:S(2)}) collective-permute-start(bf16[336,512]{1,0:T(8,128)(2,1)S(1)} %scale_rows.1.refs_0_.after_ref), channel_id=1, source_target_pairs={{0,1},{1,0},{2,3},{3,2},{4,5},{5,4},{6,7},{7,6},{8,9},{9,8},{10,11... | collective-permute-start | bytes 1032200 | tf_op jit(solution)/shard_map/ppermute | solution.py:476
  12.8 11.2 %collective-permute-start.1 = (bf16[336,512]{1,0:T(8,128)(2,1)S(1)}, bf16[336,512]{1,0:T(8,128)(2,1)S(1)}, u32[]{:S(2)}, u32[]{:S(2)}) collective-permute-start(bf16[336,512]{1,0:T(8,128)(2,1)S(1)} %scale_rows.1.refs_0_.after_ref), channel_id=1, source_target_pairs={{0,16},{16,0},{1,17},{17,1},{2,18},{18,2},{3,19},{19,3},{4,20},{20... | collective-permute-start | bytes 1032200 | tf_op jit(solution)/shard_map/ppermute | solution.py:477
  12.8 2.2 %copy-start = (bf16[256,8192]{1,0:T(8,128)(2,1)S(1)}, bf16[256,8192]{1,0:T(8,128)(2,1)}, u32[]{:S(2)}) copy-start(bf16[256,8192]{1,0:T(8,128)(2,1)} %weight_ref.5) | copy-start | bytes 12582916
  16.5 16.6 %collective-permute-start.3 = (bf16[256,1024]{1,0:T(8,128)(2,1)}, bf16[256,1024]{1,0:T(8,128)(2,1)S(1)}, u32[]{:S(2)}, u32[]{:S(2)}) collective-permute-start(bf16[256,1024]{1,0:T(8,128)(2,1)} %get-tuple-element.11), channel_id=1, source_target_pairs={{0,1},{1,0},{2,3},{3,2},{4,5},{5,4},{6,7},{7,6},{8,9},{9,8},{10,11... | collective-permute-start | bytes 1572872 | tf_op jit(solution)/shard_map/ppermute | solution.py:479
  23.4 9.7 %collective-permute-start.2 = (bf16[336,512]{1,0:T(8,128)(2,1)}, bf16[336,512]{1,0:T(8,128)(2,1)S(1)}, u32[]{:S(2)}, u32[]{:S(2)}) collective-permute-start(bf16[336,512]{1,0:T(8,128)(2,1)} %collective-permute-done.refs_1_), channel_id=1, source_target_pairs={{0,16},{16,0},{1,17},{17,1},{2,18},{18,2},{3,19},{19,3},{4,20},{20... | collective-permute-start | bytes 1032200 | tf_op jit(solution)/shard_map/ppermute | solution.py:477
  40.1 14.2 %collective-permute-start.4 = (bf16[8,64,512]{2,1,0:T(8,128)(2,1)}, bf16[8,64,512]{2,1,0:T(8,128)(2,1)}, u32[]{:S(2)}, u32[]{:S(2)}) collective-permute-start(bf16[8,64,512]{2,1,0:T(8,128)(2,1)} %split.1.own_ref), channel_id=1, source_target_pairs={{0,1},{1,0},{2,3},{3,2},{4,5},{5,4},{6,7},{7,6},{8,9},{9,8},{10,11... | collective-permute-start | bytes 1572872 | tf_op jit(solution)/shard_map/ppermute | solution.py:481
  43.2 17.5 %all-to-all-start.1 = ((bf16[8,176,128]{2,1,0:T(8,128)(2,1)}), bf16[8,176,128]{2,1,0:T(8,128)(2,1)S(1)}, u32[]{:S(2)}, u32[]{:S(2)}) async-start(bf16[8,176,128]{2,1,0:T(8,128)(2,1)} %partial_products.1), calls=%async_computation.1 | async-start | bytes 720896 | tf_op jit(solution)/shard_map/all_to_all | solution.py:434
  54.3 2.2 %copy-start.4 = (bf16[8192,256]{1,0:T(8,128)(2,1)S(1)}, bf16[8192,256]{1,0:T(8,128)(2,1)}, u32[]{:S(2)}) copy-start(bf16[8192,256]{1,0:T(8,128)(2,1)} %weight_ref.4) | copy-start | bytes 12582916
  62.1 15.6 %all-to-all-start.2 = ((bf16[16,144,128]{2,1,0:T(8,128)(2,1)}), bf16[16,144,128]{2,1,0:T(8,128)(2,1)S(1)}, u32[]{:S(2)}, u32[]{:S(2)}) async-start(bf16[16,144,128]{2,1,0:T(8,128)(2,1)} %finish_keys.1), calls=%async_computation.2 | async-start | bytes 1179648 | tf_op jit(solution)/shard_map/all_to_all | solution.py:434
  67.6 19.2 %collective-permute-start.12 = (bf16[256,1024]{1,0:T(8,128)(2,1)S(1)}, bf16[256,1024]{1,0:T(8,128)(2,1)S(1)}, u32[]{:S(2)}, u32[]{:S(2)}) collective-permute-start(bf16[256,1024]{1,0:T(8,128)(2,1)S(1)} %get-tuple-element.12.refs_3_), channel_id=1, source_target_pairs={{0,1},{1,0},{2,3},{3,2},{4,5},{5,4},{6,7},{7,6},{8,9},{9,8},{10,11... | collective-permute-start | bytes 1572872 | tf_op jit(solution)/shard_map/ppermute | solution.py:479
  67.8 5.8 %collective-permute-start.5 = (bf16[64,256]{1,0:T(8,128)(2,1)S(1)}, bf16[64,256]{1,0:T(8,128)(2,1)S(1)}, u32[]{:S(2)}, u32[]{:S(2)}) collective-permute-start(bf16[64,256]{1,0:T(8,128)(2,1)S(1)} %queries.1.refs_0_), channel_id=1, source_target_pairs={{0,32},{32,64},{64,96},{96,0},{1,33},{33,65},{65,97},{97,1},{2,34}... | collective-permute-start | bytes 98312 | tf_op jit(solution)/shard_map/ppermute | solution.py:490
  69.4 5.4 %collective-permute-start.6 = (bf16[64,256]{1,0:T(8,128)(2,1)S(1)}, bf16[64,256]{1,0:T(8,128)(2,1)S(1)}, u32[]{:S(2)}, u32[]{:S(2)}) collective-permute-start(bf16[64,256]{1,0:T(8,128)(2,1)S(1)} %queries.1.refs_0_), channel_id=1, source_target_pairs={{0,64},{32,96},{64,0},{96,32},{1,65},{33,97},{65,1},{97,33},{2,66}... | collective-permute-start | bytes 98312 | tf_op jit(solution)/shard_map/ppermute | solution.py:490
  72.3 3.9 %collective-permute-start.7 = (bf16[64,256]{1,0:T(8,128)(2,1)S(1)}, bf16[64,256]{1,0:T(8,128)(2,1)S(1)}, u32[]{:S(2)}, u32[]{:S(2)}) collective-permute-start(bf16[64,256]{1,0:T(8,128)(2,1)S(1)} %queries.1.refs_0_), channel_id=1, source_target_pairs={{0,96},{32,0},{64,32},{96,64},{1,97},{33,1},{65,33},{97,65},{2,98}... | collective-permute-start | bytes 98312 | tf_op jit(solution)/shard_map/ppermute | solution.py:490
  80.2 6.5 %collective-permute-start.8 = (bf16[64,384]{1,0:T(8,128)(2,1)S(1)}, bf16[64,384]{1,0:T(8,128)(2,1)S(1)}, u32[]{:S(2)}, u32[]{:S(2)}) collective-permute-start(bf16[64,384]{1,0:T(8,128)(2,1)S(1)} %get-tuple-element.13), channel_id=1, source_target_pairs={{0,64},{32,96},{64,0},{96,32},{1,65},{33,97},{65,1},{97,33},{2,66}... | collective-permute-start | bytes 147464 | tf_op jit(solution)/shard_map/ppermute | solution.py:490
  83.5 4.1 %collective-permute-start.9 = (bf16[64,384]{1,0:T(8,128)(2,1)S(1)}, bf16[64,384]{1,0:T(8,128)(2,1)S(1)}, u32[]{:S(2)}, u32[]{:S(2)}) collective-permute-start(bf16[64,384]{1,0:T(8,128)(2,1)S(1)} %get-tuple-element.14), channel_id=1, source_target_pairs={{0,96},{32,0},{64,32},{96,64},{1,97},{33,1},{65,33},{97,65},{2,98}... | collective-permute-start | bytes 147464 | tf_op jit(solution)/shard_map/ppermute | solution.py:490
  84.6 5.3 %collective-permute-start.10 = (bf16[64,384]{1,0:T(8,128)(2,1)S(1)}, bf16[64,384]{1,0:T(8,128)(2,1)S(1)}, u32[]{:S(2)}, u32[]{:S(2)}) collective-permute-start(bf16[64,384]{1,0:T(8,128)(2,1)S(1)} %get-tuple-element.15), channel_id=1, source_target_pairs={{0,32},{32,64},{64,96},{96,0},{1,33},{33,65},{65,97},{97,1},{2,34}... | collective-permute-start | bytes 147464 | tf_op jit(solution)/shard_map/ppermute | solution.py:490
  85.5 9.4 %collective-permute-start.13 = (bf16[256,1024]{1,0:T(8,128)(2,1)S(1)}, bf16[256,1024]{1,0:T(8,128)(2,1)S(1)}, u32[]{:S(2)}, u32[]{:S(2)}) collective-permute-start(bf16[256,1024]{1,0:T(8,128)(2,1)S(1)} %collective-permute-done.3.refs_2_.refs_0_), channel_id=1, source_target_pairs={{0,16},{16,0},{1,17},{17,1},{2,18},{18,2},{3,19},{19,3},{4,20},{20... | collective-permute-start | bytes 1572872 | tf_op jit(solution)/shard_map/ppermute | solution.py:485
  86.8 8.1 %collective-permute-start.14 = (bf16[256,1024]{1,0:T(8,128)(2,1)S(1)}, bf16[256,1024]{1,0:T(8,128)(2,1)S(1)}, u32[]{:S(2)}, u32[]{:S(2)}) collective-permute-start(bf16[256,1024]{1,0:T(8,128)(2,1)S(1)} %collective-permute-done.12.refs_1_), channel_id=1, source_target_pairs={{0,16},{16,0},{1,17},{17,1},{2,18},{18,2},{3,19},{19,3},{4,20},{20... | collective-permute-start | bytes 1572872 | tf_op jit(solution)/shard_map/ppermute | solution.py:485
  90.2 4.8 %collective-permute-start.11 = (bf16[64,256]{1,0:T(8,128)(2,1)S(1)}, bf16[64,256]{1,0:T(8,128)(2,1)S(1)}, u32[]{:S(2)}, u32[]{:S(2)}) collective-permute-start(bf16[64,256]{1,0:T(8,128)(2,1)S(1)} %merge.1.own_ref), channel_id=1, source_target_pairs={{0,1},{1,0},{2,3},{3,2},{4,5},{5,4},{6,7},{7,6},{8,9},{9,8},{10,11... | collective-permute-start | bytes 98312 | tf_op jit(solution)/shard_map/ppermute | solution.py:496
  91.7 2.2 %copy-start.1 = (bf16[256,8192]{1,0:T(8,128)(2,1)S(1)}, bf16[256,8192]{1,0:T(8,128)(2,1)}, u32[]{:S(2)}) copy-start(bf16[256,8192]{1,0:T(8,128)(2,1)} %weight_ref.5) | copy-start | bytes 12582916
  96.8 18.7 %all-to-all-start.3 = ((bf16[8,64,512]{2,1,0:T(8,128)(2,1)}), bf16[8,64,512]{2,1,0:T(8,128)(2,1)S(1)}, u32[]{:S(2)}, u32[]{:S(2)}) async-start(bf16[8,64,512]{2,1,0:T(8,128)(2,1)} %project.1), calls=%async_computation.3 | async-start | bytes 1048576 | tf_op jit(solution)/shard_map/all_to_all | solution.py:434

commit v7 on v5

--- a/solution.py
+++ b/solution.py
@@ -337,7 +337,7 @@
 
 
 def merge_kernel(*refs):
-    parts, out_ref = refs[:4], refs[4]
+    parts, out_ref = refs[:4], refs[-1]
     lane = iota((RESP, 128), 1)
     row, col = iota((128, 128), 0), iota((128, 128), 1)
     order = jnp.where(row == by_device(col), 1.0, 0.0).astype(BF16)
@@ -354,37 +354,56 @@
         out_ref[:, head] = dot(mean, order).astype(BF16)
 
 
-def merge(parts):
+def merge(parts, after):
     vmem = pl.BlockSpec(memory_space=pltpu.VMEM)
     return pl.pallas_call(
         merge_kernel,
-        in_specs=[vmem] * 4,
+        in_specs=[vmem] * 5,
         out_shape=jax.ShapeDtypeStruct((RESP, 256), BF16),
         compiler_params=params(SMALL),
         name="merge",
-    )(*parts)
+    )(*parts, after)
 
 
 def z_of(i, info):
     return (4 * info[CORE_AT]) ^ i
 
 
-def project_own_kernel(info_ref, own_ref, weight_ref, out_ref):
+def near_kernel(info_ref, weight_ref, after_ref, *out_refs):
     for i in range(8):
         at = (2 * z_of(i, info_ref) + info_ref[XL_AT]) * BLOCK
-        out_ref[i] = dot(own_ref[...], weight_ref[:, pl.ds(pl.multiple_of(at, BLOCK), BLOCK)])
-
-
-def project_own(info, own, weight):
+        columns = weight_ref[:, pl.ds(pl.multiple_of(at, BLOCK), BLOCK)]
+        out_refs[i // 2][:, (i % 2) * BLOCK : (i % 2) * BLOCK + BLOCK] = columns
+
+
+def near_columns(info, weight, after):
+    vmem = pl.BlockSpec(memory_space=pltpu.VMEM)
+    return pl.pallas_call(
+        near_kernel,
+        in_specs=[pl.BlockSpec(memory_space=pltpu.SMEM)] + [vmem] * 2,
+        out_shape=(jax.ShapeDtypeStruct((256, 2 * BLOCK), BF16),) * 4,
+        compiler_params=params(SMALL),
+        cost_estimate=LONG,
+        name="near_columns",
+    )(info, weight, after)
+
+
+def project_own_kernel(own_ref, *refs):
+    weights, out_ref = refs[:4], refs[4]
+    for i in range(8):
+        out_ref[i] = dot(own_ref[...], weights[i // 2][:, pl.ds((i % 2) * BLOCK, BLOCK)])
+
+
+def project_own(own, weights):
     vmem = pl.BlockSpec(memory_space=pltpu.VMEM)
     return pl.pallas_call(
         project_own_kernel,
-        in_specs=[pl.BlockSpec(memory_space=pltpu.SMEM)] + [vmem] * 2,
+        in_specs=[vmem] * 5,
         out_shape=jax.ShapeDtypeStruct((8, RESP, BLOCK), F32),
         compiler_params=params(SMALL),
         cost_estimate=LONG,
         name="project_own",
-    )(info, own, weight)
+    )(own, *weights)
 
 
 def project_kernel(info_ref, started_ref, other_ref, *refs):
@@ -484,9 +503,10 @@
 
     pooled = [queries] + [along(queries, step) for step in (1, 2, 3)]
     parts = attend(info, rows, pooled)
-    attention = merge([parts[0]] + [along(parts[step], -step) for step in (1, 2, 3)])
+    near = near_columns(info, output_weight, parts[0])
+    attention = merge([parts[0]] + [along(parts[step], -step) for step in (1, 2, 3)], near[0])
     partner = lax.ppermute(attention, "xl", flip)
-    partial = project(info, project_own(info, attention, output_weight), partner, cross)
+    partial = project(info, project_own(attention, near), partner, cross)
     summed = jnp.sum(swap(partial, ZRING).astype(F32), axis=0)
     live = jnp.arange(RESP, dtype=jnp.int32) < response_lengths[0]
     return jnp.where(live[:, None], summed, 0.0).astype(BF16)

time: 117 us -> 127 us (1.085)
  waiting for transfers between devices: 53.7 us -> 62.7 us
    ppermute x2, waiting for transfers between devices: 10.8 us -> 22.1 us  [body(): early, late = (lax.ppermute(piece, 'xl', flip) for piece in sent)]
    ppermute x6, waiting for transfers between devices: 5.23 us -> 1.92 us  [along(): return lax.ppermute(values, 'y', [(i, (i + step) % 4) for i in range(4)])]
    ppermute x1, waiting for transfers between devices: 0.01 us -> 1.73 us  [body(): partner = lax.ppermute(attention, 'xl', flip)]
  transfers between devices with their start and end apart: 19 -> 19, of which waited for: 12 -> 10; matrix products, arithmetic and copies ran while one was open for 1% -> 1% of each run, Pallas kernels for 10% -> 9%
where the time goes in v7:
time: 127 us; the launch traced here: 126 us
  waiting for transfers between devices  62.7 us (49%)
  starting transfers between devices  36.1 us (28%)
  Pallas kernels  17.2 us (14%)
  local copies, waits for them, and re-layouts  6.66 us (5%)
  between operations  1.48 us (1%)
  other arithmetic  1.46 us (1%)
    all_to_all x4, waiting for transfers between devices, swap(): return lax.all_to_all(values, axis, 0, 0, tiled=False)  23.9 us
    ppermute x2, waiting for transfers between devices, body(): early, late = (lax.ppermute(piece, 'xl', flip) for piece in sent)  22.1 us
    all_to_all x4, starting transfers between devices, swap(): return lax.all_to_all(values, axis, 0, 0, tiled=False)  20.9 us
    ppermute x6, starting transfers between devices, along(): return lax.ppermute(values, 'y', [(i, (i + step) % 4) for i in range(4)])  10.7 us
    ppermute x1, waiting for transfers between devices, body(): other_hidden = lax.ppermute(own_hidden, 'xl', flip)  7.67 us
    unnamed x12, local copies, waits for them, and re-layouts  6.57 us
    ppermute x1, waiting for transfers between devices, body(): beside = lax.ppermute(scaled, 'xl', flip)  5.39 us
    pallas_call x1, Pallas kernels, attend(): pl.pallas_call(attend_kernel, in_specs=[pl.BlockSpec(memory_space=pltpu.S...  2.54 us
  transfers between devices with their start and end apart: 19, of which 10 were waited for; matrix products, arithmetic and copies ran while one was open for 1% of the time, Pallas kernels for 9%

profile of v7, /device:TPU:2, one launch (start us, length us, event | category | flops | bytes accessed | tf_op | source)
XLA Modules:
  0.0 125.7 jit_solution(2468427598602420218)
XLA Ops:
  0.0 0.0 copy-start.2
  0.0 0.0 copy-start.5
  0.0 0.0 copy-start.3
  0.0 2.1 %pack.1 = bf16[8,128,512]{2,1,0:T(8,128)(2,1)} custom-call(s32[1]{0:T(128)} %bitcast.1.core_ref, bf16[32,8192]{1,0:T(8,128)(2,1)} %bitcast.15, bf16[32,8192]{1,0:T(8,128)(2,1)} %bitcast.16, bf16[64,512]{1,0:T(8,128)(2,1)} %resp_ref.1), custom_call_target="tpu_custom_call" | custom-call | tf_op jit(solution)/shard_map/pack/pallas_call | solution.py:69
  2.1 8.5 %all-to-all-start = ((bf16[8,128,512]{2,1,0:T(8,128)(2,1)}), bf16[8,128,512]{2,1,0:T(8,128)(2,1)S(1)}, u32[]{:S(2)}, u32[]{:S(2)}) async-start(bf16[8,128,512]{2,1,0:T(8,128)(2,1)} %pack.1), calls=%async_computation | async-start | bytes 2097152 | tf_op jit(solution)/shard_map/all_to_all | solution.py:446
  11.2 0.0 copy-done.5
  11.2 0.1 stack.28.info_ref
  11.3 0.0 copy-done.2
  11.3 0.0 copy-done.3
  11.3 1.0 scale_rows.1.refs_0_.after_ref
  12.3 0.6 collective-permute-start
  12.8 0.0 collective-permute-start.1
  12.8 0.0 copy-start
  12.8 2.2 %copy-done = bf16[256,8192]{1,0:T(8,128)(2,1)S(1)} copy-done((bf16[256,8192]{1,0:T(8,128)(2,1)S(1)}, bf16[256,8192]{1,0:T(8,128)(2,1)}, u32[]{:S(2)}) %copy-start) | copy-done | bytes 4194328
  15.0 1.4 %pick_columns.1 = (bf16[256,1024]{1,0:T(8,128)(2,1)}, bf16[256,1024]{1,0:T(8,128)(2,1)S(1)}) custom-call(s32[6]{0:T(128)S(1)} %stack.28.info_ref, bf16[256,8192]{1,0:T(8,128)(2,1)S(1)} %copy-done, bf16[336,512]{1,0:T(8,128)(2,1)S(1)} %scale_rows.1.refs_0_.after_ref), custom_call_target="tpu_custom_call" | custom-call | tf_op jit(solution)/shard_map/pick_columns/pallas_call | solution.py:436
  16.5 1.5 %collective-permute-start.3 = (bf16[256,1024]{1,0:T(8,128)(2,1)}, bf16[256,1024]{1,0:T(8,128)(2,1)S(1)}, u32[]{:S(2)}, u32[]{:S(2)}) collective-permute-start(bf16[256,1024]{1,0:T(8,128)(2,1)} %get-tuple-element.15), channel_id=1, source_target_pairs={{0,1},{1,0},{2,3},{3,2},{4,5},{5,4},{6,7},{7,6},{8,9},{9,8},{10,11... | collective-permute-start | bytes 1572872 | tf_op jit(solution)/shard_map/ppermute | solution.py:491
  18.0 5.4 %collective-permute-done.refs_1_ = bf16[336,512]{1,0:T(8,128)(2,1)} collective-permute-done((bf16[336,512]{1,0:T(8,128)(2,1)S(1)}, bf16[336,512]{1,0:T(8,128)(2,1)}, u32[]{:S(2)}, u32[]{:S(2)}) %collective-permute-start) | collective-permute-done | bytes 344096 | tf_op jit(solution)/shard_map/ppermute | solution.py:488
  23.4 0.0 collective-permute-start.2
  23.4 0.6 fusion.11
  24.0 0.0 collective-permute-done.1.refs_2_.refs_0_
  24.1 9.0 %collective-permute-done.3.refs_2_.refs_0_ = bf16[256,1024]{1,0:T(8,128)(2,1)S(1)} collective-permute-done((bf16[256,1024]{1,0:T(8,128)(2,1)}, bf16[256,1024]{1,0:T(8,128)(2,1)S(1)}, u32[]{:S(2)}, u32[]{:S(2)}) %collective-permute-start.3) | collective-permute-done | bytes 524320 | tf_op jit(solution)/shard_map/ppermute | solution.py:491
  33.0 0.0 collective-permute-done.2.refs_3_.refs_1_
  33.1 6.2 %all-to-all-done.got_ref = bf16[8,128,512]{2,1,0:T(8,128)(2,1)S(1)} async-done(((bf16[8,128,512]{2,1,0:T(8,128)(2,1)}), bf16[8,128,512]{2,1,0:T(8,128)(2,1)S(1)}, u32[]{:S(2)}, u32[]{:S(2)}) %all-to-all-start) | async-done | bytes 1048608 | tf_op jit(solution)/shard_map/all_to_all | solution.py:446
  39.3 0.8 split.1.own_ref
  40.1 0.5 collective-permute-start.4
  40.6 2.5 %partial_products.1 = bf16[8,176,128]{2,1,0:T(8,128)(2,1)} custom-call(s32[6]{0:T(128)S(1)} %stack.28.info_ref, bf16[8,128,512]{2,1,0:T(8,128)(2,1)S(1)} %all-to-all-done.got_ref, bf16[336,512]{1,0:T(8,128)(2,1)S(1)} %scale_rows.1.refs_0_.after_ref, bf16[336,512]{1,0:T(8,128)(2,1)} %collective-permute-done.refs_1_, ...), custom_call_target="tpu_custom_call" | custom-call | tf_op jit(solution)/shard_map/partial_products/pallas_call | solution.py:162
  43.1 3.4 %all-to-all-start.1 = ((bf16[8,176,128]{2,1,0:T(8,128)(2,1)}), bf16[8,176,128]{2,1,0:T(8,128)(2,1)S(1)}, u32[]{:S(2)}, u32[]{:S(2)}) async-start(bf16[8,176,128]{2,1,0:T(8,128)(2,1)} %partial_products.1), calls=%async_computation.1 | async-start | bytes 720896 | tf_op jit(solution)/shard_map/all_to_all | solution.py:446
  46.6 7.7 %collective-permute-done.4.other_ref = bf16[8,64,512]{2,1,0:T(8,128)(2,1)} collective-permute-done((bf16[8,64,512]{2,1,0:T(8,128)(2,1)}, bf16[8,64,512]{2,1,0:T(8,128)(2,1)}, u32[]{:S(2)}, u32[]{:S(2)}) %collective-permute-start.4) | collective-permute-done | bytes 524320 | tf_op jit(solution)/shard_map/ppermute | solution.py:493
  54.3 2.2 %copy-done.4 = bf16[8192,256]{1,0:T(8,128)(2,1)S(1)} copy-done((bf16[8192,256]{1,0:T(8,128)(2,1)S(1)}, bf16[8192,256]{1,0:T(8,128)(2,1)}, u32[]{:S(2)}) %copy-start.4) | copy-done | bytes 4194328
  56.5 2.3 %queries.1.refs_0_ = bf16[64,256]{1,0:T(8,128)(2,1)S(1)} custom-call(s32[6]{0:T(128)S(1)} %stack.28.info_ref, f32[16,1,512]{2,1,0:T(1,128)S(1)} %bitcast.14, f32[2,224,128]{2,1,0:T(8,128)S(1)} %pad_maximum_fusion.refs_4_.trig_ref, bf16[8192,256]{1,0:T(8,128)(2,1)S(1)} %copy-done.4, bf16[8,64,512]{2,1,0:T(8,128)(2,1)} %split.1.own_ref, ...), custom_call_target="tpu_custom_call" | custom-call | flops 30000001024 | bytes 1000000 | tf_op jit(solution)/shard_map/queries/pallas_call | solution.py:245
  58.8 1.9 %all-to-all-done.1.parts_ref = bf16[8,176,128]{2,1,0:T(8,128)(2,1)S(1)} async-done(((bf16[8,176,128]{2,1,0:T(8,128)(2,1)}), bf16[8,176,128]{2,1,0:T(8,128)(2,1)S(1)}, u32[]{:S(2)}, u32[]{:S(2)}) %all-to-all-start.1) | async-done | bytes 360480 | tf_op jit(solution)/shard_map/all_to_all | solution.py:446
  60.7 1.3 finish_keys.1
  61.9 5.5 %all-to-all-start.2 = ((bf16[16,144,128]{2,1,0:T(8,128)(2,1)}), bf16[16,144,128]{2,1,0:T(8,128)(2,1)S(1)}, u32[]{:S(2)}, u32[]{:S(2)}) async-start(bf16[16,144,128]{2,1,0:T(8,128)(2,1)} %finish_keys.1), calls=%async_computation.2 | async-start | bytes 1179648 | tf_op jit(solution)/shard_map/all_to_all | solution.py:446
  67.5 0.2 collective-permute-start.12
  67.6 1.6 %collective-permute-start.5 = (bf16[64,256]{1,0:T(8,128)(2,1)S(1)}, bf16[64,256]{1,0:T(8,128)(2,1)S(1)}, u32[]{:S(2)}, u32[]{:S(2)}) collective-permute-start(bf16[64,256]{1,0:T(8,128)(2,1)S(1)} %queries.1.refs_0_), channel_id=1, source_target_pairs={{0,32},{32,64},{64,96},{96,0},{1,33},{33,65},{65,97},{97,1},{2,34}... | collective-permute-start | bytes 98312 | tf_op jit(solution)/shard_map/ppermute | solution.py:502
  69.2 2.9 %collective-permute-start.6 = (bf16[64,256]{1,0:T(8,128)(2,1)S(1)}, bf16[64,256]{1,0:T(8,128)(2,1)S(1)}, u32[]{:S(2)}, u32[]{:S(2)}) collective-permute-start(bf16[64,256]{1,0:T(8,128)(2,1)S(1)} %queries.1.refs_0_), channel_id=1, source_target_pairs={{0,64},{32,96},{64,0},{96,32},{1,65},{33,97},{65,1},{97,33},{2,66}... | collective-permute-start | bytes 98312 | tf_op jit(solution)/shard_map/ppermute | solution.py:502
  72.1 1.3 %collective-permute-start.7 = (bf16[64,256]{1,0:T(8,128)(2,1)S(1)}, bf16[64,256]{1,0:T(8,128)(2,1)S(1)}, u32[]{:S(2)}, u32[]{:S(2)}) collective-permute-start(bf16[64,256]{1,0:T(8,128)(2,1)S(1)} %queries.1.refs_0_), channel_id=1, source_target_pairs={{0,96},{32,0},{64,32},{96,64},{1,97},{33,1},{65,33},{97,65},{2,98}... | collective-permute-start | bytes 98312 | tf_op jit(solution)/shard_map/ppermute | solution.py:502
  73.5 0.0 collective-permute-start.13
  73.5 13.1 %collective-permute-done.12.refs_1_ = bf16[256,1024]{1,0:T(8,128)(2,1)S(1)} collective-permute-done((bf16[256,1024]{1,0:T(8,128)(2,1)S(1)}, bf16[256,1024]{1,0:T(8,128)(2,1)S(1)}, u32[]{:S(2)}, u32[]{:S(2)}) %collective-permute-start.12) | collective-permute-done | bytes 524320 | tf_op jit(solution)/shard_map/ppermute | solution.py:491
  86.6 0.0 collective-permute-start.14
  86.6 0.0 collective-permute-done.5.refs_1_
  86.6 0.0 collective-permute-done.6.refs_2_
  86.6 0.0 collective-permute-done.7.refs_3_
  86.6 0.0 all-to-all-done.2.rows_ref
  86.6 2.5 %attend.1 = (bf16[64,384]{1,0:T(8,128)(2,1)S(1)}, bf16[64,384]{1,0:T(8,128)(2,1)S(1)}, bf16[64,384]{1,0:T(8,128)(2,1)S(1)}, bf16[64,384]{1,0:T(8,128)(2,1)S(1)}) custom-call(s32[6]{0:T(128)S(1)} %stack.28.info_ref, bf16[16,144,128]{2,1,0:T(8,128)(2,1)S(1)} %all-to-all-done.2.rows_ref, bf16[64,256]{1,0:T(8,128)(2,1)S(1)} %queries.1.refs_0_, ...), custom_call_target="tpu_custom_call" | custom-call | tf_op jit(solution)/shard_map/attend/pallas_call | solution.py:330
  89.2 3.3 %collective-permute-start.8 = (bf16[64,384]{1,0:T(8,128)(2,1)S(1)}, bf16[64,384]{1,0:T(8,128)(2,1)S(1)}, u32[]{:S(2)}, u32[]{:S(2)}) collective-permute-start(bf16[64,384]{1,0:T(8,128)(2,1)S(1)} %get-tuple-element.18), channel_id=1, source_target_pairs={{0,96},{32,0},{64,32},{96,64},{1,97},{33,1},{65,33},{97,65},{2,98}... | collective-permute-start | bytes 147464 | tf_op jit(solution)/shard_map/ppermute | solution.py:502
  92.5 0.6 collective-permute-start.9
  93.1 1.0 collective-permute-start.10
  94.1 2.2 %copy-done.1 = bf16[256,8192]{1,0:T(8,128)(2,1)S(1)} copy-done((bf16[256,8192]{1,0:T(8,128)(2,1)S(1)}, bf16[256,8192]{1,0:T(8,128)(2,1)}, u32[]{:S(2)}) %copy-start.1) | copy-done | bytes 4194328
  96.3 0.7 near_columns.1
  97.0 0.0 collective-permute-done.8.refs_1_
  97.0 1.4 %collective-permute-done.9.refs_2_ = bf16[64,384]{1,0:T(8,128)(2,1)S(1)} collective-permute-done((bf16[64,384]{1,0:T(8,128)(2,1)S(1)}, bf16[64,384]{1,0:T(8,128)(2,1)S(1)}, u32[]{:S(2)}, u32[]{:S(2)}) %collective-permute-start.9) | collective-permute-done | bytes 49184 | tf_op jit(solution)/shard_map/ppermute | solution.py:502
  98.4 0.5 collective-permute-done.10.refs_3_
  98.9 0.3 merge.1.own_ref
  99.2 1.8 %collective-permute-start.11 = (bf16[64,256]{1,0:T(8,128)(2,1)S(1)}, bf16[64,256]{1,0:T(8,128)(2,1)S(1)}, u32[]{:S(2)}, u32[]{:S(2)}) collective-permute-start(bf16[64,256]{1,0:T(8,128)(2,1)S(1)} %merge.1.own_ref), channel_id=1, source_target_pairs={{0,1},{1,0},{2,3},{3,2},{4,5},{5,4},{6,7},{7,6},{8,9},{9,8},{10,11... | collective-permute-start | bytes 98312 | tf_op jit(solution)/shard_map/ppermute | solution.py:508
  100.9 0.5 project_own.1.started_ref
  101.4 0.0 collective-permute-done.13.refs_2_
  101.4 0.0 collective-permute-done.14.refs_3_
  101.4 1.7 %collective-permute-done.11.other_ref = bf16[64,256]{1,0:T(8,128)(2,1)S(1)} collective-permute-done((bf16[64,256]{1,0:T(8,128)(2,1)S(1)}, bf16[64,256]{1,0:T(8,128)(2,1)S(1)}, u32[]{:S(2)}, u32[]{:S(2)}) %collective-permute-start.11) | collective-permute-done | bytes 32800 | tf_op jit(solution)/shard_map/ppermute | solution.py:508
  103.2 1.8 %project.1 = bf16[8,64,512]{2,1,0:T(8,128)(2,1)} custom-call(s32[6]{0:T(128)S(1)} %stack.28.info_ref, f32[8,64,512]{2,1,0:T(8,128)S(1)} %project_own.1.started_ref, bf16[64,256]{1,0:T(8,128)(2,1)S(1)} %collective-permute-done.11.other_ref, bf16[256,1024]{1,0:T(8,128)(2,1)S(1)} %collective-permute-done.3.refs_2_.refs_0_, ...), custom_call_target="tpu_custom_call" | custom-call | tf_op jit(solution)/shard_map/project/pallas_call | solution.py:418
  105.0 3.5 %all-to-all-start.3 = ((bf16[8,64,512]{2,1,0:T(8,128)(2,1)}), bf16[8,64,512]{2,1,0:T(8,128)(2,1)S(1)}, u32[]{:S(2)}, u32[]{:S(2)}) async-start(bf16[8,64,512]{2,1,0:T(8,128)(2,1)} %project.1), calls=%async_computation.3 | async-start | bytes 1048576 | tf_op jit(solution)/shard_map/all_to_all | solution.py:446
  109.2 15.8 %all-to-all-done.3 = bf16[8,64,512]{2,1,0:T(8,128)(2,1)S(1)} async-done(((bf16[8,64,512]{2,1,0:T(8,128)(2,1)}), bf16[8,64,512]{2,1,0:T(8,128)(2,1)S(1)}, u32[]{:S(2)}, u32[]{:S(2)}) %all-to-all-start.3) | async-done | bytes 524320 | tf_op jit(solution)/shard_map/all_to_all | solution.py:446
  124.9 0.1 convert_reduce_fusion
  125.0 0.7 select_convert_fusion
  (9 shorter events, 0.1 us)
Async XLA Ops:
  0.0 11.3 %copy-start.2 = (bf16[64,512]{1,0:T(8,128)(2,1)S(1)}, bf16[64,512]{1,0:T(8,128)(2,1)}, u32[]{:S(2)}) copy-start(bf16[64,512]{1,0:T(8,128)(2,1)} %resp_ref.1) | copy-start | bytes 196612
  0.0 11.2 %copy-start.5 = (bf16[8192]{0:T(1024)(128)(2,1)S(1)}, bf16[8192]{0:T(1024)(128)(2,1)}, u32[]{:S(2)}) copy-start(bf16[8192]{0:T(1024)(128)(2,1)} %param.11) | copy-start | bytes 49156
  0.0 11.3 %copy-start.3 = (bf16[256,512]{1,0:T(8,128)(2,1)S(1)}, bf16[256,512]{1,0:T(8,128)(2,1)}, u32[]{:S(2)}) copy-start(bf16[256,512]{1,0:T(8,128)(2,1)} %prompt_ref.1) | copy-start | bytes 786436
  2.1 37.2 %all-to-all-start = ((bf16[8,128,512]{2,1,0:T(8,128)(2,1)}), bf16[8,128,512]{2,1,0:T(8,128)(2,1)S(1)}, u32[]{:S(2)}, u32[]{:S(2)}) async-start(bf16[8,128,512]{2,1,0:T(8,128)(2,1)} %pack.1), calls=%async_computation | async-start | bytes 2097152 | tf_op jit(solution)/shard_map/all_to_all | solution.py:446
  12.3 11.1 %collective-permute-start = (bf16[336,512]{1,0:T(8,128)(2,1)S(1)}, bf16[336,512]{1,0:T(8,128)(2,1)}, u32[]{:S(2)}, u32[]{:S(2)}) collective-permute-start(bf16[336,512]{1,0:T(8,128)(2,1)S(1)} %scale_rows.1.refs_0_.after_ref), channel_id=1, source_target_pairs={{0,1},{1,0},{2,3},{3,2},{4,5},{5,4},{6,7},{7,6},{8,9},{9,8},{10,11... | collective-permute-start | bytes 1032200 | tf_op jit(solution)/shard_map/ppermute | solution.py:488
  12.8 11.2 %collective-permute-start.1 = (bf16[336,512]{1,0:T(8,128)(2,1)S(1)}, bf16[336,512]{1,0:T(8,128)(2,1)S(1)}, u32[]{:S(2)}, u32[]{:S(2)}) collective-permute-start(bf16[336,512]{1,0:T(8,128)(2,1)S(1)} %scale_rows.1.refs_0_.after_ref), channel_id=1, source_target_pairs={{0,16},{16,0},{1,17},{17,1},{2,18},{18,2},{3,19},{19,3},{4,20},{20... | collective-permute-start | bytes 1032200 | tf_op jit(solution)/shard_map/ppermute | solution.py:489
  12.8 2.2 %copy-start = (bf16[256,8192]{1,0:T(8,128)(2,1)S(1)}, bf16[256,8192]{1,0:T(8,128)(2,1)}, u32[]{:S(2)}) copy-start(bf16[256,8192]{1,0:T(8,128)(2,1)} %weight_ref.5) | copy-start | bytes 12582916
  16.5 16.6 %collective-permute-start.3 = (bf16[256,1024]{1,0:T(8,128)(2,1)}, bf16[256,1024]{1,0:T(8,128)(2,1)S(1)}, u32[]{:S(2)}, u32[]{:S(2)}) collective-permute-start(bf16[256,1024]{1,0:T(8,128)(2,1)} %get-tuple-element.15), channel_id=1, source_target_pairs={{0,1},{1,0},{2,3},{3,2},{4,5},{5,4},{6,7},{7,6},{8,9},{9,8},{10,11... | collective-permute-start | bytes 1572872 | tf_op jit(solution)/shard_map/ppermute | solution.py:491
  23.4 9.7 %collective-permute-start.2 = (bf16[336,512]{1,0:T(8,128)(2,1)}, bf16[336,512]{1,0:T(8,128)(2,1)S(1)}, u32[]{:S(2)}, u32[]{:S(2)}) collective-permute-start(bf16[336,512]{1,0:T(8,128)(2,1)} %collective-permute-done.refs_1_), channel_id=1, source_target_pairs={{0,16},{16,0},{1,17},{17,1},{2,18},{18,2},{3,19},{19,3},{4,20},{20... | collective-permute-start | bytes 1032200 | tf_op jit(solution)/shard_map/ppermute | solution.py:489
  40.1 14.2 %collective-permute-start.4 = (bf16[8,64,512]{2,1,0:T(8,128)(2,1)}, bf16[8,64,512]{2,1,0:T(8,128)(2,1)}, u32[]{:S(2)}, u32[]{:S(2)}) collective-permute-start(bf16[8,64,512]{2,1,0:T(8,128)(2,1)} %split.1.own_ref), channel_id=1, source_target_pairs={{0,1},{1,0},{2,3},{3,2},{4,5},{5,4},{6,7},{7,6},{8,9},{9,8},{10,11... | collective-permute-start | bytes 1572872 | tf_op jit(solution)/shard_map/ppermute | solution.py:493
  43.1 17.5 %all-to-all-start.1 = ((bf16[8,176,128]{2,1,0:T(8,128)(2,1)}), bf16[8,176,128]{2,1,0:T(8,128)(2,1)S(1)}, u32[]{:S(2)}, u32[]{:S(2)}) async-start(bf16[8,176,128]{2,1,0:T(8,128)(2,1)} %partial_products.1), calls=%async_computation.1 | async-start | bytes 720896 | tf_op jit(solution)/shard_map/all_to_all | solution.py:446
  54.3 2.2 %copy-start.4 = (bf16[8192,256]{1,0:T(8,128)(2,1)S(1)}, bf16[8192,256]{1,0:T(8,128)(2,1)}, u32[]{:S(2)}) copy-start(bf16[8192,256]{1,0:T(8,128)(2,1)} %weight_ref.4) | copy-start | bytes 12582916
  61.9 24.7 %all-to-all-start.2 = ((bf16[16,144,128]{2,1,0:T(8,128)(2,1)}), bf16[16,144,128]{2,1,0:T(8,128)(2,1)S(1)}, u32[]{:S(2)}, u32[]{:S(2)}) async-start(bf16[16,144,128]{2,1,0:T(8,128)(2,1)} %finish_keys.1), calls=%async_computation.2 | async-start | bytes 1179648 | tf_op jit(solution)/shard_map/all_to_all | solution.py:446
  67.5 19.2 %collective-permute-start.12 = (bf16[256,1024]{1,0:T(8,128)(2,1)S(1)}, bf16[256,1024]{1,0:T(8,128)(2,1)S(1)}, u32[]{:S(2)}, u32[]{:S(2)}) collective-permute-start(bf16[256,1024]{1,0:T(8,128)(2,1)S(1)} %get-tuple-element.16.refs_3_), channel_id=1, source_target_pairs={{0,1},{1,0},{2,3},{3,2},{4,5},{5,4},{6,7},{7,6},{8,9},{9,8},{10,11... | collective-permute-start | bytes 1572872 | tf_op jit(solution)/shard_map/ppermute | solution.py:491
  67.6 19.0 %collective-permute-start.5 = (bf16[64,256]{1,0:T(8,128)(2,1)S(1)}, bf16[64,256]{1,0:T(8,128)(2,1)S(1)}, u32[]{:S(2)}, u32[]{:S(2)}) collective-permute-start(bf16[64,256]{1,0:T(8,128)(2,1)S(1)} %queries.1.refs_0_), channel_id=1, source_target_pairs={{0,32},{32,64},{64,96},{96,0},{1,33},{33,65},{65,97},{97,1},{2,34}... | collective-permute-start | bytes 98312 | tf_op jit(solution)/shard_map/ppermute | solution.py:502
  69.2 17.4 %collective-permute-start.6 = (bf16[64,256]{1,0:T(8,128)(2,1)S(1)}, bf16[64,256]{1,0:T(8,128)(2,1)S(1)}, u32[]{:S(2)}, u32[]{:S(2)}) collective-permute-start(bf16[64,256]{1,0:T(8,128)(2,1)S(1)} %queries.1.refs_0_), channel_id=1, source_target_pairs={{0,64},{32,96},{64,0},{96,32},{1,65},{33,97},{65,1},{97,33},{2,66}... | collective-permute-start | bytes 98312 | tf_op jit(solution)/shard_map/ppermute | solution.py:502
  72.1 14.5 %collective-permute-start.7 = (bf16[64,256]{1,0:T(8,128)(2,1)S(1)}, bf16[64,256]{1,0:T(8,128)(2,1)S(1)}, u32[]{:S(2)}, u32[]{:S(2)}) collective-permute-start(bf16[64,256]{1,0:T(8,128)(2,1)S(1)} %queries.1.refs_0_), channel_id=1, source_target_pairs={{0,96},{32,0},{64,32},{96,64},{1,97},{33,1},{65,33},{97,65},{2,98}... | collective-permute-start | bytes 98312 | tf_op jit(solution)/shard_map/ppermute | solution.py:502
  73.5 27.9 %collective-permute-start.13 = (bf16[256,1024]{1,0:T(8,128)(2,1)S(1)}, bf16[256,1024]{1,0:T(8,128)(2,1)S(1)}, u32[]{:S(2)}, u32[]{:S(2)}) collective-permute-start(bf16[256,1024]{1,0:T(8,128)(2,1)S(1)} %collective-permute-done.3.refs_2_.refs_0_), channel_id=1, source_target_pairs={{0,16},{16,0},{1,17},{17,1},{2,18},{18,2},{3,19},{19,3},{4,20},{20... | collective-permute-start | bytes 1572872 | tf_op jit(solution)/shard_map/ppermute | solution.py:497
  86.6 14.8 %collective-permute-start.14 = (bf16[256,1024]{1,0:T(8,128)(2,1)S(1)}, bf16[256,1024]{1,0:T(8,128)(2,1)S(1)}, u32[]{:S(2)}, u32[]{:S(2)}) collective-permute-start(bf16[256,1024]{1,0:T(8,128)(2,1)S(1)} %collective-permute-done.12.refs_1_), channel_id=1, source_target_pairs={{0,16},{16,0},{1,17},{17,1},{2,18},{18,2},{3,19},{19,3},{4,20},{20... | collective-permute-start | bytes 1572872 | tf_op jit(solution)/shard_map/ppermute | solution.py:497
  89.2 7.8 %collective-permute-start.8 = (bf16[64,384]{1,0:T(8,128)(2,1)S(1)}, bf16[64,384]{1,0:T(8,128)(2,1)S(1)}, u32[]{:S(2)}, u32[]{:S(2)}) collective-permute-start(bf16[64,384]{1,0:T(8,128)(2,1)S(1)} %get-tuple-element.18), channel_id=1, source_target_pairs={{0,96},{32,0},{64,32},{96,64},{1,97},{33,1},{65,33},{97,65},{2,98}... | collective-permute-start | bytes 147464 | tf_op jit(solution)/shard_map/ppermute | solution.py:502
  92.5 5.9 %collective-permute-start.9 = (bf16[64,384]{1,0:T(8,128)(2,1)S(1)}, bf16[64,384]{1,0:T(8,128)(2,1)S(1)}, u32[]{:S(2)}, u32[]{:S(2)}) collective-permute-start(bf16[64,384]{1,0:T(8,128)(2,1)S(1)} %get-tuple-element.19), channel_id=1, source_target_pairs={{0,64},{32,96},{64,0},{96,32},{1,65},{33,97},{65,1},{97,33},{2,66}... | collective-permute-start | bytes 147464 | tf_op jit(solution)/shard_map/ppermute | solution.py:502
  93.1 5.8 %collective-permute-start.10 = (bf16[64,384]{1,0:T(8,128)(2,1)S(1)}, bf16[64,384]{1,0:T(8,128)(2,1)S(1)}, u32[]{:S(2)}, u32[]{:S(2)}) collective-permute-start(bf16[64,384]{1,0:T(8,128)(2,1)S(1)} %get-tuple-element.20), channel_id=1, source_target_pairs={{0,32},{32,64},{64,96},{96,0},{1,33},{33,65},{65,97},{97,1},{2,34}... | collective-permute-start | bytes 147464 | tf_op jit(solution)/shard_map/ppermute | solution.py:502
  94.1 2.2 %copy-start.1 = (bf16[256,8192]{1,0:T(8,128)(2,1)S(1)}, bf16[256,8192]{1,0:T(8,128)(2,1)}, u32[]{:S(2)}) copy-start(bf16[256,8192]{1,0:T(8,128)(2,1)} %weight_ref.5) | copy-start | bytes 12582916
  99.2 4.0 %collective-permute-start.11 = (bf16[64,256]{1,0:T(8,128)(2,1)S(1)}, bf16[64,256]{1,0:T(8,128)(2,1)S(1)}, u32[]{:S(2)}, u32[]{:S(2)}) collective-permute-start(bf16[64,256]{1,0:T(8,128)(2,1)S(1)} %merge.1.own_ref), channel_id=1, source_target_pairs={{0,1},{1,0},{2,3},{3,2},{4,5},{5,4},{6,7},{7,6},{8,9},{9,8},{10,11... | collective-permute-start | bytes 98312 | tf_op jit(solution)/shard_map/ppermute | solution.py:508
  105.0 19.9 %all-to-all-start.3 = ((bf16[8,64,512]{2,1,0:T(8,128)(2,1)}), bf16[8,64,512]{2,1,0:T(8,128)(2,1)S(1)}, u32[]{:S(2)}, u32[]{:S(2)}) async-start(bf16[8,64,512]{2,1,0:T(8,128)(2,1)} %project.1), calls=%async_computation.3 | async-start | bytes 1048576 | tf_op jit(solution)/shard_map/all_to_all | solution.py:446

commit v8 on v5

--- a/solution.py
+++ b/solution.py
@@ -482,9 +482,10 @@
     def along(values, step):
         return lax.ppermute(values, "y", [(i, (i + step) % 4) for i in range(4)])
 
-    pooled = [queries] + [along(queries, step) for step in (1, 2, 3)]
+    around = {step: along(queries, step) for step in (2, 1, 3)}
+    pooled = [queries] + [around[step] for step in (1, 2, 3)]
     parts = attend(info, rows, pooled)
-    attention = merge([parts[0]] + [along(parts[step], -step) for step in (1, 2, 3)])
+    attention = merge([along(parts[step], -step) for step in (2, 1, 3)] + [parts[0]])
     partner = lax.ppermute(attention, "xl", flip)
     partial = project(info, project_own(info, attention, output_weight), partner, cross)
     summed = jnp.sum(swap(partial, ZRING).astype(F32), axis=0)

time: 117 us -> 117 us (level)
  no operation moved by 1% of the time
where the time goes in v8:
time: 117 us; the launch traced here: 116 us
  waiting for transfers between devices  53 us (45%)
  starting transfers between devices  36.4 us (31%)
  Pallas kernels  17.1 us (15%)
  local copies, waits for them, and re-layouts  6.66 us (6%)
  other arithmetic  1.47 us (1%)
  between operations  1.46 us (1%)
    all_to_all x4, waiting for transfers between devices, swap(): return lax.all_to_all(values, axis, 0, 0, tiled=False)  24.1 us
    all_to_all x4, starting transfers between devices, swap(): return lax.all_to_all(values, axis, 0, 0, tiled=False)  20.9 us
    ppermute x6, starting transfers between devices, along(): return lax.ppermute(values, 'y', [(i, (i + step) % 4) for i in range(4)])  11.1 us
    ppermute x2, waiting for transfers between devices, body(): early, late = (lax.ppermute(piece, 'xl', flip) for piece in sent)  10.2 us
    ppermute x1, waiting for transfers between devices, body(): other_hidden = lax.ppermute(own_hidden, 'xl', flip)  7.66 us
    unnamed x12, local copies, waits for them, and re-layouts  6.57 us
    ppermute x6, waiting for transfers between devices, along(): return lax.ppermute(values, 'y', [(i, (i + step) % 4) for i in range(4)])  5.65 us
    ppermute x1, waiting for transfers between devices, body(): beside = lax.ppermute(scaled, 'xl', flip)  5.39 us
  transfers between devices with their start and end apart: 19, of which 12 were waited for; matrix products, arithmetic and copies ran while one was open for 1% of the time, Pallas kernels for 10%

profile of v8, /device:TPU:2, one launch (start us, length us, event | category | flops | bytes accessed | tf_op | source)
XLA Modules:
  0.0 116.1 jit_solution(15212790115379333772)
XLA Ops:
  0.0 0.0 copy-start.2
  0.0 0.0 copy-start.5
  0.0 0.0 copy-start.3
  0.0 2.1 %pack.1 = bf16[8,128,512]{2,1,0:T(8,128)(2,1)} custom-call(s32[1]{0:T(128)} %bitcast.1.core_ref, bf16[32,8192]{1,0:T(8,128)(2,1)} %bitcast.15, bf16[32,8192]{1,0:T(8,128)(2,1)} %bitcast.16, bf16[64,512]{1,0:T(8,128)(2,1)} %resp_ref.1), custom_call_target="tpu_custom_call" | custom-call | tf_op jit(solution)/shard_map/pack/pallas_call | solution.py:69
  2.1 8.5 %all-to-all-start = ((bf16[8,128,512]{2,1,0:T(8,128)(2,1)}), bf16[8,128,512]{2,1,0:T(8,128)(2,1)S(1)}, u32[]{:S(2)}, u32[]{:S(2)}) async-start(bf16[8,128,512]{2,1,0:T(8,128)(2,1)} %pack.1), calls=%async_computation | async-start | bytes 2097152 | tf_op jit(solution)/shard_map/all_to_all | solution.py:427
  11.2 0.0 copy-done.5
  11.2 0.1 stack.28.info_ref
  11.3 0.0 copy-done.2
  11.3 0.0 copy-done.3
  11.3 1.0 scale_rows.1.refs_0_.after_ref
  12.3 0.6 collective-permute-start
  12.8 0.0 collective-permute-start.1
  12.8 0.0 copy-start
  12.8 2.2 %copy-done = bf16[256,8192]{1,0:T(8,128)(2,1)S(1)} copy-done((bf16[256,8192]{1,0:T(8,128)(2,1)S(1)}, bf16[256,8192]{1,0:T(8,128)(2,1)}, u32[]{:S(2)}) %copy-start) | copy-done | bytes 4194328
  15.0 1.4 %pick_columns.1 = (bf16[256,1024]{1,0:T(8,128)(2,1)}, bf16[256,1024]{1,0:T(8,128)(2,1)S(1)}) custom-call(s32[6]{0:T(128)S(1)} %stack.28.info_ref, bf16[256,8192]{1,0:T(8,128)(2,1)S(1)} %copy-done, bf16[336,512]{1,0:T(8,128)(2,1)S(1)} %scale_rows.1.refs_0_.after_ref), custom_call_target="tpu_custom_call" | custom-call | tf_op jit(solution)/shard_map/pick_columns/pallas_call | solution.py:417
  16.5 1.5 %collective-permute-start.3 = (bf16[256,1024]{1,0:T(8,128)(2,1)}, bf16[256,1024]{1,0:T(8,128)(2,1)S(1)}, u32[]{:S(2)}, u32[]{:S(2)}) collective-permute-start(bf16[256,1024]{1,0:T(8,128)(2,1)} %get-tuple-element.11), channel_id=1, source_target_pairs={{0,1},{1,0},{2,3},{3,2},{4,5},{5,4},{6,7},{7,6},{8,9},{9,8},{10,11... | collective-permute-start | bytes 1572872 | tf_op jit(solution)/shard_map/ppermute | solution.py:472
  18.0 5.4 %collective-permute-done.refs_1_ = bf16[336,512]{1,0:T(8,128)(2,1)} collective-permute-done((bf16[336,512]{1,0:T(8,128)(2,1)S(1)}, bf16[336,512]{1,0:T(8,128)(2,1)}, u32[]{:S(2)}, u32[]{:S(2)}) %collective-permute-start) | collective-permute-done | bytes 344096 | tf_op jit(solution)/shard_map/ppermute | solution.py:469
  23.4 0.0 collective-permute-start.2
  23.4 0.6 fusion.11
  24.0 0.0 collective-permute-done.1.refs_2_.refs_0_
  24.1 9.0 %collective-permute-done.3.refs_2_.refs_0_ = bf16[256,1024]{1,0:T(8,128)(2,1)S(1)} collective-permute-done((bf16[256,1024]{1,0:T(8,128)(2,1)}, bf16[256,1024]{1,0:T(8,128)(2,1)S(1)}, u32[]{:S(2)}, u32[]{:S(2)}) %collective-permute-start.3) | collective-permute-done | bytes 524320 | tf_op jit(solution)/shard_map/ppermute | solution.py:472
  33.1 0.0 collective-permute-done.2.refs_3_.refs_1_
  33.1 6.2 %all-to-all-done.got_ref = bf16[8,128,512]{2,1,0:T(8,128)(2,1)S(1)} async-done(((bf16[8,128,512]{2,1,0:T(8,128)(2,1)}), bf16[8,128,512]{2,1,0:T(8,128)(2,1)S(1)}, u32[]{:S(2)}, u32[]{:S(2)}) %all-to-all-start) | async-done | bytes 1048608 | tf_op jit(solution)/shard_map/all_to_all | solution.py:427
  39.3 0.8 split.1.own_ref
  40.1 0.5 collective-permute-start.4
  40.6 2.5 %partial_products.1 = bf16[8,176,128]{2,1,0:T(8,128)(2,1)} custom-call(s32[6]{0:T(128)S(1)} %stack.28.info_ref, bf16[8,128,512]{2,1,0:T(8,128)(2,1)S(1)} %all-to-all-done.got_ref, bf16[336,512]{1,0:T(8,128)(2,1)S(1)} %scale_rows.1.refs_0_.after_ref, bf16[336,512]{1,0:T(8,128)(2,1)} %collective-permute-done.refs_1_, ...), custom_call_target="tpu_custom_call" | custom-call | tf_op jit(solution)/shard_map/partial_products/pallas_call | solution.py:162
  43.2 3.4 %all-to-all-start.1 = ((bf16[8,176,128]{2,1,0:T(8,128)(2,1)}), bf16[8,176,128]{2,1,0:T(8,128)(2,1)S(1)}, u32[]{:S(2)}, u32[]{:S(2)}) async-start(bf16[8,176,128]{2,1,0:T(8,128)(2,1)} %partial_products.1), calls=%async_computation.1 | async-start | bytes 720896 | tf_op jit(solution)/shard_map/all_to_all | solution.py:427
  46.6 7.7 %collective-permute-done.4.other_ref = bf16[8,64,512]{2,1,0:T(8,128)(2,1)} collective-permute-done((bf16[8,64,512]{2,1,0:T(8,128)(2,1)}, bf16[8,64,512]{2,1,0:T(8,128)(2,1)}, u32[]{:S(2)}, u32[]{:S(2)}) %collective-permute-start.4) | collective-permute-done | bytes 524320 | tf_op jit(solution)/shard_map/ppermute | solution.py:474
  54.3 0.0 copy-start.4
  54.3 2.2 %copy-done.4 = bf16[8192,256]{1,0:T(8,128)(2,1)S(1)} copy-done((bf16[8192,256]{1,0:T(8,128)(2,1)S(1)}, bf16[8192,256]{1,0:T(8,128)(2,1)}, u32[]{:S(2)}) %copy-start.4) | copy-done | bytes 4194328
  56.5 2.3 %queries.1.refs_0_ = bf16[64,256]{1,0:T(8,128)(2,1)S(1)} custom-call(s32[6]{0:T(128)S(1)} %stack.28.info_ref, f32[16,1,512]{2,1,0:T(1,128)S(1)} %bitcast.14, f32[2,224,128]{2,1,0:T(8,128)S(1)} %pad_maximum_fusion.refs_4_.trig_ref, bf16[8192,256]{1,0:T(8,128)(2,1)S(1)} %copy-done.4, bf16[8,64,512]{2,1,0:T(8,128)(2,1)} %split.1.own_ref, ...), custom_call_target="tpu_custom_call" | custom-call | flops 30000001024 | bytes 1000000 | tf_op jit(solution)/shard_map/queries/pallas_call | solution.py:245
  58.8 1.9 %all-to-all-done.1.parts_ref = bf16[8,176,128]{2,1,0:T(8,128)(2,1)S(1)} async-done(((bf16[8,176,128]{2,1,0:T(8,128)(2,1)}), bf16[8,176,128]{2,1,0:T(8,128)(2,1)S(1)}, u32[]{:S(2)}, u32[]{:S(2)}) %all-to-all-start.1) | async-done | bytes 360480 | tf_op jit(solution)/shard_map/all_to_all | solution.py:427
  60.7 1.2 %finish_keys.1 = bf16[16,144,128]{2,1,0:T(8,128)(2,1)} custom-call(bf16[8,176,128]{2,1,0:T(8,128)(2,1)S(1)} %all-to-all-done.1.parts_ref, f32[2,224,128]{2,1,0:T(8,128)S(1)} %pad_maximum_fusion.refs_4_.trig_ref, bf16[64,256]{1,0:T(8,128)(2,1)S(1)} %queries.1.refs_0_), custom_call_target="tpu_custom_call" | custom-call | flops 30000001024 | bytes 1000000 | tf_op jit(solution)/shard_map/finish_keys/pallas_call | solution.py:209
  61.9 5.5 %all-to-all-start.2 = ((bf16[16,144,128]{2,1,0:T(8,128)(2,1)}), bf16[16,144,128]{2,1,0:T(8,128)(2,1)S(1)}, u32[]{:S(2)}, u32[]{:S(2)}) async-start(bf16[16,144,128]{2,1,0:T(8,128)(2,1)} %finish_keys.1), calls=%async_computation.2 | async-start | bytes 1179648 | tf_op jit(solution)/shard_map/all_to_all | solution.py:427
  67.4 0.2 collective-permute-start.12
  67.6 1.6 %collective-permute-start.5 = (bf16[64,256]{1,0:T(8,128)(2,1)S(1)}, bf16[64,256]{1,0:T(8,128)(2,1)S(1)}, u32[]{:S(2)}, u32[]{:S(2)}) collective-permute-start(bf16[64,256]{1,0:T(8,128)(2,1)S(1)} %queries.1.refs_0_), channel_id=1, source_target_pairs={{0,32},{32,64},{64,96},{96,0},{1,33},{33,65},{65,97},{97,1},{2,34}... | collective-permute-start | bytes 98312 | tf_op jit(solution)/shard_map/ppermute | solution.py:483
  69.2 2.9 %collective-permute-start.6 = (bf16[64,256]{1,0:T(8,128)(2,1)S(1)}, bf16[64,256]{1,0:T(8,128)(2,1)S(1)}, u32[]{:S(2)}, u32[]{:S(2)}) collective-permute-start(bf16[64,256]{1,0:T(8,128)(2,1)S(1)} %queries.1.refs_0_), channel_id=1, source_target_pairs={{0,64},{32,96},{64,0},{96,32},{1,65},{33,97},{65,1},{97,33},{2,66}... | collective-permute-start | bytes 98312 | tf_op jit(solution)/shard_map/ppermute | solution.py:483
  72.1 1.3 %collective-permute-start.7 = (bf16[64,256]{1,0:T(8,128)(2,1)S(1)}, bf16[64,256]{1,0:T(8,128)(2,1)S(1)}, u32[]{:S(2)}, u32[]{:S(2)}) collective-permute-start(bf16[64,256]{1,0:T(8,128)(2,1)S(1)} %queries.1.refs_0_), channel_id=1, source_target_pairs={{0,96},{32,0},{64,32},{96,64},{1,97},{33,1},{65,33},{97,65},{2,98}... | collective-permute-start | bytes 98312 | tf_op jit(solution)/shard_map/ppermute | solution.py:483
  73.5 0.0 collective-permute-done.5.refs_1_
  73.5 1.2 %collective-permute-done.6.refs_2_ = bf16[64,256]{1,0:T(8,128)(2,1)S(1)} collective-permute-done((bf16[64,256]{1,0:T(8,128)(2,1)S(1)}, bf16[64,256]{1,0:T(8,128)(2,1)S(1)}, u32[]{:S(2)}, u32[]{:S(2)}) %collective-permute-start.6) | collective-permute-done | bytes 32800 | tf_op jit(solution)/shard_map/ppermute | solution.py:483
  74.6 1.4 %collective-permute-done.7.refs_3_ = bf16[64,256]{1,0:T(8,128)(2,1)S(1)} collective-permute-done((bf16[64,256]{1,0:T(8,128)(2,1)S(1)}, bf16[64,256]{1,0:T(8,128)(2,1)S(1)}, u32[]{:S(2)}, u32[]{:S(2)}) %collective-permute-start.7) | collective-permute-done | bytes 32800 | tf_op jit(solution)/shard_map/ppermute | solution.py:483
  76.0 1.5 %all-to-all-done.2.rows_ref = bf16[16,144,128]{2,1,0:T(8,128)(2,1)S(1)} async-done(((bf16[16,144,128]{2,1,0:T(8,128)(2,1)}), bf16[16,144,128]{2,1,0:T(8,128)(2,1)S(1)}, u32[]{:S(2)}, u32[]{:S(2)}) %all-to-all-start.2) | async-done | bytes 589856 | tf_op jit(solution)/shard_map/all_to_all | solution.py:427
  77.5 2.5 %attend.1 = (bf16[64,384]{1,0:T(8,128)(2,1)S(1)}, bf16[64,384]{1,0:T(8,128)(2,1)S(1)}, bf16[64,384]{1,0:T(8,128)(2,1)S(1)}, bf16[64,384]{1,0:T(8,128)(2,1)S(1)}) custom-call(s32[6]{0:T(128)S(1)} %stack.28.info_ref, bf16[16,144,128]{2,1,0:T(8,128)(2,1)S(1)} %all-to-all-done.2.rows_ref, bf16[64,256]{1,0:T(8,128)(2,1)S(1)} %queries.1.refs_0_, ...), custom_call_target="tpu_custom_call" | custom-call | tf_op jit(solution)/shard_map/attend/pallas_call | solution.py:330
  80.1 3.3 %collective-permute-start.8 = (bf16[64,384]{1,0:T(8,128)(2,1)S(1)}, bf16[64,384]{1,0:T(8,128)(2,1)S(1)}, u32[]{:S(2)}, u32[]{:S(2)}) collective-permute-start(bf16[64,384]{1,0:T(8,128)(2,1)S(1)} %get-tuple-element.13), channel_id=1, source_target_pairs={{0,64},{32,96},{64,0},{96,32},{1,65},{33,97},{65,1},{97,33},{2,66}... | collective-permute-start | bytes 147464 | tf_op jit(solution)/shard_map/ppermute | solution.py:483
  83.3 1.1 collective-permute-start.9
  84.4 1.0 collective-permute-start.10
  85.4 0.0 collective-permute-start.13
  85.4 1.2 %collective-permute-done.12.refs_1_ = bf16[256,1024]{1,0:T(8,128)(2,1)S(1)} collective-permute-done((bf16[256,1024]{1,0:T(8,128)(2,1)S(1)}, bf16[256,1024]{1,0:T(8,128)(2,1)S(1)}, u32[]{:S(2)}, u32[]{:S(2)}) %collective-permute-start.12) | collective-permute-done | bytes 524320 | tf_op jit(solution)/shard_map/ppermute | solution.py:472
  86.6 0.0 collective-permute-start.14
  86.6 0.0 collective-permute-done.8.refs_0_
  86.6 0.8 collective-permute-done.9.refs_1_
  87.4 2.3 %collective-permute-done.10.refs_2_ = bf16[64,384]{1,0:T(8,128)(2,1)S(1)} collective-permute-done((bf16[64,384]{1,0:T(8,128)(2,1)S(1)}, bf16[64,384]{1,0:T(8,128)(2,1)S(1)}, u32[]{:S(2)}, u32[]{:S(2)}) %collective-permute-start.10) | collective-permute-done | bytes 49184 | tf_op jit(solution)/shard_map/ppermute | solution.py:483
  89.7 0.3 merge.1.own_ref
  90.0 1.5 %collective-permute-start.11 = (bf16[64,256]{1,0:T(8,128)(2,1)S(1)}, bf16[64,256]{1,0:T(8,128)(2,1)S(1)}, u32[]{:S(2)}, u32[]{:S(2)}) collective-permute-start(bf16[64,256]{1,0:T(8,128)(2,1)S(1)} %merge.1.own_ref), channel_id=1, source_target_pairs={{0,1},{1,0},{2,3},{3,2},{4,5},{5,4},{6,7},{7,6},{8,9},{9,8},{10,11... | collective-permute-start | bytes 98312 | tf_op jit(solution)/shard_map/ppermute | solution.py:489
  91.5 2.2 %copy-done.1 = bf16[256,8192]{1,0:T(8,128)(2,1)S(1)} copy-done((bf16[256,8192]{1,0:T(8,128)(2,1)S(1)}, bf16[256,8192]{1,0:T(8,128)(2,1)}, u32[]{:S(2)}) %copy-start.1) | copy-done | bytes 4194328
  93.7 1.0 project_own.1.started_ref
  94.7 0.0 collective-permute-done.13.refs_2_
  94.8 0.0 collective-permute-done.14.refs_3_
  94.8 0.0 collective-permute-done.11.other_ref
  94.8 1.8 %project.1 = bf16[8,64,512]{2,1,0:T(8,128)(2,1)} custom-call(s32[6]{0:T(128)S(1)} %stack.28.info_ref, f32[8,64,512]{2,1,0:T(8,128)S(1)} %project_own.1.started_ref, bf16[64,256]{1,0:T(8,128)(2,1)S(1)} %collective-permute-done.11.other_ref, bf16[256,1024]{1,0:T(8,128)(2,1)S(1)} %collective-permute-done.3.refs_2_.refs_0_, ...), custom_call_target="tpu_custom_call" | custom-call | tf_op jit(solution)/shard_map/project/pallas_call | solution.py:399
  96.6 3.5 %all-to-all-start.3 = ((bf16[8,64,512]{2,1,0:T(8,128)(2,1)}), bf16[8,64,512]{2,1,0:T(8,128)(2,1)S(1)}, u32[]{:S(2)}, u32[]{:S(2)}) async-start(bf16[8,64,512]{2,1,0:T(8,128)(2,1)} %project.1), calls=%async_computation.3 | async-start | bytes 1048576 | tf_op jit(solution)/shard_map/all_to_all | solution.py:427
  100.8 14.5 %all-to-all-done.3 = bf16[8,64,512]{2,1,0:T(8,128)(2,1)S(1)} async-done(((bf16[8,64,512]{2,1,0:T(8,128)(2,1)}), bf16[8,64,512]{2,1,0:T(8,128)(2,1)S(1)}, u32[]{:S(2)}, u32[]{:S(2)}) %all-to-all-start.3) | async-done | bytes 524320 | tf_op jit(solution)/shard_map/all_to_all | solution.py:427
  115.3 0.1 convert_reduce_fusion
  115.4 0.7 select_convert_fusion
  (8 shorter events, 0.1 us)
Async XLA Ops:
  0.0 11.3 %copy-start.2 = (bf16[64,512]{1,0:T(8,128)(2,1)S(1)}, bf16[64,512]{1,0:T(8,128)(2,1)}, u32[]{:S(2)}) copy-start(bf16[64,512]{1,0:T(8,128)(2,1)} %resp_ref.1) | copy-start | bytes 196612
  0.0 11.2 %copy-start.5 = (bf16[8192]{0:T(1024)(128)(2,1)S(1)}, bf16[8192]{0:T(1024)(128)(2,1)}, u32[]{:S(2)}) copy-start(bf16[8192]{0:T(1024)(128)(2,1)} %param.11) | copy-start | bytes 49156
  0.0 11.3 %copy-start.3 = (bf16[256,512]{1,0:T(8,128)(2,1)S(1)}, bf16[256,512]{1,0:T(8,128)(2,1)}, u32[]{:S(2)}) copy-start(bf16[256,512]{1,0:T(8,128)(2,1)} %prompt_ref.1) | copy-start | bytes 786436
  2.1 37.2 %all-to-all-start = ((bf16[8,128,512]{2,1,0:T(8,128)(2,1)}), bf16[8,128,512]{2,1,0:T(8,128)(2,1)S(1)}, u32[]{:S(2)}, u32[]{:S(2)}) async-start(bf16[8,128,512]{2,1,0:T(8,128)(2,1)} %pack.1), calls=%async_computation | async-start | bytes 2097152 | tf_op jit(solution)/shard_map/all_to_all | solution.py:427
  12.3 11.1 %collective-permute-start = (bf16[336,512]{1,0:T(8,128)(2,1)S(1)}, bf16[336,512]{1,0:T(8,128)(2,1)}, u32[]{:S(2)}, u32[]{:S(2)}) collective-permute-start(bf16[336,512]{1,0:T(8,128)(2,1)S(1)} %scale_rows.1.refs_0_.after_ref), channel_id=1, source_target_pairs={{0,1},{1,0},{2,3},{3,2},{4,5},{5,4},{6,7},{7,6},{8,9},{9,8},{10,11... | collective-permute-start | bytes 1032200 | tf_op jit(solution)/shard_map/ppermute | solution.py:469
  12.8 11.2 %collective-permute-start.1 = (bf16[336,512]{1,0:T(8,128)(2,1)S(1)}, bf16[336,512]{1,0:T(8,128)(2,1)S(1)}, u32[]{:S(2)}, u32[]{:S(2)}) collective-permute-start(bf16[336,512]{1,0:T(8,128)(2,1)S(1)} %scale_rows.1.refs_0_.after_ref), channel_id=1, source_target_pairs={{0,16},{16,0},{1,17},{17,1},{2,18},{18,2},{3,19},{19,3},{4,20},{20... | collective-permute-start | bytes 1032200 | tf_op jit(solution)/shard_map/ppermute | solution.py:470
  12.8 2.2 %copy-start = (bf16[256,8192]{1,0:T(8,128)(2,1)S(1)}, bf16[256,8192]{1,0:T(8,128)(2,1)}, u32[]{:S(2)}) copy-start(bf16[256,8192]{1,0:T(8,128)(2,1)} %weight_ref.5) | copy-start | bytes 12582916
  16.5 16.6 %collective-permute-start.3 = (bf16[256,1024]{1,0:T(8,128)(2,1)}, bf16[256,1024]{1,0:T(8,128)(2,1)S(1)}, u32[]{:S(2)}, u32[]{:S(2)}) collective-permute-start(bf16[256,1024]{1,0:T(8,128)(2,1)} %get-tuple-element.11), channel_id=1, source_target_pairs={{0,1},{1,0},{2,3},{3,2},{4,5},{5,4},{6,7},{7,6},{8,9},{9,8},{10,11... | collective-permute-start | bytes 1572872 | tf_op jit(solution)/shard_map/ppermute | solution.py:472
  23.4 9.7 %collective-permute-start.2 = (bf16[336,512]{1,0:T(8,128)(2,1)}, bf16[336,512]{1,0:T(8,128)(2,1)S(1)}, u32[]{:S(2)}, u32[]{:S(2)}) collective-permute-start(bf16[336,512]{1,0:T(8,128)(2,1)} %collective-permute-done.refs_1_), channel_id=1, source_target_pairs={{0,16},{16,0},{1,17},{17,1},{2,18},{18,2},{3,19},{19,3},{4,20},{20... | collective-permute-start | bytes 1032200 | tf_op jit(solution)/shard_map/ppermute | solution.py:470
  40.1 14.2 %collective-permute-start.4 = (bf16[8,64,512]{2,1,0:T(8,128)(2,1)}, bf16[8,64,512]{2,1,0:T(8,128)(2,1)}, u32[]{:S(2)}, u32[]{:S(2)}) collective-permute-start(bf16[8,64,512]{2,1,0:T(8,128)(2,1)} %split.1.own_ref), channel_id=1, source_target_pairs={{0,1},{1,0},{2,3},{3,2},{4,5},{5,4},{6,7},{7,6},{8,9},{9,8},{10,11... | collective-permute-start | bytes 1572872 | tf_op jit(solution)/shard_map/ppermute | solution.py:474
  43.2 17.5 %all-to-all-start.1 = ((bf16[8,176,128]{2,1,0:T(8,128)(2,1)}), bf16[8,176,128]{2,1,0:T(8,128)(2,1)S(1)}, u32[]{:S(2)}, u32[]{:S(2)}) async-start(bf16[8,176,128]{2,1,0:T(8,128)(2,1)} %partial_products.1), calls=%async_computation.1 | async-start | bytes 720896 | tf_op jit(solution)/shard_map/all_to_all | solution.py:427
  54.3 2.2 %copy-start.4 = (bf16[8192,256]{1,0:T(8,128)(2,1)S(1)}, bf16[8192,256]{1,0:T(8,128)(2,1)}, u32[]{:S(2)}) copy-start(bf16[8192,256]{1,0:T(8,128)(2,1)} %weight_ref.4) | copy-start | bytes 12582916
  61.9 15.6 %all-to-all-start.2 = ((bf16[16,144,128]{2,1,0:T(8,128)(2,1)}), bf16[16,144,128]{2,1,0:T(8,128)(2,1)S(1)}, u32[]{:S(2)}, u32[]{:S(2)}) async-start(bf16[16,144,128]{2,1,0:T(8,128)(2,1)} %finish_keys.1), calls=%async_computation.2 | async-start | bytes 1179648 | tf_op jit(solution)/shard_map/all_to_all | solution.py:427
  67.4 19.2 %collective-permute-start.12 = (bf16[256,1024]{1,0:T(8,128)(2,1)S(1)}, bf16[256,1024]{1,0:T(8,128)(2,1)S(1)}, u32[]{:S(2)}, u32[]{:S(2)}) collective-permute-start(bf16[256,1024]{1,0:T(8,128)(2,1)S(1)} %get-tuple-element.12.refs_3_), channel_id=1, source_target_pairs={{0,1},{1,0},{2,3},{3,2},{4,5},{5,4},{6,7},{7,6},{8,9},{9,8},{10,11... | collective-permute-start | bytes 1572872 | tf_op jit(solution)/shard_map/ppermute | solution.py:472
  67.6 5.8 %collective-permute-start.5 = (bf16[64,256]{1,0:T(8,128)(2,1)S(1)}, bf16[64,256]{1,0:T(8,128)(2,1)S(1)}, u32[]{:S(2)}, u32[]{:S(2)}) collective-permute-start(bf16[64,256]{1,0:T(8,128)(2,1)S(1)} %queries.1.refs_0_), channel_id=1, source_target_pairs={{0,32},{32,64},{64,96},{96,0},{1,33},{33,65},{65,97},{97,1},{2,34}... | collective-permute-start | bytes 98312 | tf_op jit(solution)/shard_map/ppermute | solution.py:483
  69.2 5.4 %collective-permute-start.6 = (bf16[64,256]{1,0:T(8,128)(2,1)S(1)}, bf16[64,256]{1,0:T(8,128)(2,1)S(1)}, u32[]{:S(2)}, u32[]{:S(2)}) collective-permute-start(bf16[64,256]{1,0:T(8,128)(2,1)S(1)} %queries.1.refs_0_), channel_id=1, source_target_pairs={{0,64},{32,96},{64,0},{96,32},{1,65},{33,97},{65,1},{97,33},{2,66}... | collective-permute-start | bytes 98312 | tf_op jit(solution)/shard_map/ppermute | solution.py:483
  72.1 3.9 %collective-permute-start.7 = (bf16[64,256]{1,0:T(8,128)(2,1)S(1)}, bf16[64,256]{1,0:T(8,128)(2,1)S(1)}, u32[]{:S(2)}, u32[]{:S(2)}) collective-permute-start(bf16[64,256]{1,0:T(8,128)(2,1)S(1)} %queries.1.refs_0_), channel_id=1, source_target_pairs={{0,96},{32,0},{64,32},{96,64},{1,97},{33,1},{65,33},{97,65},{2,98}... | collective-permute-start | bytes 98312 | tf_op jit(solution)/shard_map/ppermute | solution.py:483
  80.1 6.6 %collective-permute-start.8 = (bf16[64,384]{1,0:T(8,128)(2,1)S(1)}, bf16[64,384]{1,0:T(8,128)(2,1)S(1)}, u32[]{:S(2)}, u32[]{:S(2)}) collective-permute-start(bf16[64,384]{1,0:T(8,128)(2,1)S(1)} %get-tuple-element.13), channel_id=1, source_target_pairs={{0,64},{32,96},{64,0},{96,32},{1,65},{33,97},{65,1},{97,33},{2,66}... | collective-permute-start | bytes 147464 | tf_op jit(solution)/shard_map/ppermute | solution.py:483
  83.3 4.1 %collective-permute-start.9 = (bf16[64,384]{1,0:T(8,128)(2,1)S(1)}, bf16[64,384]{1,0:T(8,128)(2,1)S(1)}, u32[]{:S(2)}, u32[]{:S(2)}) collective-permute-start(bf16[64,384]{1,0:T(8,128)(2,1)S(1)} %get-tuple-element.14), channel_id=1, source_target_pairs={{0,96},{32,0},{64,32},{96,64},{1,97},{33,1},{65,33},{97,65},{2,98}... | collective-permute-start | bytes 147464 | tf_op jit(solution)/shard_map/ppermute | solution.py:483
  84.4 5.3 %collective-permute-start.10 = (bf16[64,384]{1,0:T(8,128)(2,1)S(1)}, bf16[64,384]{1,0:T(8,128)(2,1)S(1)}, u32[]{:S(2)}, u32[]{:S(2)}) collective-permute-start(bf16[64,384]{1,0:T(8,128)(2,1)S(1)} %get-tuple-element.15), channel_id=1, source_target_pairs={{0,32},{32,64},{64,96},{96,0},{1,33},{33,65},{65,97},{97,1},{2,34}... | collective-permute-start | bytes 147464 | tf_op jit(solution)/shard_map/ppermute | solution.py:483
  85.4 9.4 %collective-permute-start.13 = (bf16[256,1024]{1,0:T(8,128)(2,1)S(1)}, bf16[256,1024]{1,0:T(8,128)(2,1)S(1)}, u32[]{:S(2)}, u32[]{:S(2)}) collective-permute-start(bf16[256,1024]{1,0:T(8,128)(2,1)S(1)} %collective-permute-done.3.refs_2_.refs_0_), channel_id=1, source_target_pairs={{0,16},{16,0},{1,17},{17,1},{2,18},{18,2},{3,19},{19,3},{4,20},{20... | collective-permute-start | bytes 1572872 | tf_op jit(solution)/shard_map/ppermute | solution.py:478
  86.6 8.2 %collective-permute-start.14 = (bf16[256,1024]{1,0:T(8,128)(2,1)S(1)}, bf16[256,1024]{1,0:T(8,128)(2,1)S(1)}, u32[]{:S(2)}, u32[]{:S(2)}) collective-permute-start(bf16[256,1024]{1,0:T(8,128)(2,1)S(1)} %collective-permute-done.12.refs_1_), channel_id=1, source_target_pairs={{0,16},{16,0},{1,17},{17,1},{2,18},{18,2},{3,19},{19,3},{4,20},{20... | collective-permute-start | bytes 1572872 | tf_op jit(solution)/shard_map/ppermute | solution.py:478
  90.0 4.8 %collective-permute-start.11 = (bf16[64,256]{1,0:T(8,128)(2,1)S(1)}, bf16[64,256]{1,0:T(8,128)(2,1)S(1)}, u32[]{:S(2)}, u32[]{:S(2)}) collective-permute-start(bf16[64,256]{1,0:T(8,128)(2,1)S(1)} %merge.1.own_ref), channel_id=1, source_target_pairs={{0,1},{1,0},{2,3},{3,2},{4,5},{5,4},{6,7},{7,6},{8,9},{9,8},{10,11... | collective-permute-start | bytes 98312 | tf_op jit(solution)/shard_map/ppermute | solution.py:489
  91.5 2.2 %copy-start.1 = (bf16[256,8192]{1,0:T(8,128)(2,1)S(1)}, bf16[256,8192]{1,0:T(8,128)(2,1)}, u32[]{:S(2)}) copy-start(bf16[256,8192]{1,0:T(8,128)(2,1)} %weight_ref.5) | copy-start | bytes 12582916
  96.6 18.7 %all-to-all-start.3 = ((bf16[8,64,512]{2,1,0:T(8,128)(2,1)}), bf16[8,64,512]{2,1,0:T(8,128)(2,1)S(1)}, u32[]{:S(2)}, u32[]{:S(2)}) async-start(bf16[8,64,512]{2,1,0:T(8,128)(2,1)} %project.1), calls=%async_computation.3 | async-start | bytes 1048576 | tf_op jit(solution)/shard_map/all_to_all | solution.py:427
